TPU v7x, 256 devices: a whole 4x4x8 slice. The times are simulated.
256 devices in a mesh: space: 64 (over y, z_hi, x), mode: 4 (over z_lo, core).
Axes of the slice: x: 4, y: 4, z: 8 (z_hi: 4, z_lo: 2; z = z_hi * 2 + z_lo), core: 2. Of those that a mesh axis runs over, the one named last changes fastest.
Arguments:
- start_field: float32 [36, 128, 64, 128], P('mode', 'space'), may hold values from -1.8 to 1.8
- source: float32 [36, 128, 64, 128], P('mode', 'space')
- mean_field: float32 [128, 64, 128], P('space'), may hold values from 0.5 to 2
- kl_fields: float32 [4, 128, 64, 128], P(None, 'space'), may hold values from -1 to 1
- triples: int32 [156, 3], replicated, may hold values from 0 to 35, as said below
- coef: float32 [156], replicated, may hold values from 0.5 to 2
Outputs:
- smoothed: float32 [36, 128, 64, 128], P('mode', 'space')
- residual: float32 [36, 128, 64, 128], P('mode', 'space')
Inputs may be any that keep to these rules, and one draw needn't show every extreme that they name: Rows of triples are distinct. Field 0 appears only in the rows (0, s, s), one for every slot s of the 36 slots; the other rows name a field 1 to 4 and two different slots.
All inputs are finite; a program needn't handle non-finite values.
Results may differ from a plain program's by a relative error of at most 0.00022.
Values sent between devices are 32-bit elements; how exact they have to be, the bound alone decides.
No kernel may reach another device: no remote copies, remote signals or barrier semaphores. Data moves between devices by JAX's collectives and lax.ppermute only.
A program may use at most 64 MiB of HBM per device.

v0:
```python
import jax
import jax.numpy as jnp
from jax import lax
from jax.sharding import PartitionSpec as P


def extended(block, sides, width):
    for axis, dim in sides:
        count = lax.axis_size(axis)
        forward = [(i, i + 1) for i in range(count - 1)]
        backward = [(target, source) for source, target in forward]
        low = lax.ppermute(
            lax.slice_in_dim(block, block.shape[dim] - width, None, axis=dim), axis, forward
        )
        high = lax.ppermute(lax.slice_in_dim(block, 0, width, axis=dim), axis, backward)
        block = jnp.concatenate([low, block, high], axis=dim)
    return block


def neighbour_views(arr):
    return [
        arr[..., 2:, 1:-1, 1:-1],
        arr[..., :-2, 1:-1, 1:-1],
        arr[..., 1:-1, 2:, 1:-1],
        arr[..., 1:-1, :-2, 1:-1],
        arr[..., 1:-1, 1:-1, 2:],
        arr[..., 1:-1, 1:-1, :-2],
    ]


def stencil(field_pad, coeff_pad):
    centre = field_pad[..., 1:-1, 1:-1, 1:-1]
    own = coeff_pad[..., 1:-1, 1:-1, 1:-1]
    result = None
    for value, other in zip(neighbour_views(field_pad), neighbour_views(coeff_pad)):
        term = 0.5 * (own + other) * (centre - value)
        result = term if result is None else result + term
    return result


def face_total(coeff_pad):
    own = coeff_pad[..., 1:-1, 1:-1, 1:-1]
    result = None
    for other in neighbour_views(coeff_pad):
        term = 0.5 * (own + other)
        result = term if result is None else result + term
    return result


def pad_sides(arr):
    return jnp.pad(arr, [(0, 0)] * (arr.ndim - 2) + [(1, 1), (1, 1)])


def body(start_field, source, mean_field, kl_fields, triples, coef):
    highest = lax.Precision.HIGHEST
    local = start_field.shape[0]
    groups = lax.axis_size("mode")
    slots = local * groups
    nfields = kl_fields.shape[0] + 1
    first_slot = lax.axis_index("mode") * local
    field_ids = (triples[:, 0:1] == jnp.arange(nfields, dtype=jnp.int32)[None]).astype(
        jnp.float32
    ) * coef[:, None]
    row_ids = (triples[:, 1:2] == jnp.arange(slots, dtype=jnp.int32)[None]).astype(jnp.float32)
    col_ids = (triples[:, 2:3] == jnp.arange(slots, dtype=jnp.int32)[None]).astype(jnp.float32)
    coupling = jnp.einsum("nm,ni,nj->mij", field_ids, row_ids, col_ids, precision=highest)
    fields = jnp.concatenate([mean_field[None], kl_fields], axis=0)
    fields_z = extended(fields, (("space", 1),), 1)
    coeff_pad = pad_sides(fields_z)
    mean_faces = face_total(coeff_pad[0])
    mode_diag = jnp.diagonal(coupling[0])
    rows_here = lax.dynamic_slice_in_dim(coupling, first_slot, local, axis=1)
    scaling = (
        lax.dynamic_slice_in_dim(mode_diag, first_slot, local)[:, None, None, None]
        * mean_faces[None]
    )

    def operator(field):
        field_z = extended(field, (("space", 1),), 1)
        mixed = jnp.einsum(
            "mij,jzxy->mizxy",
            rows_here,
            lax.all_gather(field_z, "mode", axis=0, tiled=True),
            precision=highest,
        )
        return jnp.sum(stencil(pad_sides(mixed), coeff_pad[:, None]), axis=0)

    first = source - operator(start_field)
    middle = start_field + 0.8 * first / scaling
    residual = source - operator(middle)
    smoothed = middle + 0.8 * residual / scaling
    return (smoothed, residual)


def solution(mesh):
    return jax.shard_map(
        body,
        mesh=mesh,
        in_specs=(
            P("mode", "space", None, None),
            P("mode", "space", None, None),
            P("space", None, None),
            P(None, "space", None, None),
            P(),
            P(),
        ),
        out_specs=(P("mode", "space", None, None), P("mode", "space", None, None)),
        check_vma=False,
    )
```

profile of v0, /device:TPU:9, one launch (start us, length us, event | category | flops | bytes accessed | tf_op | source)
XLA Modules:
  0.0 253.0 jit_solution(4873273783387995792)
XLA Ops:
  7.3 1.1 fusion.79
  8.4 3.1 %collective-permute-start.2 = (f32[9,1,64,128]{3,2,1,0:T(8,128)S(1)}, f32[9,1,64,128]{3,2,1,0:T(8,128)S(1)}, u32[]{:S(2)}, u32[]{:S(2)}) collective-permute-start(f32[9,1,64,128]{3,2,1,0:T(8,128)S(1)} %get-tuple-element.18), channel_id=1, source_target_pairs={{0,4},{4,8},{8,12},{12,16},{16,20},{20,24},{24,28},{28,32},{32,36}... | collective-permute-start | bytes 884744 | tf_op jit(solution)/shard_map/ppermute | solution.py:12
  11.5 8.8 %collective-permute-start.3 = (f32[9,1,64,128]{3,2,1,0:T(8,128)S(1)}, f32[9,1,64,128]{3,2,1,0:T(8,128)S(1)}, u32[]{:S(2)}, u32[]{:S(2)}) collective-permute-start(f32[9,1,64,128]{3,2,1,0:T(8,128)S(1)} %get-tuple-element.19), channel_id=1, source_target_pairs={{4,0},{8,4},{12,8},{16,12},{20,16},{24,20},{28,24},{32,28},{36,32}... | collective-permute-start | bytes 884744 | tf_op jit(solution)/shard_map/ppermute | solution.py:15
  20.3 6.8 %collective-permute-done.2 = f32[9,1,64,128]{3,2,1,0:T(8,128)S(1)} collective-permute-done((f32[9,1,64,128]{3,2,1,0:T(8,128)S(1)}, f32[9,1,64,128]{3,2,1,0:T(8,128)S(1)}, u32[]{:S(2)}, u32[]{:S(2)}) %collective-permute-start.2) | collective-permute-done | bytes 294944 | tf_op jit(solution)/shard_map/ppermute | solution.py:12
  27.1 5.7 %collective-permute-done.3 = f32[9,1,64,128]{3,2,1,0:T(8,128)S(1)} collective-permute-done((f32[9,1,64,128]{3,2,1,0:T(8,128)S(1)}, f32[9,1,64,128]{3,2,1,0:T(8,128)S(1)}, u32[]{:S(2)}, u32[]{:S(2)}) %collective-permute-start.3) | collective-permute-done | bytes 294944 | tf_op jit(solution)/shard_map/ppermute | solution.py:15
  32.8 2.2 pad_maximum_fusion.1
  35.1 1.0 fusion.58
  36.2 1.9 collective-permute-start
  38.1 9.2 %collective-permute-start.1 = (f32[5,1,64,128]{3,2,1,0:T(8,128)S(1)}, f32[5,1,64,128]{3,2,1,0:T(8,128)S(1)}, u32[]{:S(2)}, u32[]{:S(2)}) collective-permute-start(f32[5,1,64,128]{3,2,1,0:T(8,128)S(1)} %get-tuple-element.21), channel_id=1, source_target_pairs={{4,0},{8,4},{12,8},{16,12},{20,16},{24,20},{28,24},{32,28},{36,32}... | collective-permute-start | bytes 491528 | tf_op jit(solution)/shard_map/ppermute | solution.py:15
  47.7 1.0 gather_fusion
  48.7 1.6 collective-permute-done
  52.0 40.1 %all-gather.3.cloned.1.call-done = f32[36,4,64,128]{3,2,1,0:T(8,128)} async-done(((f32[9,4,64,128]{3,2,1,0:T(8,128)}), f32[36,4,64,128]{3,2,1,0:T(8,128)}) %all-gather.3.cloned.1.call-update) | async-done | bytes 4718608 | tf_op jit(solution)/shard_map/all_gather | solution.py:83
  92.1 15.9 %fusion.32 = f32[5,9,4,64,128]{4,1,3,2,0:T(8,128)} fusion(f32[36,4,64,128]{3,2,1,0:T(8,128)} %all-gather.3.cloned.1.call-done, f32[36,5,36]{2,0,1:T(8,128)S(1)} %fusion.56, s32[]{:T(128)S(6)} %select_n.8), kind=kOutput, calls=%fused_computation.45 | convolution fusion | flops 637009920 | bytes 10657796 | tf_op jit(solution)/shard_map/mij,jzxy->mizxy/dot_general | solution.py:80
  108.0 14.7 %fusion.37 = f32[9,2,64,128]{3,0,2,1:T(8,128)S(1)} fusion(f32[5,9,4,64,128]{4,1,3,2,0:T(8,128)} %fusion.32, f32[5,2,64,128]{3,2,1,0:T(8,128)S(1)} %get-tuple-element.15, f32[5,2,64,128]{3,2,1,0:T(8,128)S(1)} %get-tuple-element.11, f32[5,2,64,128]{3,2,1,0:T(8,128)S(1)} %get-tuple-element.12, f32[5,2,64,128]{3,2,1,0:T(8,128)S(1)} %get-tuple-element.13, ...), kind=kLoop, calls=%fused_computation.50 | loop fusion | flops 13123584 | bytes 28770304 | tf_op jit(solution)/shard_map/reduce_sum | solution.py:86
  123.6 1.9 collective-permute-start.4
  125.5 8.5 %collective-permute-start.5 = (f32[9,1,64,128]{3,0,2,1:T(8,128)S(1)}, f32[9,1,64,128]{3,0,2,1:T(8,128)S(1)}, u32[]{:S(2)}, u32[]{:S(2)}) collective-permute-start(f32[9,1,64,128]{3,0,2,1:T(8,128)S(1)} %get-tuple-element.17), channel_id=1, source_target_pairs={{4,0},{8,4},{12,8},{16,12},{20,16},{24,20},{28,24},{32,28},{36,32}... | collective-permute-start | bytes 884744 | tf_op jit(solution)/shard_map/ppermute | solution.py:15
  134.0 21.0 %collective-permute-done.4 = f32[9,1,64,128]{3,0,2,1:T(8,128)S(1)} collective-permute-done((f32[9,1,64,128]{3,0,2,1:T(8,128)S(1)}, f32[9,1,64,128]{3,0,2,1:T(8,128)S(1)}, u32[]{:S(2)}, u32[]{:S(2)}) %collective-permute-start.4) | collective-permute-done | bytes 294944 | tf_op jit(solution)/shard_map/ppermute | solution.py:12
  155.6 1.4 copy.29
  157.0 54.9 %all-gather.5.cloned.1.call-done = f32[36,4,64,128]{3,2,1,0:T(8,128)} async-done(((f32[9,4,64,128]{3,2,1,0:T(8,128)}), f32[36,4,64,128]{3,2,1,0:T(8,128)}) %all-gather.5.cloned.1.call-update) | async-done | bytes 4718608 | tf_op jit(solution)/shard_map/all_gather | solution.py:83
  211.9 15.9 %fusion.30 = f32[5,9,4,64,128]{4,1,3,2,0:T(8,128)} fusion(f32[36,4,64,128]{3,2,1,0:T(8,128)} %all-gather.5.cloned.1.call-done, f32[36,5,36]{2,0,1:T(8,128)S(1)} %fusion.56, s32[]{:T(128)S(6)} %select_n.8), kind=kOutput, calls=%fused_computation.43 | convolution fusion | flops 637009920 | bytes 10657796 | tf_op jit(solution)/shard_map/mij,jzxy->mizxy/dot_general | solution.py:80
  227.8 14.7 %fusion.36 = f32[9,2,64,128]{3,0,2,1:T(8,128)S(1)} fusion(f32[5,9,4,64,128]{4,1,3,2,0:T(8,128)} %fusion.30, f32[5,2,64,128]{3,2,1,0:T(8,128)S(1)} %get-tuple-element.15, f32[5,2,64,128]{3,2,1,0:T(8,128)S(1)} %get-tuple-element.11, f32[5,2,64,128]{3,2,1,0:T(8,128)S(1)} %get-tuple-element.12, f32[5,2,64,128]{3,2,1,0:T(8,128)S(1)} %get-tuple-element.13, ...), kind=kLoop, calls=%fused_computation.49 | loop fusion | flops 13123584 | bytes 28770304 | tf_op jit(solution)/shard_map/reduce_sum | solution.py:86
  242.5 1.6 fusion.43
  244.2 1.0 copy.32
  245.2 1.0 copy.33
  (33 shorter events, 3.5 us)
Async XLA Ops:
  7.2 43.1 %copy-start.2 = (f32[4,2,64,128]{3,2,1,0:T(8,128)S(1)}, f32[4,2,64,128]{3,2,1,0:T(8,128)}, u32[]{:S(2)}) copy-start(f32[4,2,64,128]{3,2,1,0:T(8,128)} %param.9) | copy-start | bytes 786436
  7.2 43.1 %copy-start.3 = (f32[2,64,128]{2,1,0:T(8,128)S(1)}, f32[2,64,128]{2,1,0:T(8,128)}, u32[]{:S(2)}) copy-start(f32[2,64,128]{2,1,0:T(8,128)} %param.8) | copy-start | bytes 196612
  7.2 40.1 %copy-start.4 = (s32[156,3]{0,1:T(4,128)S(1)}, s32[156,3]{0,1:T(4,128)}, u32[]{:S(2)}) copy-start(s32[156,3]{0,1:T(4,128)} %param.10) | copy-start | bytes 5620
  7.2 40.2 %copy-start.5 = (f32[156]{0:T(256)S(1)}, f32[156]{0:T(256)}, u32[]{:S(2)}) copy-start(f32[156]{0:T(256)} %param.11) | copy-start | bytes 1876
  7.2 84.8 %all-gather.3.cloned.1.call-start = ((), (), s32[]{:S(2)}) async-start(), calls=%async_computation | async-start | bytes 5898240 | tf_op jit(solution)/shard_map/all_gather | solution.py:83
  8.4 18.7 %collective-permute-start.2 = (f32[9,1,64,128]{3,2,1,0:T(8,128)S(1)}, f32[9,1,64,128]{3,2,1,0:T(8,128)S(1)}, u32[]{:S(2)}, u32[]{:S(2)}) collective-permute-start(f32[9,1,64,128]{3,2,1,0:T(8,128)S(1)} %get-tuple-element.18), channel_id=1, source_target_pairs={{0,4},{4,8},{8,12},{12,16},{16,20},{20,24},{24,28},{28,32},{32,36}... | collective-permute-start | bytes 884744 | tf_op jit(solution)/shard_map/ppermute | solution.py:12
  11.5 21.3 %collective-permute-start.3 = (f32[9,1,64,128]{3,2,1,0:T(8,128)S(1)}, f32[9,1,64,128]{3,2,1,0:T(8,128)S(1)}, u32[]{:S(2)}, u32[]{:S(2)}) collective-permute-start(f32[9,1,64,128]{3,2,1,0:T(8,128)S(1)} %get-tuple-element.19), channel_id=1, source_target_pairs={{4,0},{8,4},{12,8},{16,12},{20,16},{24,20},{28,24},{32,28},{36,32}... | collective-permute-start | bytes 884744 | tf_op jit(solution)/shard_map/ppermute | solution.py:15
  35.1 176.8 %all-gather.5.cloned.1.call-start = ((), (), s32[]{:S(2)}) async-start(), calls=%async_computation.1 | async-start | bytes 5898240 | tf_op jit(solution)/shard_map/all_gather | solution.py:83
  36.2 14.1 %collective-permute-start = (f32[5,1,64,128]{3,2,1,0:T(8,128)S(1)}, f32[5,1,64,128]{3,2,1,0:T(8,128)S(1)}, u32[]{:S(2)}, u32[]{:S(2)}) collective-permute-start(f32[5,1,64,128]{3,2,1,0:T(8,128)S(1)} %get-tuple-element.20), channel_id=1, source_target_pairs={{0,4},{4,8},{8,12},{12,16},{16,20},{20,24},{24,28},{28,32},{32,36}... | collective-permute-start | bytes 491528 | tf_op jit(solution)/shard_map/ppermute | solution.py:12
  38.1 12.2 %collective-permute-start.1 = (f32[5,1,64,128]{3,2,1,0:T(8,128)S(1)}, f32[5,1,64,128]{3,2,1,0:T(8,128)S(1)}, u32[]{:S(2)}, u32[]{:S(2)}) collective-permute-start(f32[5,1,64,128]{3,2,1,0:T(8,128)S(1)} %get-tuple-element.21), channel_id=1, source_target_pairs={{4,0},{8,4},{12,8},{16,12},{20,16},{24,20},{28,24},{32,28},{36,32}... | collective-permute-start | bytes 491528 | tf_op jit(solution)/shard_map/ppermute | solution.py:15
  107.9 14.7 %copy-start = (f32[9,2,64,128]{3,2,1,0:T(8,128)S(1)}, f32[9,2,64,128]{3,2,1,0:T(8,128)}, u32[]{:S(2)}) copy-start(f32[9,2,64,128]{3,2,1,0:T(8,128)} %param.6) | copy-start | bytes 1769476
  107.9 14.8 %copy-start.1 = (f32[9,2,64,128]{3,2,1,0:T(8,128)S(1)}, f32[9,2,64,128]{3,2,1,0:T(8,128)}, u32[]{:S(2)}) copy-start(f32[9,2,64,128]{3,2,1,0:T(8,128)} %param.7) | copy-start | bytes 1769476
  123.6 31.5 %collective-permute-start.4 = (f32[9,1,64,128]{3,0,2,1:T(8,128)S(1)}, f32[9,1,64,128]{3,0,2,1:T(8,128)S(1)}, u32[]{:S(2)}, u32[]{:S(2)}) collective-permute-start(f32[9,1,64,128]{3,0,2,1:T(8,128)S(1)} %get-tuple-element.16), channel_id=1, source_target_pairs={{0,4},{4,8},{8,12},{12,16},{16,20},{20,24},{24,28},{28,32},{32,36}... | collective-permute-start | bytes 884744 | tf_op jit(solution)/shard_map/ppermute | solution.py:12
  125.5 29.9 %collective-permute-start.5 = (f32[9,1,64,128]{3,0,2,1:T(8,128)S(1)}, f32[9,1,64,128]{3,0,2,1:T(8,128)S(1)}, u32[]{:S(2)}, u32[]{:S(2)}) collective-permute-start(f32[9,1,64,128]{3,0,2,1:T(8,128)S(1)} %get-tuple-element.17), channel_id=1, source_target_pairs={{4,0},{8,4},{12,8},{16,12},{20,16},{24,20},{28,24},{32,28},{36,32}... | collective-permute-start | bytes 884744 | tf_op jit(solution)/shard_map/ppermute | solution.py:15
Sparse Core Ops, SparseCore 0:
  35.2 56.8 all-gather.2
  157.1 54.7 all-gather.4
where the time goes:
time: 254 us; the launch traced here: 253 us
  waiting for transfers between devices  130 us (51%)
  other arithmetic  37 us (15%)
  starting transfers between devices  33.6 us (13%)
  matrix products  32 us (13%)
  between operations  14.3 us (6%)
  local copies, waits for them, and re-layouts  5.71 us (2%)
    all_gather x2, waiting for transfers between devices, operator(): lax.all_gather(field_z, 'mode', axis=0, tiled=True)  95 us
    dot_general x2, matrix products, operator(): jnp.einsum('mij,jzxy->mizxy', rows_here, lax.all_gather(field_z, 'mode',...  31.8 us
    reduce_sum x2, other arithmetic, operator(): return jnp.sum(stencil(pad_sides(mixed), coeff_pad[:, None]), axis=0)  29.5 us
    ppermute x3, waiting for transfers between devices, extended(): lax.ppermute(lax.slice_in_dim(block, block.shape[dim] - width, None, axis...  29.4 us
    ppermute x3, starting transfers between devices, extended(): lax.ppermute(lax.slice_in_dim(block, 0, width, axis=dim), axis, backward)  26.5 us
    ppermute x3, starting transfers between devices, extended(): lax.ppermute(lax.slice_in_dim(block, block.shape[dim] - width, None, axis...  6.96 us
    ppermute x3, waiting for transfers between devices, extended(): lax.ppermute(lax.slice_in_dim(block, 0, width, axis=dim), axis, backward)  6.07 us
  transfers between devices with their start and end apart: 8, of which 7 were waited for; matrix products, arithmetic and copies ran while one was open for 2% of the time, Pallas kernels for 0%

commit v1 on v0

v1 whole, which is shorter than its diff:
```python
import functools

import jax
import jax.numpy as jnp
from jax import lax
from jax.experimental import pallas as pl
from jax.experimental.pallas import tpu as pltpu
from jax.sharding import PartitionSpec as P

LOCAL, ROWS, LANES, HELD = 9, 64, 128, 16
GROUPS = 4
SLOTS = LOCAL * GROUPS
FIELDS = 5
ENTRIES = 156
F32 = jnp.float32
VMEM = pl.BlockSpec(memory_space=pltpu.VMEM)
SMEM = pl.BlockSpec(memory_space=pltpu.SMEM)
ANY = pl.BlockSpec(memory_space=pl.ANY)
PARAMS = dict(compiler_params=pltpu.CompilerParams(vmem_limit_bytes=40 * 2**20))


def shape(*dims):
    return jax.ShapeDtypeStruct(dims, F32)


def cost(flops, nbytes):
    return pl.CostEstimate(flops=flops, bytes_accessed=nbytes, transcendentals=0)


def window(ref, lead, g, low, count):
    rows = ref[(*lead, pl.ds(pl.multiple_of(HELD * g, HELD), 32), slice(None))]
    return rows[..., 8 + low : 8 + low + count, :]


def fill_padded(src, padded, sem):
    copy = pltpu.make_async_copy(src, padded.at[..., pl.ds(8, ROWS), :], sem)
    copy.start()
    edge = jnp.zeros((*padded.shape[:-2], 8, LANES), F32)
    padded[..., 0:8, :] = edge
    padded[..., 8 + ROWS : 16 + ROWS, :] = edge
    return copy


def lane_next(x):
    lane = lax.broadcasted_iota(jnp.int32, x.shape, x.ndim - 1)
    return jnp.where(lane == LANES - 1, 0.0, pltpu.roll(x, LANES - 1, x.ndim - 1))


def lane_prev(x):
    lane = lax.broadcasted_iota(jnp.int32, x.shape, x.ndim - 1)
    return jnp.where(lane == 0, 0.0, pltpu.roll(x, 1, x.ndim - 1))


def pack_start(g_ref, start, o0, o1, o2, o3, padded, sem):
    g = g_ref[0]
    fill_padded(start, padded, sem).wait()
    for d, out in enumerate((o0, o1, o2, o3)):
        for p in range(2):
            for k in range(LOCAL):
                at = k * 40 + 20 * p
                out[at : at + 20, :] = window(padded, (k, p), g ^ d, -2, 20)


def pack_source(g_ref, source, mean, kl, o0, o1, o2, o3, low, high, padded, klp, sems):
    g = g_ref[0]
    one = fill_padded(source, padded, sems.at[0])
    two = fill_padded(kl, klp, sems.at[1])
    three = pltpu.make_async_copy(mean.at[0], low.at[pl.ds(0, ROWS), :], sems.at[2])
    four = pltpu.make_async_copy(mean.at[1], high.at[pl.ds(0, ROWS), :], sems.at[3])
    three.start()
    four.start()
    two.wait()
    for p, out in enumerate((low, high)):
        for m in range(FIELDS - 1):
            at = ROWS + 18 * m
            out[at : at + 18, :] = window(klp, (m, p), g, -1, 18)
    one.wait()
    for d, out in enumerate((o0, o1, o2, o3)):
        for p in range(2):
            for k in range(LOCAL):
                at = k * 36 + 18 * p
                out[at : at + 18, :] = window(padded, (k, p), g ^ d, -1, 18)
    three.wait()
    four.wait()


def pack_edges(s0, s1, s2, s3, low, high):
    for d, src in enumerate((s0, s1, s2, s3)):
        for k in range(LOCAL):
            at = 18 * (LOCAL * d + k)
            low[at : at + 18, :] = src[k * 40 + 1 : k * 40 + 19, :]
            high[at : at + 18, :] = src[k * 40 + 21 : k * 40 + 39, :]


def accumulate(trip, cf, acc, count, faces, views):
    acc[...] = jnp.zeros(acc.shape, F32)

    def step(e, carry):
        m, i, j = trip[e], trip[ENTRIES + e], trip[2 * ENTRIES + e]
        c = cf[e]
        for p in range(2):
            total = None
            for b, view in enumerate(views(j, p)):
                term = faces[m, b, p] * view
                total = term if total is None else total + term
            acc[i, p] += c * total
        return carry

    lax.fori_loop(0, count, step, 0, unroll=2)


def first_sweep(
    trip, cf, g_ref, s0, s1, s2, s3, t0, t1, t2, t3, mean, kl, fl, fh, zl, zh,
    mid, b0, b1, b2, b3, low, high, faces_out,
    klp, ae, faces, vv, nxt, prv, acc, sems,
):
    g = g_ref[0]
    one = fill_padded(mean, klp.at[0], sems.at[0])
    two = fill_padded(kl, klp.at[pl.ds(1, FIELDS - 1)], sems.at[1])
    for d, src in enumerate((s0, s1, s2, s3)):
        for k in range(LOCAL):
            pos = LOCAL * d + k
            vv[pos, 0, 8:26, :] = zl[18 * pos : 18 * pos + 18, :]
            vv[pos, 3, 8:26, :] = zh[18 * pos : 18 * pos + 18, :]
            for p in range(2):
                vv[pos, 1 + p, 7:27, :] = src[k * 40 + 20 * p : k * 40 + 20 * p + 20, :]
                mine = vv[pos, 1 + p, 8:32, :]
                nxt[pos, p] = lane_next(mine)
                prv[pos, p] = lane_prev(mine)
    one.wait()
    two.wait()
    for m in range(FIELDS):
        for p in range(2):
            ae[m, 1 + p, 7:27, :] = window(klp, (m, p), g, -2, 20)
    for m in range(FIELDS - 1):
        at = ROWS + 18 * m
        ae[1 + m, 0, 8:26, :] = fl[at : at + 18, :]
        ae[1 + m, 3, 8:26, :] = fh[at : at + 18, :]
    for src, plane in ((fl, 0), (fh, 3)):
        klp[0, 0, 8 : 8 + ROWS, :] = src[0:ROWS, :]
        ae[0, plane, 8:26, :] = window(klp, (0, 0), g, -1, 18)
    for m in range(FIELDS):
        for p in range(2):
            own = ae[m, 1 + p, 8:32, :]
            others = (
                ae[m, 2 + p, 8:32, :], ae[m, p, 8:32, :],
                ae[m, 1 + p, 9:33, :], ae[m, 1 + p, 7:31, :],
                lane_next(own), lane_prev(own),
            )
            total = None
            for b, other in enumerate(others):
                face = 0.5 * (own + other)
                total = face if total is None else total + face
                faces[m, 1 + b, p] = -face
                faces_out[m, 1 + b, p] = -face[1 : 1 + HELD]
            faces[m, 0, p] = total
            faces_out[m, 0, p] = total[1 : 1 + HELD]

    def views(j, p):
        return (
            vv[j, 1 + p, 8:32, :], vv[j, 2 + p, 8:32, :], vv[j, p, 8:32, :],
            vv[j, 1 + p, 9:33, :], vv[j, 1 + p, 7:31, :], nxt[j, p], prv[j, p],
        )

    accumulate(trip, cf, acc, ENTRIES, faces, views)
    row = HELD * g - 1 + lax.broadcasted_iota(jnp.int32, (18, LANES), 0)
    inside = (row >= 0) & (row < ROWS)
    for p in range(2):
        rate = 0.8 / faces[0, 0, p, 0:18, :]
        for d, (src, out) in enumerate(((t0, b0), (t1, b1), (t2, b2), (t3, b3))):
            for k in range(LOCAL):
                pos = LOCAL * d + k
                at = k * 36 + 18 * p
                first = src[at : at + 18, :] - acc[pos, p, 0:18, :]
                moved = vv[pos, 1 + p, 8:26, :] + first * rate * cf[ENTRIES + pos]
                moved = jnp.where(inside, moved, 0.0)
                mid[pos, p, 7:25, :] = moved
                held = moved[1 : 1 + HELD]
                out[k, p] = held
                (low, high)[p][pos] = held


def second_residual(
    trip, cf, t0, t1, t2, t3, mid, faces, zl, zh, o0, o1, o2, o3, nxt, prv, acc
):
    for pos in range(SLOTS):
        for p in range(2):
            mine = mid[pos, p, 8:24, :]
            nxt[pos, p] = lane_next(mine)
            prv[pos, p] = lane_prev(mine)

    def views(j, p):
        return (
            mid[j, p, 8:24, :],
            zh[j] if p else mid[j, 1, 8:24, :],
            mid[j, 0, 8:24, :] if p else zl[j],
            mid[j, p, 9:25, :], mid[j, p, 7:23, :], nxt[j, p], prv[j, p],
        )

    accumulate(trip, cf, acc, ENTRIES, faces, views)
    for d, (src, out) in enumerate(((t0, o0), (t1, o1), (t2, o2), (t3, o3))):
        for k in range(LOCAL):
            for p in range(2):
                at = k * 36 + 18 * p + 1
                out[k, p] = src[at : at + HELD, :] - acc[LOCAL * d + k, p]


def second_sweep(
    cf, g_ref, mean, fl, fh, m0, m1, m2, m3, r0, r1, r2, r3, smoothed, residual, rate, pad
):
    g = g_ref[0]
    pad[0:8, :] = jnp.zeros((8, LANES), F32)
    pad[8 + ROWS :, :] = jnp.zeros((8, LANES), F32)
    for p in range(2):
        own = mean[p]
        pad[8 : 8 + ROWS, :] = own
        others = (
            fh[0:ROWS, :] if p else mean[1],
            mean[0] if p else fl[0:ROWS, :],
            pad[9 : 9 + ROWS, :], pad[7 : 7 + ROWS, :],
            lane_next(own), lane_prev(own),
        )
        total = None
        for other in others:
            face = 0.5 * (own + other)
            total = face if total is None else total + face
        rate[p] = 0.8 / total
    for d, (mid, res) in enumerate(((m0, r0), (m1, r1), (m2, r2), (m3, r3))):
        rows = pl.ds(pl.multiple_of(HELD * (g ^ d), HELD), HELD)
        for p in range(2):
            here = rate[p, rows, :]
            for k in range(LOCAL):
                left = res[k, p]
                residual[k, p, rows, :] = left
                smoothed[k, p, rows, :] = mid[k, p] + left * here * cf[ENTRIES + k]


def body(start_field, source, mean_field, kl_fields, triples, coef):
    g = lax.axis_index("mode")
    gs = g.astype(jnp.int32).reshape(1)
    modes = triples[:, 1:]
    at = LOCAL * ((modes // LOCAL) ^ g) + modes % LOCAL
    trip = jnp.concatenate([triples[:, 0], at[:, 0], at[:, 1]])
    diag = jnp.sum(
        jnp.where(
            (triples[:, 0:1] == 0) & (at[:, 0:1] == jnp.arange(SLOTS)[None]), coef[:, None], 0.0
        ),
        axis=0,
    )
    cf = jnp.concatenate([coef, 1.0 / diag])

    count = lax.axis_size("space")
    forward = [(i, i + 1) for i in range(count - 1)]
    backward = [(b, a) for a, b in forward]

    def up(x):
        return lax.ppermute(x, "space", forward)

    def down(x):
        return lax.ppermute(x, "space", backward)

    def trade(parts):
        return [parts[0]] + [
            lax.ppermute(parts[d], "mode", [(i, i ^ d) for i in range(GROUPS)])
            for d in range(1, GROUPS)
        ]

    sends = pl.pallas_call(
        pack_start,
        out_shape=[shape(360, LANES)] * 4,
        in_specs=[SMEM, ANY],
        out_specs=[VMEM] * 4,
        scratch_shapes=[pltpu.VMEM((LOCAL, 2, ROWS + 16, LANES), F32), pltpu.SemaphoreType.DMA],
        name="pack_start",
        **PARAMS,
    )(gs, start_field)
    starts = trade(sends)
    *sources, field_low, field_high = pl.pallas_call(
        pack_source,
        out_shape=[shape(324, LANES)] * 4 + [shape(136, LANES)] * 2,
        in_specs=[SMEM, ANY, ANY, ANY],
        out_specs=[VMEM] * 6,
        scratch_shapes=[
            pltpu.VMEM((LOCAL, 2, ROWS + 16, LANES), F32),
            pltpu.VMEM((FIELDS - 1, 2, ROWS + 16, LANES), F32),
            pltpu.SemaphoreType.DMA((4,)),
        ],
        name="pack_source",
        **PARAMS,
    )(gs, source, mean_field, kl_fields)
    below, above = up(field_high), down(field_low)
    sources = trade(sources)
    low, high = pl.pallas_call(
        pack_edges,
        out_shape=[shape(18 * SLOTS, LANES)] * 2,
        in_specs=[VMEM] * 4,
        out_specs=[VMEM] * 2,
        name="pack_edges",
        **PARAMS,
    )(*starts)
    zl, zh = up(high), down(low)
    mid, *mids, low, high, faces = pl.pallas_call(
        first_sweep,
        out_shape=[shape(SLOTS, 2, 32, LANES)]
        + [shape(LOCAL, 2, HELD, LANES)] * 4
        + [shape(SLOTS, HELD, LANES)] * 2
        + [shape(FIELDS, 7, 2, HELD, LANES)],
        in_specs=[SMEM] * 3 + [VMEM] * 8 + [ANY] * 2 + [VMEM] * 4,
        out_specs=[VMEM] * 8,
        scratch_shapes=[
            pltpu.VMEM((FIELDS, 2, ROWS + 16, LANES), F32),
            pltpu.VMEM((FIELDS, 4, 40, LANES), F32),
            pltpu.VMEM((FIELDS, 7, 2, 24, LANES), F32),
            pltpu.VMEM((SLOTS, 4, 40, LANES), F32),
            pltpu.VMEM((SLOTS, 2, 24, LANES), F32),
            pltpu.VMEM((SLOTS, 2, 24, LANES), F32),
            pltpu.VMEM((SLOTS, 2, 24, LANES), F32),
            pltpu.SemaphoreType.DMA((2,)),
        ],
        name="first_sweep",
        **PARAMS,
    )(trip, cf, gs, *starts, *sources, mean_field, kl_fields, below, above, zl, zh)
    zl, zh = up(high), down(low)
    mids = trade(mids)
    lefts = pl.pallas_call(
        second_residual,
        out_shape=[shape(LOCAL, 2, HELD, LANES)] * 4,
        in_specs=[SMEM] * 2 + [VMEM] * 8,
        out_specs=[VMEM] * 4,
        scratch_shapes=[pltpu.VMEM((SLOTS, 2, HELD, LANES), F32)] * 3,
        name="second_residual",
        **PARAMS,
    )(trip, cf, *sources, mid, faces, zl, zh)
    lefts = trade(lefts)
    smoothed, residual = pl.pallas_call(
        second_sweep,
        out_shape=[shape(LOCAL, 2, ROWS, LANES)] * 2,
        in_specs=[SMEM] * 2 + [VMEM] * 11,
        out_specs=[VMEM] * 2,
        scratch_shapes=[
            pltpu.VMEM((2, ROWS, LANES), F32),
            pltpu.VMEM((ROWS + 16, LANES), F32),
        ],
        name="second_sweep",
        **PARAMS,
    )(cf, gs, mean_field, below, above, *mids, *lefts)
    return (smoothed, residual)


def solution(mesh):
    return jax.shard_map(
        body,
        mesh=mesh,
        in_specs=(
            P("mode", "space", None, None),
            P("mode", "space", None, None),
            P("space", None, None),
            P(None, "space", None, None),
            P(),
            P(),
        ),
        out_specs=(P("mode", "space", None, None), P("mode", "space", None, None)),
        check_vma=False,
    )
```

time: 254 us -> 97.8 us (0.39)
  the two profiles are of different devices: /device:TPU:9 before, /device:TPU:71 now
where the time goes in v1:
time: 97.8 us; the launch traced here: 97.4 us
  waiting for transfers between devices  40.7 us (42%)
  starting transfers between devices  40.4 us (41%)
  Pallas kernels  11.1 us (11%)
  local copies, waits for them, and re-layouts  3.98 us (4%)
    ppermute x3, starting transfers between devices, up(): return lax.ppermute(x, 'space', forward)  24.5 us
    ppermute x12, waiting for transfers between devices, trade(): lax.ppermute(parts[d], 'mode', [(i, i ^ d) for i in range(GROUPS)])  24.3 us
    ppermute x3, waiting for transfers between devices, down(): return lax.ppermute(x, 'space', backward)  10.6 us
    ppermute x12, starting transfers between devices, trade(): lax.ppermute(parts[d], 'mode', [(i, i ^ d) for i in range(GROUPS)])  10.1 us
    ppermute x3, waiting for transfers between devices, up(): return lax.ppermute(x, 'space', forward)  5.84 us
    ppermute x3, starting transfers between devices, down(): return lax.ppermute(x, 'space', backward)  5.76 us
    pallas_call x1, Pallas kernels, body(): pl.pallas_call(first_sweep, out_shape=[shape(SLOTS, 2, 32, LANES)] + [sha...  5.04 us
    pallas_call x1, Pallas kernels, body(): pl.pallas_call(second_residual, out_shape=[shape(LOCAL, 2, HELD, LANES)]...  3.98 us
  transfers between devices with their start and end apart: 18, of which 6 were waited for; matrix products, arithmetic and copies ran while one was open for 0% of the time, Pallas kernels for 4%

profile of v1, /device:TPU:71, one launch (start us, length us, event | category | flops | bytes accessed | tf_op | source)
XLA Modules:
  0.0 97.4 jit_solution(4483637299408275140)
XLA Ops:
  0.7 1.1 %copy-done.4 = f32[9,2,64,128]{3,2,1,0:T(8,128)S(1)} copy-done((f32[9,2,64,128]{3,2,1,0:T(8,128)S(1)}, f32[9,2,64,128]{3,2,1,0:T(8,128)}, u32[]{:S(2)}) %copy-start.4) | copy-done | bytes 589848
  2.7 1.7 %collective-permute-start.3 = (f32[360,128]{1,0:T(8,128)S(1)}, f32[360,128]{1,0:T(8,128)S(1)}, u32[]{:S(2)}, u32[]{:S(2)}) collective-permute-start(f32[360,128]{1,0:T(8,128)S(1)} %get-tuple-element.30), channel_id=1, source_target_pairs={{0,2},{1,3},{2,0},{3,1},{4,6},{5,7},{6,4},{7,5},{8,10},{9,11},{10,... | collective-permute-start | bytes 552968 | tf_op jit(solution)/shard_map/ppermute | solution.py:264
  4.4 0.9 copy-done
  5.3 0.8 copy-done.2
  6.2 1.1 %copy-done.5 = f32[9,2,64,128]{3,2,1,0:T(8,128)S(1)} copy-done((f32[9,2,64,128]{3,2,1,0:T(8,128)S(1)}, f32[9,2,64,128]{3,2,1,0:T(8,128)}, u32[]{:S(2)}) %copy-start.5) | copy-done | bytes 589848
  7.5 6.0 %collective-permute-start = (f32[136,128]{1,0:T(8,128)S(1)}, f32[136,128]{1,0:T(8,128)S(1)}, u32[]{:S(2)}, u32[]{:S(2)}) collective-permute-start(f32[136,128]{1,0:T(8,128)S(1)} %get-tuple-element.26), channel_id=1, source_target_pairs={{0,4},{4,8},{8,12},{12,16},{16,20},{20,24},{24,28},{28,32},{32,36}... | collective-permute-start | bytes 208904 | tf_op jit(solution)/shard_map/ppermute | solution.py:257
  13.6 1.9 %collective-permute-start.1 = (f32[136,128]{1,0:T(8,128)S(1)}, f32[136,128]{1,0:T(8,128)S(1)}, u32[]{:S(2)}, u32[]{:S(2)}) collective-permute-start(f32[136,128]{1,0:T(8,128)S(1)} %get-tuple-element.27), channel_id=1, source_target_pairs={{4,0},{8,4},{12,8},{16,12},{20,16},{24,20},{28,24},{32,28},{36,32}... | collective-permute-start | bytes 208904 | tf_op jit(solution)/shard_map/ppermute | solution.py:260
  16.3 7.9 %collective-permute-start.8 = (f32[648,128]{1,0:T(8,128)S(1)}, f32[648,128]{1,0:T(8,128)S(1)}, u32[]{:S(2)}, u32[]{:S(2)}) collective-permute-start(f32[648,128]{1,0:T(8,128)S(1)} %get-tuple-element.36), channel_id=1, source_target_pairs={{0,4},{4,8},{8,12},{12,16},{16,20},{20,24},{24,28},{28,32},{32,36}... | collective-permute-start | bytes 995336 | tf_op jit(solution)/shard_map/ppermute | solution.py:257
  24.2 1.9 %collective-permute-start.9 = (f32[648,128]{1,0:T(8,128)S(1)}, f32[648,128]{1,0:T(8,128)S(1)}, u32[]{:S(2)}, u32[]{:S(2)}) collective-permute-start(f32[648,128]{1,0:T(8,128)S(1)} %get-tuple-element.37), channel_id=1, source_target_pairs={{4,0},{8,4},{12,8},{16,12},{20,16},{24,20},{28,24},{32,28},{36,32}... | collective-permute-start | bytes 995336 | tf_op jit(solution)/shard_map/ppermute | solution.py:260
  26.9 1.2 %collective-permute-start.7 = (f32[324,128]{1,0:T(8,128)S(1)}, f32[324,128]{1,0:T(8,128)S(1)}, u32[]{:S(2)}, u32[]{:S(2)}) collective-permute-start(f32[324,128]{1,0:T(8,128)S(1)} %get-tuple-element.35), channel_id=1, source_target_pairs={{0,3},{1,2},{2,1},{3,0},{4,7},{5,6},{6,5},{7,4},{8,11},{9,10},{10,... | collective-permute-start | bytes 497672 | tf_op jit(solution)/shard_map/ppermute | solution.py:264
  28.3 13.7 %collective-permute-done.6.t2 = f32[324,128]{1,0:T(8,128)S(1)} collective-permute-done((f32[324,128]{1,0:T(8,128)S(1)}, f32[324,128]{1,0:T(8,128)S(1)}, u32[]{:S(2)}, u32[]{:S(2)}) %collective-permute-start.6) | collective-permute-done | bytes 165920 | tf_op jit(solution)/shard_map/ppermute | solution.py:264
  42.0 3.6 %collective-permute-done.7.t3 = f32[324,128]{1,0:T(8,128)S(1)} collective-permute-done((f32[324,128]{1,0:T(8,128)S(1)}, f32[324,128]{1,0:T(8,128)S(1)}, u32[]{:S(2)}, u32[]{:S(2)}) %collective-permute-start.7) | collective-permute-done | bytes 165920 | tf_op jit(solution)/shard_map/ppermute | solution.py:264
  45.6 5.0 %first_sweep.1 = (f32[36,2,32,128]{3,2,1,0:T(8,128)S(1)}, f32[9,2,16,128]{3,2,1,0:T(8,128)S(1)}, f32[9,2,16,128]{3,2,1,0:T(8,128)S(1)}, f32[9,2,16,128]{3,2,1,0:...) custom-call(s32[468]{0:T(512)S(1)} %pad_add_fusion.trip, ...), custom_call_target="tpu_custom_call" | custom-call | tf_op jit(solution)/shard_map/first_sweep/pallas_call | solution.py:302
  50.7 10.7 %collective-permute-start.13 = (f32[36,16,128]{2,1,0:T(8,128)S(1)}, f32[36,16,128]{2,1,0:T(8,128)S(1)}, u32[]{:S(2)}, u32[]{:S(2)}) collective-permute-start(f32[36,16,128]{2,1,0:T(8,128)S(1)} %get-tuple-element.44), channel_id=1, source_target_pairs={{0,4},{4,8},{8,12},{12,16},{16,20},{20,24},{24,28},{28,32},{32,36}... | collective-permute-start | bytes 884744 | tf_op jit(solution)/shard_map/ppermute | solution.py:257
  61.3 1.9 %collective-permute-start.14 = (f32[36,16,128]{2,1,0:T(8,128)S(1)}, f32[36,16,128]{2,1,0:T(8,128)S(1)}, u32[]{:S(2)}, u32[]{:S(2)}) collective-permute-start(f32[36,16,128]{2,1,0:T(8,128)S(1)} %get-tuple-element.45), channel_id=1, source_target_pairs={{4,0},{8,4},{12,8},{16,12},{20,16},{24,20},{28,24},{32,28},{36,32}... | collective-permute-start | bytes 884744 | tf_op jit(solution)/shard_map/ppermute | solution.py:260
  63.6 1.9 %collective-permute-start.12 = (f32[9,2,16,128]{3,2,1,0:T(8,128)S(1)}, f32[9,2,16,128]{3,2,1,0:T(8,128)S(1)}, u32[]{:S(2)}, u32[]{:S(2)}) collective-permute-start(f32[9,2,16,128]{3,2,1,0:T(8,128)S(1)} %get-tuple-element.41), channel_id=1, source_target_pairs={{0,3},{1,2},{2,1},{3,0},{4,7},{5,6},{6,5},{7,4},{8,11},{9,10},{10,... | collective-permute-start | bytes 442376 | tf_op jit(solution)/shard_map/ppermute | solution.py:264
  65.5 5.8 %collective-permute-done.13.zl = f32[36,16,128]{2,1,0:T(8,128)S(1)} collective-permute-done((f32[36,16,128]{2,1,0:T(8,128)S(1)}, f32[36,16,128]{2,1,0:T(8,128)S(1)}, u32[]{:S(2)}, u32[]{:S(2)}) %collective-permute-start.13) | collective-permute-done | bytes 294944 | tf_op jit(solution)/shard_map/ppermute | solution.py:257
  71.3 10.6 %collective-permute-done.14.zh = f32[36,16,128]{2,1,0:T(8,128)S(1)} collective-permute-done((f32[36,16,128]{2,1,0:T(8,128)S(1)}, f32[36,16,128]{2,1,0:T(8,128)S(1)}, u32[]{:S(2)}, u32[]{:S(2)}) %collective-permute-start.14) | collective-permute-done | bytes 294944 | tf_op jit(solution)/shard_map/ppermute | solution.py:260
  81.9 4.0 %second_residual.1 = (f32[9,2,16,128]{3,2,1,0:T(8,128)S(1)}, f32[9,2,16,128]{3,2,1,0:T(8,128)S(1)}, f32[9,2,16,128]{3,2,1,0:T(8,128)S(1)}, f32[9,2,16,128]{3,2,1,0:T(8,128)S(1)}) custom-call(s32[468]{0:T(512)S(1)} %pad_add_fusion.trip, f32[192]{0:T(256)S(1)} %pad_maximum_fusion.cf, f32[324,128]{1,0:T(8,128)S(1)} %get-tuple-element.32.t0, ...), custom_call_target="tpu_custom_call" | custom-call | tf_op jit(solution)/shard_map/second_residual/pallas_call | solution.py:325
  85.8 1.1 %collective-permute-start.15 = (f32[9,2,16,128]{3,2,1,0:T(8,128)S(1)}, f32[9,2,16,128]{3,2,1,0:T(8,128)S(1)}, u32[]{:S(2)}, u32[]{:S(2)}) collective-permute-start(f32[9,2,16,128]{3,2,1,0:T(8,128)S(1)} %get-tuple-element.47), channel_id=1, source_target_pairs={{0,1},{1,0},{2,3},{3,2},{4,5},{5,4},{6,7},{7,6},{8,9},{9,8},{10,11... | collective-permute-start | bytes 442376 | tf_op jit(solution)/shard_map/ppermute | solution.py:264
  87.0 1.7 %collective-permute-start.17 = (f32[9,2,16,128]{3,2,1,0:T(8,128)S(1)}, f32[9,2,16,128]{3,2,1,0:T(8,128)S(1)}, u32[]{:S(2)}, u32[]{:S(2)}) collective-permute-start(f32[9,2,16,128]{3,2,1,0:T(8,128)S(1)} %get-tuple-element.49), channel_id=1, source_target_pairs={{0,3},{1,2},{2,1},{3,0},{4,7},{5,6},{6,5},{7,4},{8,11},{9,10},{10,... | collective-permute-start | bytes 442376 | tf_op jit(solution)/shard_map/ppermute | solution.py:264
  88.7 3.7 %collective-permute-done.16.r2 = f32[9,2,16,128]{3,2,1,0:T(8,128)S(1)} collective-permute-done((f32[9,2,16,128]{3,2,1,0:T(8,128)S(1)}, f32[9,2,16,128]{3,2,1,0:T(8,128)S(1)}, u32[]{:S(2)}, u32[]{:S(2)}) %collective-permute-start.16) | collective-permute-done | bytes 147488 | tf_op jit(solution)/shard_map/ppermute | solution.py:264
  92.4 3.3 %collective-permute-done.17.r3 = f32[9,2,16,128]{3,2,1,0:T(8,128)S(1)} collective-permute-done((f32[9,2,16,128]{3,2,1,0:T(8,128)S(1)}, f32[9,2,16,128]{3,2,1,0:T(8,128)S(1)}, u32[]{:S(2)}, u32[]{:S(2)}) %collective-permute-start.17) | collective-permute-done | bytes 147488 | tf_op jit(solution)/shard_map/ppermute | solution.py:264
  95.7 1.7 %second_sweep.1 = (f32[9,2,64,128]{3,2,1,0:T(8,128)}, f32[9,2,64,128]{3,2,1,0:T(8,128)}) custom-call(f32[192]{0:T(256)S(1)} %pad_maximum_fusion.cf, s32[1]{0:T(128)} %bitcast.1.g_ref, f32[2,64,128]{2,1,0:T(8,128)S(1)} %copy-done.3, f32[136,128]{1,0:T(8,128)S(1)} %collective-permute-done.fl, f32[136,128]{1,0:T(8,128)S(1)} %collective-permute-done.1.fh, ...), custom_call_target="tpu_custom_call" | custom-call | tf_op jit(solution)/shard_map/second_sweep/pallas_call | solution.py:335
  (43 shorter events, 3.4 us)
Async XLA Ops:
  0.6 45.0 %copy-start.1 = (f32[4,2,64,128]{3,2,1,0:T(8,128)S(1)}, f32[4,2,64,128]{3,2,1,0:T(8,128)}, u32[]{:S(2)}) copy-start(f32[4,2,64,128]{3,2,1,0:T(8,128)} %kl.3) | copy-start | bytes 786436
  0.6 1.1 %copy-start.4 = (f32[9,2,64,128]{3,2,1,0:T(8,128)S(1)}, f32[9,2,64,128]{3,2,1,0:T(8,128)}, u32[]{:S(2)}) copy-start(f32[9,2,64,128]{3,2,1,0:T(8,128)} %start.1) | copy-start | bytes 1769476
  1.8 13.8 %copy-start.7 = (s32[156,3]{0,1:T(4,128)S(1)}, s32[156,3]{0,1:T(4,128)}, u32[]{:S(2)}) copy-start(s32[156,3]{0,1:T(4,128)} %param.10) | copy-start | bytes 5620
  1.8 13.8 %copy-start.6 = (f32[156]{0:T(256)S(1)}, f32[156]{0:T(256)}, u32[]{:S(2)}) copy-start(f32[156]{0:T(256)} %param.11) | copy-start | bytes 1876
  1.8 26.5 %slice-start = ((s32[156,3]{0,1:T(4,128)}), s32[156,1]{0,1:T(1,128)S(1)}, s32[]{:S(2)}) async-start(s32[156,3]{0,1:T(4,128)} %param.10), calls=%async_computation | async-start | bytes 2048 | tf_op jit(solution)/shard_map/slice | solution.py:246
  1.9 13.8 %collective-permute-start.2 = (f32[360,128]{1,0:T(8,128)S(1)}, f32[360,128]{1,0:T(8,128)S(1)}, u32[]{:S(2)}, u32[]{:S(2)}) collective-permute-start(f32[360,128]{1,0:T(8,128)S(1)} %get-tuple-element.29), channel_id=1, source_target_pairs={{0,1},{1,0},{2,3},{3,2},{4,5},{5,4},{6,7},{7,6},{8,9},{9,8},{10,11... | collective-permute-start | bytes 552968 | tf_op jit(solution)/shard_map/ppermute | solution.py:264
  2.7 13.6 %collective-permute-start.3 = (f32[360,128]{1,0:T(8,128)S(1)}, f32[360,128]{1,0:T(8,128)S(1)}, u32[]{:S(2)}, u32[]{:S(2)}) collective-permute-start(f32[360,128]{1,0:T(8,128)S(1)} %get-tuple-element.30), channel_id=1, source_target_pairs={{0,2},{1,3},{2,0},{3,1},{4,6},{5,7},{6,4},{7,5},{8,10},{9,11},{10,... | collective-permute-start | bytes 552968 | tf_op jit(solution)/shard_map/ppermute | solution.py:264
  4.3 11.9 %collective-permute-start.4 = (f32[360,128]{1,0:T(8,128)S(1)}, f32[360,128]{1,0:T(8,128)S(1)}, u32[]{:S(2)}, u32[]{:S(2)}) collective-permute-start(f32[360,128]{1,0:T(8,128)S(1)} %get-tuple-element.31), channel_id=1, source_target_pairs={{0,3},{1,2},{2,1},{3,0},{4,7},{5,6},{6,5},{7,4},{8,11},{9,10},{10,... | collective-permute-start | bytes 552968 | tf_op jit(solution)/shard_map/ppermute | solution.py:264
  7.5 18.6 %collective-permute-start = (f32[136,128]{1,0:T(8,128)S(1)}, f32[136,128]{1,0:T(8,128)S(1)}, u32[]{:S(2)}, u32[]{:S(2)}) collective-permute-start(f32[136,128]{1,0:T(8,128)S(1)} %get-tuple-element.26), channel_id=1, source_target_pairs={{0,4},{4,8},{8,12},{12,16},{16,20},{20,24},{24,28},{28,32},{32,36}... | collective-permute-start | bytes 208904 | tf_op jit(solution)/shard_map/ppermute | solution.py:257
  13.6 13.4 %collective-permute-start.1 = (f32[136,128]{1,0:T(8,128)S(1)}, f32[136,128]{1,0:T(8,128)S(1)}, u32[]{:S(2)}, u32[]{:S(2)}) collective-permute-start(f32[136,128]{1,0:T(8,128)S(1)} %get-tuple-element.27), channel_id=1, source_target_pairs={{4,0},{8,4},{12,8},{16,12},{20,16},{24,20},{28,24},{32,28},{36,32}... | collective-permute-start | bytes 208904 | tf_op jit(solution)/shard_map/ppermute | solution.py:260
  15.7 12.6 %collective-permute-start.5 = (f32[324,128]{1,0:T(8,128)S(1)}, f32[324,128]{1,0:T(8,128)S(1)}, u32[]{:S(2)}, u32[]{:S(2)}) collective-permute-start(f32[324,128]{1,0:T(8,128)S(1)} %get-tuple-element.33), channel_id=1, source_target_pairs={{0,1},{1,0},{2,3},{3,2},{4,5},{5,4},{6,7},{7,6},{8,9},{9,8},{10,11... | collective-permute-start | bytes 497672 | tf_op jit(solution)/shard_map/ppermute | solution.py:264
  16.3 29.3 %collective-permute-start.8 = (f32[648,128]{1,0:T(8,128)S(1)}, f32[648,128]{1,0:T(8,128)S(1)}, u32[]{:S(2)}, u32[]{:S(2)}) collective-permute-start(f32[648,128]{1,0:T(8,128)S(1)} %get-tuple-element.36), channel_id=1, source_target_pairs={{0,4},{4,8},{8,12},{12,16},{16,20},{20,24},{24,28},{28,32},{32,36}... | collective-permute-start | bytes 995336 | tf_op jit(solution)/shard_map/ppermute | solution.py:257
  24.2 21.4 %collective-permute-start.9 = (f32[648,128]{1,0:T(8,128)S(1)}, f32[648,128]{1,0:T(8,128)S(1)}, u32[]{:S(2)}, u32[]{:S(2)}) collective-permute-start(f32[648,128]{1,0:T(8,128)S(1)} %get-tuple-element.37), channel_id=1, source_target_pairs={{4,0},{8,4},{12,8},{16,12},{20,16},{24,20},{28,24},{32,28},{36,32}... | collective-permute-start | bytes 995336 | tf_op jit(solution)/shard_map/ppermute | solution.py:260
  26.1 15.9 %collective-permute-start.6 = (f32[324,128]{1,0:T(8,128)S(1)}, f32[324,128]{1,0:T(8,128)S(1)}, u32[]{:S(2)}, u32[]{:S(2)}) collective-permute-start(f32[324,128]{1,0:T(8,128)S(1)} %get-tuple-element.34), channel_id=1, source_target_pairs={{0,2},{1,3},{2,0},{3,1},{4,6},{5,7},{6,4},{7,5},{8,10},{9,11},{10,... | collective-permute-start | bytes 497672 | tf_op jit(solution)/shard_map/ppermute | solution.py:264
  26.9 18.7 %collective-permute-start.7 = (f32[324,128]{1,0:T(8,128)S(1)}, f32[324,128]{1,0:T(8,128)S(1)}, u32[]{:S(2)}, u32[]{:S(2)}) collective-permute-start(f32[324,128]{1,0:T(8,128)S(1)} %get-tuple-element.35), channel_id=1, source_target_pairs={{0,3},{1,2},{2,1},{3,0},{4,7},{5,6},{6,5},{7,4},{8,11},{9,10},{10,... | collective-permute-start | bytes 497672 | tf_op jit(solution)/shard_map/ppermute | solution.py:264
  50.7 20.6 %collective-permute-start.13 = (f32[36,16,128]{2,1,0:T(8,128)S(1)}, f32[36,16,128]{2,1,0:T(8,128)S(1)}, u32[]{:S(2)}, u32[]{:S(2)}) collective-permute-start(f32[36,16,128]{2,1,0:T(8,128)S(1)} %get-tuple-element.44), channel_id=1, source_target_pairs={{0,4},{4,8},{8,12},{12,16},{16,20},{20,24},{24,28},{28,32},{32,36}... | collective-permute-start | bytes 884744 | tf_op jit(solution)/shard_map/ppermute | solution.py:257
  61.3 20.5 %collective-permute-start.14 = (f32[36,16,128]{2,1,0:T(8,128)S(1)}, f32[36,16,128]{2,1,0:T(8,128)S(1)}, u32[]{:S(2)}, u32[]{:S(2)}) collective-permute-start(f32[36,16,128]{2,1,0:T(8,128)S(1)} %get-tuple-element.45), channel_id=1, source_target_pairs={{4,0},{8,4},{12,8},{16,12},{20,16},{24,20},{28,24},{32,28},{36,32}... | collective-permute-start | bytes 884744 | tf_op jit(solution)/shard_map/ppermute | solution.py:260
  63.2 23.7 %collective-permute-start.10 = (f32[9,2,16,128]{3,2,1,0:T(8,128)S(1)}, f32[9,2,16,128]{3,2,1,0:T(8,128)S(1)}, u32[]{:S(2)}, u32[]{:S(2)}) collective-permute-start(f32[9,2,16,128]{3,2,1,0:T(8,128)S(1)} %get-tuple-element.39), channel_id=1, source_target_pairs={{0,1},{1,0},{2,3},{3,2},{4,5},{5,4},{6,7},{7,6},{8,9},{9,8},{10,11... | collective-permute-start | bytes 442376 | tf_op jit(solution)/shard_map/ppermute | solution.py:264
  63.5 25.2 %collective-permute-start.11 = (f32[9,2,16,128]{3,2,1,0:T(8,128)S(1)}, f32[9,2,16,128]{3,2,1,0:T(8,128)S(1)}, u32[]{:S(2)}, u32[]{:S(2)}) collective-permute-start(f32[9,2,16,128]{3,2,1,0:T(8,128)S(1)} %get-tuple-element.40), channel_id=1, source_target_pairs={{0,2},{1,3},{2,0},{3,1},{4,6},{5,7},{6,4},{7,5},{8,10},{9,11},{10,... | collective-permute-start | bytes 442376 | tf_op jit(solution)/shard_map/ppermute | solution.py:264
  63.6 25.2 %collective-permute-start.12 = (f32[9,2,16,128]{3,2,1,0:T(8,128)S(1)}, f32[9,2,16,128]{3,2,1,0:T(8,128)S(1)}, u32[]{:S(2)}, u32[]{:S(2)}) collective-permute-start(f32[9,2,16,128]{3,2,1,0:T(8,128)S(1)} %get-tuple-element.41), channel_id=1, source_target_pairs={{0,3},{1,2},{2,1},{3,0},{4,7},{5,6},{6,5},{7,4},{8,11},{9,10},{10,... | collective-permute-start | bytes 442376 | tf_op jit(solution)/shard_map/ppermute | solution.py:264
  81.9 13.9 %copy-start.3 = (f32[2,64,128]{2,1,0:T(8,128)S(1)}, f32[2,64,128]{2,1,0:T(8,128)}, u32[]{:S(2)}) copy-start(f32[2,64,128]{2,1,0:T(8,128)} %mean.5) | copy-start | bytes 196612
  85.8 2.9 %collective-permute-start.15 = (f32[9,2,16,128]{3,2,1,0:T(8,128)S(1)}, f32[9,2,16,128]{3,2,1,0:T(8,128)S(1)}, u32[]{:S(2)}, u32[]{:S(2)}) collective-permute-start(f32[9,2,16,128]{3,2,1,0:T(8,128)S(1)} %get-tuple-element.47), channel_id=1, source_target_pairs={{0,1},{1,0},{2,3},{3,2},{4,5},{5,4},{6,7},{7,6},{8,9},{9,8},{10,11... | collective-permute-start | bytes 442376 | tf_op jit(solution)/shard_map/ppermute | solution.py:264
  87.0 5.4 %collective-permute-start.16 = (f32[9,2,16,128]{3,2,1,0:T(8,128)S(1)}, f32[9,2,16,128]{3,2,1,0:T(8,128)S(1)}, u32[]{:S(2)}, u32[]{:S(2)}) collective-permute-start(f32[9,2,16,128]{3,2,1,0:T(8,128)S(1)} %get-tuple-element.48), channel_id=1, source_target_pairs={{0,2},{1,3},{2,0},{3,1},{4,6},{5,7},{6,4},{7,5},{8,10},{9,11},{10,... | collective-permute-start | bytes 442376 | tf_op jit(solution)/shard_map/ppermute | solution.py:264
  87.0 8.7 %collective-permute-start.17 = (f32[9,2,16,128]{3,2,1,0:T(8,128)S(1)}, f32[9,2,16,128]{3,2,1,0:T(8,128)S(1)}, u32[]{:S(2)}, u32[]{:S(2)}) collective-permute-start(f32[9,2,16,128]{3,2,1,0:T(8,128)S(1)} %get-tuple-element.49), channel_id=1, source_target_pairs={{0,3},{1,2},{2,1},{3,0},{4,7},{5,6},{6,5},{7,4},{8,11},{9,10},{10,... | collective-permute-start | bytes 442376 | tf_op jit(solution)/shard_map/ppermute | solution.py:264
  (3 other events, 2.9 us)

commit v2 on v1

v2 whole, which is shorter than its diff:
```python
import functools

import jax
import jax.numpy as jnp
from jax import lax
from jax.experimental import pallas as pl
from jax.experimental.pallas import tpu as pltpu
from jax.sharding import PartitionSpec as P

LOCAL, ROWS, LANES, HELD = 9, 64, 128, 16
GROUPS = 4
SLOTS = LOCAL * GROUPS
FIELDS = 5
ENTRIES = 156
EDGE = 18 * SLOTS
EDGE_FIELDS = ROWS + 18 * (FIELDS - 1)
RELAY_FIRST, RELAY_SECOND = True, True
NEAR = 2 * LOCAL
F32 = jnp.float32
VMEM = pl.BlockSpec(memory_space=pltpu.VMEM)
SMEM = pl.BlockSpec(memory_space=pltpu.SMEM)
HBM = pl.BlockSpec(memory_space=pltpu.HBM)
COST = pl.CostEstimate(flops=20_000_000, bytes_accessed=12_000_000, transcendentals=0)
PARAMS = dict(compiler_params=pltpu.CompilerParams(vmem_limit_bytes=40 * 2**20))


def shape(*dims):
    return jax.ShapeDtypeStruct(dims, F32)


def window(ref, lead, g, low, count):
    rows = ref[(*lead, pl.ds(pl.multiple_of(HELD * g, HELD), 32), slice(None))]
    return rows[..., 8 + low : 8 + low + count, :]


def fill_padded(src, padded, sem):
    copy = pltpu.make_async_copy(src, padded.at[..., pl.ds(8, ROWS), :], sem)
    copy.start()
    edge = jnp.zeros((*padded.shape[:-2], 8, LANES), F32)
    padded[..., 0:8, :] = edge
    padded[..., 8 + ROWS : 16 + ROWS, :] = edge
    return copy


def lane_next(x):
    lane = lax.broadcasted_iota(jnp.int32, x.shape, x.ndim - 1)
    return jnp.where(lane == LANES - 1, 0.0, pltpu.roll(x, LANES - 1, x.ndim - 1))


def lane_prev(x):
    lane = lax.broadcasted_iota(jnp.int32, x.shape, x.ndim - 1)
    return jnp.where(lane == 0, 0.0, pltpu.roll(x, 1, x.ndim - 1))


def pack_start(ids, start, o0, o1, o2, o3, padded, sem):
    g = ids[0]
    fill_padded(start, padded, sem).wait()
    for d, out in enumerate((o0, o1, o2, o3)):
        for p in range(2):
            for k in range(LOCAL):
                at = k * 40 + 20 * p
                out[at : at + 20, :] = window(padded, (k, p), g ^ d, -2, 20)


def pack_fields(ids, mean, kl, even, odd, klp, sems):
    g, parity = ids[0], ids[1]
    two = fill_padded(kl, klp, sems.at[0])
    edges = []
    for out, plane, sem in ((even, 1 - parity, 1), (odd, parity, 2)):
        edges.append(
            pltpu.make_async_copy(mean.at[plane], out.at[pl.ds(0, ROWS), :], sems.at[sem])
        )
        edges[-1].start()
    two.wait()
    for out, plane in ((even, 1 - parity), (odd, parity)):
        for m in range(FIELDS - 1):
            at = ROWS + 18 * m
            out[at : at + 18, :] = window(klp, (m, plane), g, -1, 18)
    for edge in edges:
        edge.wait()


def pack_source(ids, source, o0, o1, o2, o3, padded, sem):
    g = ids[0]
    fill_padded(source, padded, sem).wait()
    for d, out in enumerate((o0, o1, o2, o3)):
        for p in range(2):
            for k in range(LOCAL):
                at = k * 36 + 18 * p
                out[at : at + 18, :] = window(padded, (k, p), g ^ d, -1, 18)


def edge(src, k, top, upward):
    low = src[k * 40 + 1 : k * 40 + 19, :]
    high = src[k * 40 + 21 : k * 40 + 39, :]
    return jnp.where(top == upward, high, low)


def pack_near(ids, s0, s1, odd):
    top = ids[1] == 0
    for d, src in enumerate((s0, s1)):
        for k in range(LOCAL):
            at = 18 * (LOCAL * d + k)
            odd[at : at + 18, :] = edge(src, k, top, False)


def pack_far(ids, s0, s1, s2, s3, field_even, field_odd, even, odd):
    top = ids[1] == 0
    for d, src in enumerate((s0, s1, s2, s3)):
        for k in range(LOCAL):
            pos = LOCAL * d + k
            even[18 * pos : 18 * pos + 18, :] = edge(src, k, top, True)
            if pos >= NEAR:
                at = 18 * (pos - NEAR)
                odd[at : at + 18, :] = edge(src, k, top, False)
    even[EDGE:, :] = field_even[...]
    odd[EDGE // 2 :, :] = field_odd[...]


def sides(ids, from_even, from_odd):
    top = ids[1] == 0
    return jnp.where(top, from_odd, from_even), jnp.where(top, from_even, from_odd)


def near_odd(ids, straight, relayed):
    return straight if relayed is None else jnp.where(ids[2] == 1, relayed, straight)


def accumulate(trip, cf, acc, term):
    def step(e, carry):
        m, i, j = trip[e], trip[ENTRIES + e], trip[2 * ENTRIES + e]
        c = cf[e]
        for p in range(2):
            acc[i, p] += c * term(m, j, p)
        return carry

    lax.fori_loop(0, ENTRIES, step, 0, unroll=2)


def first_inner(
    trip, cf, ids, s0, s1, s2, s3, mean, kl, acc, faces, klp, ae, vv, nxt, prv, sems
):
    g = ids[0]
    one = fill_padded(mean, klp.at[0], sems.at[0])
    two = fill_padded(kl, klp.at[pl.ds(1, FIELDS - 1)], sems.at[1])
    for d, src in enumerate((s0, s1, s2, s3)):
        for k in range(LOCAL):
            pos = LOCAL * d + k
            for p in range(2):
                vv[pos, p, 7:27, :] = src[k * 40 + 20 * p : k * 40 + 20 * p + 20, :]
                mine = vv[pos, p, 8:32, :]
                nxt[pos, p] = lane_next(mine)
                prv[pos, p] = lane_prev(mine)
    one.wait()
    two.wait()
    for m in range(FIELDS):
        for p in range(2):
            ae[m, p, 7:27, :] = window(klp, (m, p), g, -2, 20)
    for m in range(FIELDS):
        for p in range(2):
            own = ae[m, p, 8:32, :]
            others = (
                ae[m, 1 - p, 8:32, :],
                ae[m, p, 9:33, :], ae[m, p, 7:31, :],
                lane_next(own), lane_prev(own),
            )
            total = None
            for b, other in enumerate(others):
                face = 0.5 * (own + other)
                total = face if total is None else total + face
                faces[m, 2 + b, p] = -face
            faces[m, 0, p] = total
            faces[m, 1, p] = own
    acc[...] = jnp.zeros(acc.shape, F32)

    def term(m, j, p):
        total = faces[m, 0, p] * vv[j, p, 8:32, :] + faces[m, 2, p] * vv[j, 1 - p, 8:32, :]
        total += faces[m, 3, p] * vv[j, p, 9:33, :] + faces[m, 4, p] * vv[j, p, 7:31, :]
        return total + (faces[m, 5, p] * nxt[j, p] + faces[m, 6, p] * prv[j, p])

    accumulate(trip, cf, acc, term)


def first_outer(
    trip, cf, ids, inner, faces, *rest
):
    relayed, rest = (rest[0], rest[1:]) if RELAY_FIRST else (None, rest)
    s0, s1, s2, s3, t0, t1, t2, t3, near, far, ev = rest[:11]
    mid, b0, b1, b2, b3, even, odd_a, odd_b, outer, acc, zz, pad = rest[11:]
    g, top = ids[0], ids[1] == 0
    for m in range(FIELDS):
        at = ROWS + 18 * (m - 1)
        rows = slice(at, at + 18) if m else slice(0, ROWS)
        e = ev[EDGE + rows.start : EDGE + rows.stop, :]
        o = far[EDGE // 2 + rows.start : EDGE // 2 + rows.stop, :]
        for p, other in enumerate(sides(ids, e, o)):
            if m == 0:
                pad[0:8, :] = jnp.zeros((8, LANES), F32)
                pad[8 : 8 + ROWS, :] = other
                pad[8 + ROWS :, :] = jnp.zeros((8, LANES), F32)
                other = window(pad, (), g, -1, 18)
            outer[m, p, 0:18, :] = 0.5 * (faces[m, 1, p, 0:18, :] + other)
    for d, src in enumerate((s0, s1, s2, s3)):
        for k in range(LOCAL):
            pos = LOCAL * d + k
            rows = slice(18 * pos, 18 * pos + 18)
            if pos < NEAR:
                o = near_odd(ids, near[rows, :], None if relayed is None else relayed[rows, :])
            else:
                o = far[18 * (pos - NEAR) : 18 * (pos - NEAR) + 18, :]
            for p, z in enumerate(sides(ids, ev[rows, :], o)):
                at = k * 40 + 20 * p + 1
                zz[pos, p, 0:18, :] = src[at : at + 18, :] - z
    acc[...] = inner[...]
    accumulate(trip, cf, acc, lambda m, j, p: outer[m, p] * zz[j, p])
    row = HELD * g - 1 + lax.broadcasted_iota(jnp.int32, (18, LANES), 0)
    inside = (row >= 0) & (row < ROWS)
    rates = [0.8 / (faces[0, 0, p, 0:18, :] + outer[0, p, 0:18, :]) for p in range(2)]
    for d, (start, src, out) in enumerate(
        ((s0, t0, b0), (s1, t1, b1), (s2, t2, b2), (s3, t3, b3))
    ):
        for k in range(LOCAL):
            pos = LOCAL * d + k
            helds = []
            for p in range(2):
                at = k * 36 + 18 * p
                first = src[at : at + 18, :] - acc[pos, p, 0:18, :]
                at = k * 40 + 20 * p + 1
                moved = start[at : at + 18, :] + first * rates[p] * cf[ENTRIES + pos]
                moved = jnp.where(inside, moved, 0.0)
                mid[pos, p, 7:25, :] = moved
                held = moved[1 : 1 + HELD]
                out[k, p] = held
                helds.append(held)
            even[pos] = jnp.where(top, helds[1], helds[0])
            (odd_a if pos < NEAR else odd_b)[pos % NEAR] = jnp.where(top, helds[0], helds[1])


def second_inner(trip, cf, mid, faces, acc, nxt, prv):
    for pos in range(SLOTS):
        for p in range(2):
            mine = mid[pos, p, 8:24, :]
            nxt[pos, p] = lane_next(mine)
            prv[pos, p] = lane_prev(mine)
    acc[...] = jnp.zeros(acc.shape, F32)
    held = slice(1, 1 + HELD)

    def term(m, j, p):
        total = faces[m, 0, p, held] * mid[j, p, 8:24, :]
        total += faces[m, 2, p, held] * mid[j, 1 - p, 8:24, :]
        total += faces[m, 3, p, held] * mid[j, p, 9:25, :] + faces[m, 4, p, held] * mid[j, p, 7:23, :]
        return total + (faces[m, 5, p, held] * nxt[j, p] + faces[m, 6, p, held] * prv[j, p])

    accumulate(trip, cf, acc, term)


def second_outer(trip, cf, ids, inner, outer, mid, *rest):
    relayed, rest = (rest[0], rest[1:]) if RELAY_SECOND else (None, rest)
    t0, t1, t2, t3, near, far, ev, o0, o1, o2, o3, acc, zz = rest
    for pos in range(SLOTS):
        if pos < NEAR:
            o = near_odd(ids, near[pos], None if relayed is None else relayed[pos])
        else:
            o = far[pos - NEAR]
        for p, z in enumerate(sides(ids, ev[pos], o)):
            zz[pos, p] = mid[pos, p, 8:24, :] - z
    acc[...] = inner[...]
    accumulate(trip, cf, acc, lambda m, j, p: outer[m, p, slice(1, 1 + HELD)] * zz[j, p])
    for d, (src, out) in enumerate(((t0, o0), (t1, o1), (t2, o2), (t3, o3))):
        for k in range(LOCAL):
            for p in range(2):
                at = k * 36 + 18 * p + 1
                out[k, p] = src[at : at + HELD, :] - acc[LOCAL * d + k, p]


def second_sweep(
    cf, ids, mean, far, ev, m0, m1, m2, m3, r0, r1, r2, r3, smoothed, residual, rate, pad
):
    g = ids[0]
    below, above = sides(ids, ev[EDGE : EDGE + ROWS, :], far[EDGE // 2 : EDGE // 2 + ROWS, :])
    pad[0:8, :] = jnp.zeros((8, LANES), F32)
    pad[8 + ROWS :, :] = jnp.zeros((8, LANES), F32)
    for p in range(2):
        own = mean[p]
        pad[8 : 8 + ROWS, :] = own
        others = (
            above if p else mean[1],
            mean[0] if p else below,
            pad[9 : 9 + ROWS, :], pad[7 : 7 + ROWS, :],
            lane_next(own), lane_prev(own),
        )
        total = None
        for other in others:
            face = 0.5 * (own + other)
            total = face if total is None else total + face
        rate[p] = 0.8 / total
    for d, (mid, res) in enumerate(((m0, r0), (m1, r1), (m2, r2), (m3, r3))):
        rows = pl.ds(pl.multiple_of(HELD * (g ^ d), HELD), HELD)
        for p in range(2):
            here = rate[p, rows, :]
            for k in range(LOCAL):
                left = res[k, p]
                residual[k, p, rows, :] = left
                smoothed[k, p, rows, :] = mid[k, p] + left * here * cf[ENTRIES + k]


def body(start_field, source, mean_field, kl_fields, triples, coef):
    g = lax.axis_index("mode").astype(jnp.int32)
    slab = lax.axis_index("space").astype(jnp.int32)
    ids = jnp.stack([g, slab % 2, ((slab % 4 == 0) | (slab % 4 == 3)).astype(jnp.int32)])
    modes = triples[:, 1:]
    at = LOCAL * ((modes // LOCAL) ^ g) + modes % LOCAL
    trip = jnp.concatenate([triples[:, 0], at[:, 0], at[:, 1]])
    diag = jnp.sum(
        jnp.where(
            (triples[:, 0:1] == 0) & (at[:, 0:1] == jnp.arange(SLOTS)[None]), coef[:, None], 0.0
        ),
        axis=0,
    )
    cf = jnp.concatenate([coef, 1.0 / diag])

    count = lax.axis_size("space")
    def both(pairs):
        return [pair for a, b in pairs for pair in ((a, b), (b, a))]

    evens = both([(i, i + 1) for i in range(0, count, 2)])
    odds = both([(i, i + 1) for i in range(1, count - 1, 2)])
    inner = [(i + 1, i + 2) for i in range(0, count, 4)]
    hops = both(inner + [(i, i + 3) for i in range(0, count, 4)])
    relay = [(i, i + 4) for i in range(0, count - 4, 4)]
    relay += [(i + 7, i + 3) for i in range(0, count - 4, 4)]

    def meet(x, pairs):
        return lax.ppermute(x, "space", pairs)

    def trade(parts):
        return [parts[0]] + [
            lax.ppermute(parts[d], "mode", [(i, i ^ d) for i in range(GROUPS)])
            for d in range(1, GROUPS)
        ]

    sends = pl.pallas_call(
        pack_start,
        out_shape=[shape(360, LANES)] * 4,
        in_specs=[SMEM, HBM],
        out_specs=[VMEM] * 4,
        scratch_shapes=[pltpu.VMEM((LOCAL, 2, ROWS + 16, LANES), F32), pltpu.SemaphoreType.DMA],
        name="pack_start",
        **PARAMS,
    )(ids, start_field)
    starts = trade(sends)
    fields = pl.pallas_call(
        pack_fields,
        out_shape=[shape(EDGE_FIELDS, LANES)] * 2,
        in_specs=[SMEM, HBM, HBM],
        out_specs=[VMEM] * 2,
        scratch_shapes=[
            pltpu.VMEM((FIELDS - 1, 2, ROWS + 16, LANES), F32),
            pltpu.SemaphoreType.DMA((3,)),
        ],
        name="pack_fields",
        **PARAMS,
    )(ids, mean_field, kl_fields)
    near = pl.pallas_call(
        pack_near,
        out_shape=shape(EDGE // 2, LANES),
        in_specs=[SMEM] + [VMEM] * 2,
        out_specs=VMEM,
        name="pack_near",
        **PARAMS,
    )(ids, *starts[:2])
    near = meet(near, hops if RELAY_FIRST else odds)
    even, odd = pl.pallas_call(
        pack_far,
        out_shape=[shape(EDGE + EDGE_FIELDS, LANES), shape(EDGE // 2 + EDGE_FIELDS, LANES)],
        in_specs=[SMEM] + [VMEM] * 6,
        out_specs=[VMEM] * 2,
        name="pack_far",
        **PARAMS,
    )(ids, *starts, *fields)
    edges = (near, meet(odd, odds), meet(even, evens))
    source, odd = lax.optimization_barrier((source, odd))
    sources = trade(pl.pallas_call(
        pack_source,
        out_shape=[shape(324, LANES)] * 4,
        in_specs=[SMEM, HBM],
        out_specs=[VMEM] * 4,
        scratch_shapes=[pltpu.VMEM((LOCAL, 2, ROWS + 16, LANES), F32), pltpu.SemaphoreType.DMA],
        name="pack_source",
        **PARAMS,
    )(ids, source))
    relayed = ()
    if RELAY_FIRST:
        near, sources[0] = lax.optimization_barrier((near, sources[0]))
        relayed = (meet(near, relay),)
    acc, faces = pl.pallas_call(
        first_inner,
        out_shape=[shape(SLOTS, 2, 24, LANES), shape(FIELDS, 7, 2, 24, LANES)],
        in_specs=[SMEM] * 3 + [VMEM] * 4 + [HBM] * 2,
        out_specs=[VMEM] * 2,
        scratch_shapes=[
            pltpu.VMEM((FIELDS, 2, ROWS + 16, LANES), F32),
            pltpu.VMEM((FIELDS, 2, 40, LANES), F32),
            pltpu.VMEM((SLOTS, 2, 40, LANES), F32),
            pltpu.VMEM((SLOTS, 2, 24, LANES), F32),
            pltpu.VMEM((SLOTS, 2, 24, LANES), F32),
            pltpu.SemaphoreType.DMA((2,)),
        ],
        cost_estimate=COST,
        name="first_inner",
        **PARAMS,
    )(trip, cf, ids, *starts, mean_field, kl_fields)
    operands = (trip, cf, ids, acc, faces, *relayed, *starts, *sources, *edges)
    mid, *mids, even, odd_a, odd_b, outer = pl.pallas_call(
        first_outer,
        out_shape=[shape(SLOTS, 2, 32, LANES)]
        + [shape(LOCAL, 2, HELD, LANES)] * 4
        + [shape(SLOTS, HELD, LANES)]
        + [shape(SLOTS // 2, HELD, LANES)] * 2
        + [shape(FIELDS, 2, 24, LANES)],
        in_specs=[SMEM] * 3 + [VMEM] * (len(operands) - 3),
        out_specs=[VMEM] * 9,
        scratch_shapes=[pltpu.VMEM((SLOTS, 2, 24, LANES), F32)] * 2
        + [pltpu.VMEM((ROWS + 16, LANES), F32)],
        name="first_outer",
        **PARAMS,
    )(*operands)
    near = meet(odd_a, hops if RELAY_SECOND else odds)
    met = (near, meet(odd_b, odds), meet(even, evens))
    relayed = (meet(near, relay),) if RELAY_SECOND else ()
    mids = trade(mids)
    acc = pl.pallas_call(
        second_inner,
        out_shape=shape(SLOTS, 2, HELD, LANES),
        in_specs=[SMEM] * 2 + [VMEM] * 2,
        out_specs=VMEM,
        scratch_shapes=[pltpu.VMEM((SLOTS, 2, HELD, LANES), F32)] * 2,
        cost_estimate=COST,
        name="second_inner",
        **PARAMS,
    )(trip, cf, mid, faces)
    operands = (trip, cf, ids, acc, outer, mid, *relayed, *sources, *met)
    lefts = pl.pallas_call(
        second_outer,
        out_shape=[shape(LOCAL, 2, HELD, LANES)] * 4,
        in_specs=[SMEM] * 3 + [VMEM] * (len(operands) - 3),
        out_specs=[VMEM] * 4,
        scratch_shapes=[pltpu.VMEM((SLOTS, 2, HELD, LANES), F32)] * 2,
        name="second_outer",
        **PARAMS,
    )(*operands)
    lefts = trade(lefts)
    smoothed, residual = pl.pallas_call(
        second_sweep,
        out_shape=[shape(LOCAL, 2, ROWS, LANES)] * 2,
        in_specs=[SMEM] * 2 + [VMEM] * 11,
        out_specs=[VMEM] * 2,
        scratch_shapes=[
            pltpu.VMEM((2, ROWS, LANES), F32),
            pltpu.VMEM((ROWS + 16, LANES), F32),
        ],
        name="second_sweep",
        **PARAMS,
    )(cf, ids, mean_field, *edges[1:], *mids, *lefts)
    return (smoothed, residual)


def solution(mesh):
    return jax.shard_map(
        body,
        mesh=mesh,
        in_specs=(
            P("mode", "space", None, None),
            P("mode", "space", None, None),
            P("space", None, None),
            P(None, "space", None, None),
            P(),
            P(),
        ),
        out_specs=(P("mode", "space", None, None), P("mode", "space", None, None)),
        check_vma=False,
    )
```

time: 97.8 us -> 77.7 us (0.79)
  the two profiles are of different devices: /device:TPU:71 before, /device:TPU:9 now
where the time goes in v2:
time: 77.7 us; the launch traced here: 77.3 us
  starting transfers between devices  35.9 us (46%)
  waiting for transfers between devices  18 us (23%)
  Pallas kernels  17.3 us (22%)
  local copies, waits for them, and re-layouts  2.87 us (4%)
  other arithmetic  2.44 us (3%)
  between operations  0.84 us (1%)
    ppermute x8, starting transfers between devices, meet(): return lax.ppermute(x, 'space', pairs)  22.4 us
    ppermute x12, waiting for transfers between devices, trade(): lax.ppermute(parts[d], 'mode', [(i, i ^ d) for i in range(GROUPS)])  16.3 us
    ppermute x12, starting transfers between devices, trade(): lax.ppermute(parts[d], 'mode', [(i, i ^ d) for i in range(GROUPS)])  13.6 us
    pallas_call x1, Pallas kernels, body(): pl.pallas_call(first_inner, out_shape=[shape(SLOTS, 2, 24, LANES), shape(...  4.41 us
    pallas_call x1, Pallas kernels, body(): pl.pallas_call(second_inner, out_shape=shape(SLOTS, 2, HELD, LANES), in_s...  3.49 us
    unnamed x14, local copies, waits for them, and re-layouts  2.86 us
    pallas_call x1, Pallas kernels, body(): pl.pallas_call(first_outer, out_shape=[shape(SLOTS, 2, 32, LANES)] + [sha...  2.45 us
    pallas_call x1, Pallas kernels, body(): pl.pallas_call(second_outer, out_shape=[shape(LOCAL, 2, HELD, LANES)] * 4...  2.02 us
  transfers between devices with their start and end apart: 20, of which 8 were waited for; matrix products, arithmetic and copies ran while one was open for 3% of the time, Pallas kernels for 16%

profile of v2, /device:TPU:9, one launch (start us, length us, event | category | flops | bytes accessed | tf_op | source)
XLA Modules:
  0.0 77.3 jit_solution(16465254895045318396)
XLA Ops:
  0.7 1.1 %copy-done.4 = f32[9,2,64,128]{3,2,1,0:T(8,128)S(1)} copy-done((f32[9,2,64,128]{3,2,1,0:T(8,128)S(1)}, f32[9,2,64,128]{3,2,1,0:T(8,128)}, u32[]{:S(2)}) %copy-start.4) | copy-done | bytes 589848
  3.2 1.7 %collective-permute-start.1 = (f32[360,128]{1,0:T(8,128)S(1)}, f32[360,128]{1,0:T(8,128)S(1)}, u32[]{:S(2)}, u32[]{:S(2)}) collective-permute-start(f32[360,128]{1,0:T(8,128)S(1)} %get-tuple-element.34), channel_id=1, source_target_pairs={{0,2},{1,3},{2,0},{3,1},{4,6},{5,7},{6,4},{7,5},{8,10},{9,11},{10,... | collective-permute-start | bytes 552968 | tf_op jit(solution)/shard_map/ppermute | solution.py:338
  5.7 0.9 %copy-done = f32[4,2,64,128]{3,2,1,0:T(8,128)S(1)} copy-done((f32[4,2,64,128]{3,2,1,0:T(8,128)S(1)}, f32[4,2,64,128]{3,2,1,0:T(8,128)}, u32[]{:S(2)}) %copy-start) | copy-done | bytes 262168
  10.3 2.6 %collective-permute-start.5 = (f32[324,128]{1,0:T(8,128)S(1)}, f32[324,128]{1,0:T(8,128)S(1)}, u32[]{:S(2)}, u32[]{:S(2)}) collective-permute-start(f32[324,128]{1,0:T(8,128)S(1)} %pack_near.1), channel_id=1, source_target_pairs={{4,8},{8,4},{20,24},{24,20},{36,40},{40,36},{52,56},{56,52},{68,72... | collective-permute-start | bytes 497672 | tf_op jit(solution)/shard_map/ppermute | solution.py:334
  12.9 0.9 %collective-permute-done.2.s3.rest_4_ = f32[360,128]{1,0:T(8,128)S(1)} collective-permute-done((f32[360,128]{1,0:T(8,128)S(1)}, f32[360,128]{1,0:T(8,128)S(1)}, u32[]{:S(2)}, u32[]{:S(2)}) %collective-permute-start.2) | collective-permute-done | bytes 184352 | tf_op jit(solution)/shard_map/ppermute | solution.py:338
  14.3 9.9 %collective-permute-start.3 = (f32[460,128]{1,0:T(8,128)S(1)}, f32[460,128]{1,0:T(8,128)S(1)}, u32[]{:S(2)}, u32[]{:S(2)}) collective-permute-start(f32[460,128]{1,0:T(8,128)S(1)} %get-tuple-element.38), channel_id=1, source_target_pairs={{4,8},{8,4},{12,16},{16,12},{20,24},{24,20},{28,32},{32,28},{36,40... | collective-permute-start | bytes 706568 | tf_op jit(solution)/shard_map/ppermute | solution.py:334
  26.4 1.0 %collective-permute-start.9 = (f32[324,128]{1,0:T(8,128)S(1)}, f32[324,128]{1,0:T(8,128)S(1)}, u32[]{:S(2)}, u32[]{:S(2)}) collective-permute-start(f32[324,128]{1,0:T(8,128)S(1)} %get-tuple-element.48), channel_id=1, source_target_pairs={{0,3},{1,2},{2,1},{3,0},{4,7},{5,6},{6,5},{7,4},{8,11},{9,10},{10,... | collective-permute-start | bytes 497672 | tf_op jit(solution)/shard_map/ppermute | solution.py:338
  27.3 1.9 %collective-permute-start.6 = (f32[324,128]{1,0:T(8,128)S(1)}, f32[324,128]{1,0:T(8,128)S(1)}, u32[]{:S(2)}, u32[]{:S(2)}) collective-permute-start(f32[324,128]{1,0:T(8,128)S(1)} %collective-permute-done.5.rest_9_), channel_id=1, source_target_pairs={{0,16},{16,32},{32,48},{48,64},{64,80},{80,96},{96,112},{112,128},... | collective-permute-start | bytes 497672 | tf_op jit(solution)/shard_map/ppermute | solution.py:334
  29.4 4.4 %first_inner.1 = (f32[36,2,24,128]{3,2,1,0:T(8,128)S(1)}, f32[5,7,2,24,128]{4,3,2,1,0:T(8,128)S(1)}) custom-call(s32[468]{0:T(512)S(1)} %pad_add_fusion.trip, f32[192]{0:T(256)S(1)} %pad_maximum_fusion.cf, s32[3]{0:T(128)S(1)} %pad_add_fusion.1.ids, f32[360,128]{1,0:T(8,128)S(1)} %get-tuple-element.32.s0.rest_1_, ...), custom_call_target="tpu_custom_call" | custom-call | flops 20000000 | bytes 12000000 | tf_op jit(solution)/shard_map/first_inner/pallas_call | solution.py:396
  33.8 4.8 %collective-permute-done.8.rest_7_.rest_3_ = f32[324,128]{1,0:T(8,128)S(1)} collective-permute-done((f32[324,128]{1,0:T(8,128)S(1)}, f32[324,128]{1,0:T(8,128)S(1)}, u32[]{:S(2)}, u32[]{:S(2)}) %collective-permute-start.8) | collective-permute-done | bytes 165920 | tf_op jit(solution)/shard_map/ppermute | solution.py:338
  38.6 3.7 %collective-permute-done.9.rest_8_.rest_4_ = f32[324,128]{1,0:T(8,128)S(1)} collective-permute-done((f32[324,128]{1,0:T(8,128)S(1)}, f32[324,128]{1,0:T(8,128)S(1)}, u32[]{:S(2)}, u32[]{:S(2)}) %collective-permute-start.9) | collective-permute-done | bytes 165920 | tf_op jit(solution)/shard_map/ppermute | solution.py:338
  42.7 2.4 %first_outer.1 = (f32[36,2,32,128]{3,2,1,0:T(8,128)S(1)}, f32[9,2,16,128]{3,2,1,0:T(8,128)S(1)}, f32[9,2,16,128]{3,2,1,0:T(8,128)S(1)}, f32[9,2,16,128]{3,2,1,0:...) custom-call(s32[468]{0:T(512)S(1)} %pad_add_fusion.trip, ...), custom_call_target="tpu_custom_call" | custom-call | tf_op jit(solution)/shard_map/first_outer/pallas_call | solution.py:414
  45.3 4.7 %collective-permute-start.15 = (f32[18,16,128]{2,1,0:T(8,128)S(1)}, f32[18,16,128]{2,1,0:T(8,128)S(1)}, u32[]{:S(2)}, u32[]{:S(2)}) collective-permute-start(f32[18,16,128]{2,1,0:T(8,128)S(1)} %get-tuple-element.56), channel_id=1, source_target_pairs={{4,8},{8,4},{12,16},{16,12},{20,24},{24,20},{28,32},{32,28},{36,40... | collective-permute-start | bytes 442376 | tf_op jit(solution)/shard_map/ppermute | solution.py:334
  50.0 0.9 %collective-permute-done.13.rest_5_ = f32[18,16,128]{2,1,0:T(8,128)S(1)} collective-permute-done((f32[18,16,128]{2,1,0:T(8,128)S(1)}, f32[18,16,128]{2,1,0:T(8,128)S(1)}, u32[]{:S(2)}, u32[]{:S(2)}) %collective-permute-start.13) | collective-permute-done | bytes 147488 | tf_op jit(solution)/shard_map/ppermute | solution.py:334
  50.9 3.1 %collective-permute-start.14 = (f32[18,16,128]{2,1,0:T(8,128)S(1)}, f32[18,16,128]{2,1,0:T(8,128)S(1)}, u32[]{:S(2)}, u32[]{:S(2)}) collective-permute-start(f32[18,16,128]{2,1,0:T(8,128)S(1)} %collective-permute-done.13.rest_5_), channel_id=1, source_target_pairs={{0,16},{16,32},{32,48},{48,64},{64,80},{80,96},{96,112},{112,128},... | collective-permute-start | bytes 442376 | tf_op jit(solution)/shard_map/ppermute | solution.py:334
  54.0 2.1 %collective-permute-start.10 = (f32[9,2,16,128]{3,2,1,0:T(8,128)S(1)}, f32[9,2,16,128]{3,2,1,0:T(8,128)S(1)}, u32[]{:S(2)}, u32[]{:S(2)}) collective-permute-start(f32[9,2,16,128]{3,2,1,0:T(8,128)S(1)} %get-tuple-element.50), channel_id=1, source_target_pairs={{0,1},{1,0},{2,3},{3,2},{4,5},{5,4},{6,7},{7,6},{8,9},{9,8},{10,11... | collective-permute-start | bytes 442376 | tf_op jit(solution)/shard_map/ppermute | solution.py:338
  56.2 3.5 %second_inner.1.inner = f32[36,2,16,128]{3,2,1,0:T(8,128)S(1)} custom-call(s32[468]{0:T(512)S(1)} %pad_add_fusion.trip, f32[192]{0:T(256)S(1)} %pad_maximum_fusion.cf, f32[36,2,32,128]{3,2,1,0:T(8,128)S(1)} %get-tuple-element.53.mid, f32[5,7,2,24,128]{4,3,2,1,0:T(8,128)S(1)} %get-tuple-element.41.faces), custom_call_target="tpu_custom_call" | custom-call | flops 20000000 | bytes 12000000 | tf_op jit(solution)/shard_map/second_inner/pallas_call | solution.py:432
  60.0 3.2 %collective-permute-start.12 = (f32[9,2,16,128]{3,2,1,0:T(8,128)S(1)}, f32[9,2,16,128]{3,2,1,0:T(8,128)S(1)}, u32[]{:S(2)}, u32[]{:S(2)}) collective-permute-start(f32[9,2,16,128]{3,2,1,0:T(8,128)S(1)} %get-tuple-element.52), channel_id=1, source_target_pairs={{0,3},{1,2},{2,1},{3,0},{4,7},{5,6},{6,5},{7,4},{8,11},{9,10},{10,... | collective-permute-start | bytes 442376 | tf_op jit(solution)/shard_map/ppermute | solution.py:338
  63.2 2.0 %second_outer.1 = (f32[9,2,16,128]{3,2,1,0:T(8,128)S(1)}, f32[9,2,16,128]{3,2,1,0:T(8,128)S(1)}, f32[9,2,16,128]{3,2,1,0:T(8,128)S(1)}, f32[9,2,16,128]{3,2,1,0:T(8,128)S(1)}) custom-call(s32[468]{0:T(512)S(1)} %pad_add_fusion.trip, f32[192]{0:T(256)S(1)} %pad_maximum_fusion.cf, s32[3]{0:T(128)S(1)} %pad_add_fusion.1.ids, ...), custom_call_target="tpu_custom_call" | custom-call | tf_op jit(solution)/shard_map/second_outer/pallas_call | solution.py:443
  65.2 1.7 %collective-permute-start.17 = (f32[9,2,16,128]{3,2,1,0:T(8,128)S(1)}, f32[9,2,16,128]{3,2,1,0:T(8,128)S(1)}, u32[]{:S(2)}, u32[]{:S(2)}) collective-permute-start(f32[9,2,16,128]{3,2,1,0:T(8,128)S(1)} %get-tuple-element.59), channel_id=1, source_target_pairs={{0,1},{1,0},{2,3},{3,2},{4,5},{5,4},{6,7},{7,6},{8,9},{9,8},{10,11... | collective-permute-start | bytes 442376 | tf_op jit(solution)/shard_map/ppermute | solution.py:338
  67.7 0.9 %collective-permute-start.19 = (f32[9,2,16,128]{3,2,1,0:T(8,128)S(1)}, f32[9,2,16,128]{3,2,1,0:T(8,128)S(1)}, u32[]{:S(2)}, u32[]{:S(2)}) collective-permute-start(f32[9,2,16,128]{3,2,1,0:T(8,128)S(1)} %get-tuple-element.61), channel_id=1, source_target_pairs={{0,3},{1,2},{2,1},{3,0},{4,7},{5,6},{6,5},{7,4},{8,11},{9,10},{10,... | collective-permute-start | bytes 442376 | tf_op jit(solution)/shard_map/ppermute | solution.py:338
  68.6 3.7 %collective-permute-done.18.r2 = f32[9,2,16,128]{3,2,1,0:T(8,128)S(1)} collective-permute-done((f32[9,2,16,128]{3,2,1,0:T(8,128)S(1)}, f32[9,2,16,128]{3,2,1,0:T(8,128)S(1)}, u32[]{:S(2)}, u32[]{:S(2)}) %collective-permute-start.18) | collective-permute-done | bytes 147488 | tf_op jit(solution)/shard_map/ppermute | solution.py:338
  72.3 3.3 %collective-permute-done.19.r3 = f32[9,2,16,128]{3,2,1,0:T(8,128)S(1)} collective-permute-done((f32[9,2,16,128]{3,2,1,0:T(8,128)S(1)}, f32[9,2,16,128]{3,2,1,0:T(8,128)S(1)}, u32[]{:S(2)}, u32[]{:S(2)}) %collective-permute-start.19) | collective-permute-done | bytes 147488 | tf_op jit(solution)/shard_map/ppermute | solution.py:338
  75.7 1.7 %second_sweep.1 = (f32[9,2,64,128]{3,2,1,0:T(8,128)}, f32[9,2,64,128]{3,2,1,0:T(8,128)}) custom-call(f32[192]{0:T(256)S(1)} %pad_maximum_fusion.cf, s32[3]{0:T(128)S(1)} %pad_add_fusion.1.ids, f32[2,64,128]{2,1,0:T(8,128)S(1)} %copy-done.3, f32[460,128]{1,0:T(8,128)S(1)} %collective-permute-done.3.rest_10_.far, ...), custom_call_target="tpu_custom_call" | custom-call | tf_op jit(solution)/shard_map/second_sweep/pallas_call | solution.py:453
  (50 shorter events, 10.5 us)
Async XLA Ops:
  1.8 22.5 %copy-start.5 = (f32[9,2,64,128]{3,2,1,0:T(8,128)S(1)}, f32[9,2,64,128]{3,2,1,0:T(8,128)}, u32[]{:S(2)}) copy-start(f32[9,2,64,128]{3,2,1,0:T(8,128)} %source) | copy-start | bytes 1769476
  2.5 7.2 %collective-permute-start = (f32[360,128]{1,0:T(8,128)S(1)}, f32[360,128]{1,0:T(8,128)S(1)}, u32[]{:S(2)}, u32[]{:S(2)}) collective-permute-start(f32[360,128]{1,0:T(8,128)S(1)} %get-tuple-element.33), channel_id=1, source_target_pairs={{0,1},{1,0},{2,3},{3,2},{4,5},{5,4},{6,7},{7,6},{8,9},{9,8},{10,11... | collective-permute-start | bytes 552968 | tf_op jit(solution)/shard_map/ppermute | solution.py:338
  3.2 9.6 %collective-permute-start.1 = (f32[360,128]{1,0:T(8,128)S(1)}, f32[360,128]{1,0:T(8,128)S(1)}, u32[]{:S(2)}, u32[]{:S(2)}) collective-permute-start(f32[360,128]{1,0:T(8,128)S(1)} %get-tuple-element.34), channel_id=1, source_target_pairs={{0,2},{1,3},{2,0},{3,1},{4,6},{5,7},{6,4},{7,5},{8,10},{9,11},{10,... | collective-permute-start | bytes 552968 | tf_op jit(solution)/shard_map/ppermute | solution.py:338
  4.9 8.8 %collective-permute-start.2 = (f32[360,128]{1,0:T(8,128)S(1)}, f32[360,128]{1,0:T(8,128)S(1)}, u32[]{:S(2)}, u32[]{:S(2)}) collective-permute-start(f32[360,128]{1,0:T(8,128)S(1)} %get-tuple-element.35), channel_id=1, source_target_pairs={{0,3},{1,2},{2,1},{3,0},{4,7},{5,6},{6,5},{7,4},{8,11},{9,10},{10,... | collective-permute-start | bytes 552968 | tf_op jit(solution)/shard_map/ppermute | solution.py:338
  7.5 21.8 %slice-start = ((s32[156,3]{0,1:T(4,128)}), s32[156,1]{0,1:T(1,128)S(1)}, s32[]{:S(2)}) async-start(s32[156,3]{0,1:T(4,128)} %param.10), calls=%async_computation | async-start | bytes 2048 | tf_op jit(solution)/shard_map/slice | solution.py:316
  7.5 21.9 %copy-start.1 = (f32[4,2,64,128]{3,2,1,0:T(8,128)S(1)}, f32[4,2,64,128]{3,2,1,0:T(8,128)}, u32[]{:S(2)}) copy-start(f32[4,2,64,128]{3,2,1,0:T(8,128)} %kl.3) | copy-start | bytes 786436
  7.5 21.9 %copy-start.3 = (f32[2,64,128]{2,1,0:T(8,128)S(1)}, f32[2,64,128]{2,1,0:T(8,128)}, u32[]{:S(2)}) copy-start(f32[2,64,128]{2,1,0:T(8,128)} %mean.5) | copy-start | bytes 196612
  10.3 16.1 %collective-permute-start.5 = (f32[324,128]{1,0:T(8,128)S(1)}, f32[324,128]{1,0:T(8,128)S(1)}, u32[]{:S(2)}, u32[]{:S(2)}) collective-permute-start(f32[324,128]{1,0:T(8,128)S(1)} %pack_near.1), channel_id=1, source_target_pairs={{4,8},{8,4},{20,24},{24,20},{36,40},{40,36},{52,56},{56,52},{68,72... | collective-permute-start | bytes 497672 | tf_op jit(solution)/shard_map/ppermute | solution.py:334
  14.3 27.9 %collective-permute-start.3 = (f32[460,128]{1,0:T(8,128)S(1)}, f32[460,128]{1,0:T(8,128)S(1)}, u32[]{:S(2)}, u32[]{:S(2)}) collective-permute-start(f32[460,128]{1,0:T(8,128)S(1)} %get-tuple-element.38), channel_id=1, source_target_pairs={{4,8},{8,4},{12,16},{16,12},{20,24},{24,20},{28,32},{32,28},{36,40... | collective-permute-start | bytes 706568 | tf_op jit(solution)/shard_map/ppermute | solution.py:334
  24.2 18.5 %collective-permute-start.4 = (f32[784,128]{1,0:T(8,128)S(1)}, f32[784,128]{1,0:T(8,128)S(1)}, u32[]{:S(2)}, u32[]{:S(2)}) collective-permute-start(f32[784,128]{1,0:T(8,128)S(1)} %get-tuple-element.39), channel_id=1, source_target_pairs={{0,4},{4,0},{8,12},{12,8},{16,20},{20,16},{24,28},{28,24},{32,36},... | collective-permute-start | bytes 1204232 | tf_op jit(solution)/shard_map/ppermute | solution.py:334
  25.0 2.3 %collective-permute-start.7 = (f32[324,128]{1,0:T(8,128)S(1)}, f32[324,128]{1,0:T(8,128)S(1)}, u32[]{:S(2)}, u32[]{:S(2)}) collective-permute-start(f32[324,128]{1,0:T(8,128)S(1)} %get-tuple-element.46), channel_id=1, source_target_pairs={{0,1},{1,0},{2,3},{3,2},{4,5},{5,4},{6,7},{7,6},{8,9},{9,8},{10,11... | collective-permute-start | bytes 497672 | tf_op jit(solution)/shard_map/ppermute | solution.py:338
  25.6 13.0 %collective-permute-start.8 = (f32[324,128]{1,0:T(8,128)S(1)}, f32[324,128]{1,0:T(8,128)S(1)}, u32[]{:S(2)}, u32[]{:S(2)}) collective-permute-start(f32[324,128]{1,0:T(8,128)S(1)} %get-tuple-element.47), channel_id=1, source_target_pairs={{0,2},{1,3},{2,0},{3,1},{4,6},{5,7},{6,4},{7,5},{8,10},{9,11},{10,... | collective-permute-start | bytes 497672 | tf_op jit(solution)/shard_map/ppermute | solution.py:338
  26.4 15.9 %collective-permute-start.9 = (f32[324,128]{1,0:T(8,128)S(1)}, f32[324,128]{1,0:T(8,128)S(1)}, u32[]{:S(2)}, u32[]{:S(2)}) collective-permute-start(f32[324,128]{1,0:T(8,128)S(1)} %get-tuple-element.48), channel_id=1, source_target_pairs={{0,3},{1,2},{2,1},{3,0},{4,7},{5,6},{6,5},{7,4},{8,11},{9,10},{10,... | collective-permute-start | bytes 497672 | tf_op jit(solution)/shard_map/ppermute | solution.py:338
  27.3 15.3 %collective-permute-start.6 = (f32[324,128]{1,0:T(8,128)S(1)}, f32[324,128]{1,0:T(8,128)S(1)}, u32[]{:S(2)}, u32[]{:S(2)}) collective-permute-start(f32[324,128]{1,0:T(8,128)S(1)} %collective-permute-done.5.rest_9_), channel_id=1, source_target_pairs={{0,16},{16,32},{32,48},{48,64},{64,80},{80,96},{96,112},{112,128},... | collective-permute-start | bytes 497672 | tf_op jit(solution)/shard_map/ppermute | solution.py:334
  45.1 5.8 %collective-permute-start.13 = (f32[18,16,128]{2,1,0:T(8,128)S(1)}, f32[18,16,128]{2,1,0:T(8,128)S(1)}, u32[]{:S(2)}, u32[]{:S(2)}) collective-permute-start(f32[18,16,128]{2,1,0:T(8,128)S(1)} %get-tuple-element.55), channel_id=1, source_target_pairs={{4,8},{8,4},{20,24},{24,20},{36,40},{40,36},{52,56},{56,52},{68,72... | collective-permute-start | bytes 442376 | tf_op jit(solution)/shard_map/ppermute | solution.py:334
  45.2 17.9 %collective-permute-start.16 = (f32[36,16,128]{2,1,0:T(8,128)S(1)}, f32[36,16,128]{2,1,0:T(8,128)S(1)}, u32[]{:S(2)}, u32[]{:S(2)}) collective-permute-start(f32[36,16,128]{2,1,0:T(8,128)S(1)} %get-tuple-element.57), channel_id=1, source_target_pairs={{0,4},{4,0},{8,12},{12,8},{16,20},{20,16},{24,28},{28,24},{32,36},... | collective-permute-start | bytes 884744 | tf_op jit(solution)/shard_map/ppermute | solution.py:334
  45.3 14.7 %collective-permute-start.15 = (f32[18,16,128]{2,1,0:T(8,128)S(1)}, f32[18,16,128]{2,1,0:T(8,128)S(1)}, u32[]{:S(2)}, u32[]{:S(2)}) collective-permute-start(f32[18,16,128]{2,1,0:T(8,128)S(1)} %get-tuple-element.56), channel_id=1, source_target_pairs={{4,8},{8,4},{12,16},{16,12},{20,24},{24,20},{28,32},{32,28},{36,40... | collective-permute-start | bytes 442376 | tf_op jit(solution)/shard_map/ppermute | solution.py:334
  50.9 12.2 %collective-permute-start.14 = (f32[18,16,128]{2,1,0:T(8,128)S(1)}, f32[18,16,128]{2,1,0:T(8,128)S(1)}, u32[]{:S(2)}, u32[]{:S(2)}) collective-permute-start(f32[18,16,128]{2,1,0:T(8,128)S(1)} %collective-permute-done.13.rest_5_), channel_id=1, source_target_pairs={{0,16},{16,32},{32,48},{48,64},{64,80},{80,96},{96,112},{112,128},... | collective-permute-start | bytes 442376 | tf_op jit(solution)/shard_map/ppermute | solution.py:334
  54.0 13.7 %collective-permute-start.10 = (f32[9,2,16,128]{3,2,1,0:T(8,128)S(1)}, f32[9,2,16,128]{3,2,1,0:T(8,128)S(1)}, u32[]{:S(2)}, u32[]{:S(2)}) collective-permute-start(f32[9,2,16,128]{3,2,1,0:T(8,128)S(1)} %get-tuple-element.50), channel_id=1, source_target_pairs={{0,1},{1,0},{2,3},{3,2},{4,5},{5,4},{6,7},{7,6},{8,9},{9,8},{10,11... | collective-permute-start | bytes 442376 | tf_op jit(solution)/shard_map/ppermute | solution.py:338
  56.2 12.5 %collective-permute-start.11 = (f32[9,2,16,128]{3,2,1,0:T(8,128)S(1)}, f32[9,2,16,128]{3,2,1,0:T(8,128)S(1)}, u32[]{:S(2)}, u32[]{:S(2)}) collective-permute-start(f32[9,2,16,128]{3,2,1,0:T(8,128)S(1)} %get-tuple-element.51), channel_id=1, source_target_pairs={{0,2},{1,3},{2,0},{3,1},{4,6},{5,7},{6,4},{7,5},{8,10},{9,11},{10,... | collective-permute-start | bytes 442376 | tf_op jit(solution)/shard_map/ppermute | solution.py:338
  60.0 8.6 %collective-permute-start.12 = (f32[9,2,16,128]{3,2,1,0:T(8,128)S(1)}, f32[9,2,16,128]{3,2,1,0:T(8,128)S(1)}, u32[]{:S(2)}, u32[]{:S(2)}) collective-permute-start(f32[9,2,16,128]{3,2,1,0:T(8,128)S(1)} %get-tuple-element.52), channel_id=1, source_target_pairs={{0,3},{1,2},{2,1},{3,0},{4,7},{5,6},{6,5},{7,4},{8,11},{9,10},{10,... | collective-permute-start | bytes 442376 | tf_op jit(solution)/shard_map/ppermute | solution.py:338
  65.2 3.5 %collective-permute-start.17 = (f32[9,2,16,128]{3,2,1,0:T(8,128)S(1)}, f32[9,2,16,128]{3,2,1,0:T(8,128)S(1)}, u32[]{:S(2)}, u32[]{:S(2)}) collective-permute-start(f32[9,2,16,128]{3,2,1,0:T(8,128)S(1)} %get-tuple-element.59), channel_id=1, source_target_pairs={{0,1},{1,0},{2,3},{3,2},{4,5},{5,4},{6,7},{7,6},{8,9},{9,8},{10,11... | collective-permute-start | bytes 442376 | tf_op jit(solution)/shard_map/ppermute | solution.py:338
  66.9 5.4 %collective-permute-start.18 = (f32[9,2,16,128]{3,2,1,0:T(8,128)S(1)}, f32[9,2,16,128]{3,2,1,0:T(8,128)S(1)}, u32[]{:S(2)}, u32[]{:S(2)}) collective-permute-start(f32[9,2,16,128]{3,2,1,0:T(8,128)S(1)} %get-tuple-element.60), channel_id=1, source_target_pairs={{0,2},{1,3},{2,0},{3,1},{4,6},{5,7},{6,4},{7,5},{8,10},{9,11},{10,... | collective-permute-start | bytes 442376 | tf_op jit(solution)/shard_map/ppermute | solution.py:338
  67.7 8.0 %collective-permute-start.19 = (f32[9,2,16,128]{3,2,1,0:T(8,128)S(1)}, f32[9,2,16,128]{3,2,1,0:T(8,128)S(1)}, u32[]{:S(2)}, u32[]{:S(2)}) collective-permute-start(f32[9,2,16,128]{3,2,1,0:T(8,128)S(1)} %get-tuple-element.61), channel_id=1, source_target_pairs={{0,3},{1,2},{2,1},{3,0},{4,7},{5,6},{6,5},{7,4},{8,11},{9,10},{10,... | collective-permute-start | bytes 442376 | tf_op jit(solution)/shard_map/ppermute | solution.py:338
  (4 other events, 24.6 us)

commit v3 on v2

--- a/solution.py
+++ b/solution.py
@@ -14,7 +14,7 @@
 ENTRIES = 156
 EDGE = 18 * SLOTS
 EDGE_FIELDS = ROWS + 18 * (FIELDS - 1)
-RELAY_FIRST, RELAY_SECOND = True, True
+UNROLL = 2
 NEAR = 2 * LOCAL
 F32 = jnp.float32
 VMEM = pl.BlockSpec(memory_space=pltpu.VMEM)
@@ -52,14 +52,27 @@
     return jnp.where(lane == 0, 0.0, pltpu.roll(x, 1, x.ndim - 1))
 
 
-def pack_start(ids, start, o0, o1, o2, o3, padded, sem):
+def pack_start(ids, start, o0, o1, o2, o3):
     g = ids[0]
-    fill_padded(start, padded, sem).wait()
     for d, out in enumerate((o0, o1, o2, o3)):
-        for p in range(2):
+        q = g ^ d
+        before = pl.ds(pl.multiple_of(jnp.maximum(HELD * q - 8, 0), 8), 8)
+        here = pl.ds(pl.multiple_of(HELD * q, HELD), HELD)
+        after = pl.ds(pl.multiple_of(jnp.minimum(HELD * q + HELD, ROWS - 8), 8), 8)
+        for k in range(LOCAL):
+            for p in range(2):
+                rows = [start[k, p, at, :] for at in (before, here, after)]
+                at = k * 40 + 20 * p
+                out[at : at + 20, :] = jnp.concatenate(rows, axis=0)[6:26]
+
+        def clear(first):
             for k in range(LOCAL):
-                at = k * 40 + 20 * p
-                out[at : at + 20, :] = window(padded, (k, p), g ^ d, -2, 20)
+                for p in range(2):
+                    at = k * 40 + 20 * p + first
+                    out[at : at + 2, :] = jnp.zeros((2, LANES), F32)
+
+        pl.when(q == 0)(functools.partial(clear, 0))
+        pl.when(q == GROUPS - 1)(functools.partial(clear, 18))
 
 
 def pack_fields(ids, mean, kl, even, odd, klp, sems):
@@ -123,22 +136,25 @@
 
 
 def near_odd(ids, straight, relayed):
-    return straight if relayed is None else jnp.where(ids[2] == 1, relayed, straight)
-
-
-def accumulate(trip, cf, acc, term):
+    return jnp.where(ids[2] == 1, relayed, straight)
+
+
+def accumulate(trip, coef, accs, term, visit=None):
     def step(e, carry):
-        m, i, j = trip[e], trip[ENTRIES + e], trip[2 * ENTRIES + e]
-        c = cf[e]
-        for p in range(2):
-            acc[i, p] += c * term(m, j, p)
+        for lane, acc in enumerate(accs):
+            n = e * len(accs) + lane
+            m, i, j, c = trip[n], trip[ENTRIES + n], trip[2 * ENTRIES + n], coef[n]
+            if visit is not None:
+                visit(m, i, c)
+            for p in range(2):
+                acc[i, p] += c * term(m, j, p)
         return carry
 
-    lax.fori_loop(0, ENTRIES, step, 0, unroll=2)
+    lax.fori_loop(0, ENTRIES // len(accs), step, 0, unroll=UNROLL)
 
 
 def first_inner(
-    trip, cf, ids, s0, s1, s2, s3, mean, kl, acc, faces, klp, ae, vv, nxt, prv, sems
+    trip, coef, ids, s0, s1, s2, s3, mean, kl, acc, faces, inverse, klp, ae, vv, nxt, prv, diag, sems
 ):
     g = ids[0]
     one = fill_padded(mean, klp.at[0], sems.at[0])
@@ -178,15 +194,20 @@
         total += faces[m, 3, p] * vv[j, p, 9:33, :] + faces[m, 4, p] * vv[j, p, 7:31, :]
         return total + (faces[m, 5, p] * nxt[j, p] + faces[m, 6, p] * prv[j, p])
 
-    accumulate(trip, cf, acc, term)
+    def visit(m, i, c):
+        diag[jnp.where(m == 0, i, SLOTS)] = c
+
+    accumulate(trip, coef, (acc,), term, visit)
+    for pos in range(SLOTS):
+        inverse[pos : pos + 1, :] = 1.0 / jnp.full((1, LANES), diag[pos], F32)
 
 
 def first_outer(
-    trip, cf, ids, inner, faces, *rest
+    trip, coef, ids, inner, faces, inverse, *rest
 ):
-    relayed, rest = (rest[0], rest[1:]) if RELAY_FIRST else (None, rest)
+    relayed, *rest = rest
     s0, s1, s2, s3, t0, t1, t2, t3, near, far, ev = rest[:11]
-    mid, b0, b1, b2, b3, even, odd_a, odd_b, outer, acc, zz, pad = rest[11:]
+    mid, b0, b1, b2, b3, even, odd_a, odd_b, outer, acc, more, zz, pad = rest[11:]
     g, top = ids[0], ids[1] == 0
     for m in range(FIELDS):
         at = ROWS + 18 * (m - 1)
@@ -205,14 +226,15 @@
             pos = LOCAL * d + k
             rows = slice(18 * pos, 18 * pos + 18)
             if pos < NEAR:
-                o = near_odd(ids, near[rows, :], None if relayed is None else relayed[rows, :])
+                o = near_odd(ids, near[rows, :], relayed[rows, :])
             else:
                 o = far[18 * (pos - NEAR) : 18 * (pos - NEAR) + 18, :]
             for p, z in enumerate(sides(ids, ev[rows, :], o)):
                 at = k * 40 + 20 * p + 1
                 zz[pos, p, 0:18, :] = src[at : at + 18, :] - z
     acc[...] = inner[...]
-    accumulate(trip, cf, acc, lambda m, j, p: outer[m, p] * zz[j, p])
+    more[...] = jnp.zeros(more.shape, F32)
+    accumulate(trip, coef, (acc, more), lambda m, j, p: outer[m, p] * zz[j, p])
     row = HELD * g - 1 + lax.broadcasted_iota(jnp.int32, (18, LANES), 0)
     inside = (row >= 0) & (row < ROWS)
     rates = [0.8 / (faces[0, 0, p, 0:18, :] + outer[0, p, 0:18, :]) for p in range(2)]
@@ -224,9 +246,9 @@
             helds = []
             for p in range(2):
                 at = k * 36 + 18 * p
-                first = src[at : at + 18, :] - acc[pos, p, 0:18, :]
+                first = src[at : at + 18, :] - (acc[pos, p, 0:18, :] + more[pos, p, 0:18, :])
                 at = k * 40 + 20 * p + 1
-                moved = start[at : at + 18, :] + first * rates[p] * cf[ENTRIES + pos]
+                moved = start[at : at + 18, :] + first * rates[p] * inverse[pos : pos + 1, :]
                 moved = jnp.where(inside, moved, 0.0)
                 mid[pos, p, 7:25, :] = moved
                 held = moved[1 : 1 + HELD]
@@ -236,7 +258,7 @@
             (odd_a if pos < NEAR else odd_b)[pos % NEAR] = jnp.where(top, helds[0], helds[1])
 
 
-def second_inner(trip, cf, mid, faces, acc, nxt, prv):
+def second_inner(trip, coef, ids, mid, faces, acc, nxt, prv):
     for pos in range(SLOTS):
         for p in range(2):
             mine = mid[pos, p, 8:24, :]
@@ -251,32 +273,32 @@
         total += faces[m, 3, p, held] * mid[j, p, 9:25, :] + faces[m, 4, p, held] * mid[j, p, 7:23, :]
         return total + (faces[m, 5, p, held] * nxt[j, p] + faces[m, 6, p, held] * prv[j, p])
 
-    accumulate(trip, cf, acc, term)
-
-
-def second_outer(trip, cf, ids, inner, outer, mid, *rest):
-    relayed, rest = (rest[0], rest[1:]) if RELAY_SECOND else (None, rest)
-    t0, t1, t2, t3, near, far, ev, o0, o1, o2, o3, acc, zz = rest
+    accumulate(trip, coef, (acc,), term)
+
+
+def second_outer(trip, coef, ids, inner, outer, mid, *rest):
+    relayed, *rest = rest
+    t0, t1, t2, t3, near, far, ev, o0, o1, o2, o3, acc, more, zz = rest
     for pos in range(SLOTS):
         if pos < NEAR:
-            o = near_odd(ids, near[pos], None if relayed is None else relayed[pos])
+            o = near_odd(ids, near[pos], relayed[pos])
         else:
             o = far[pos - NEAR]
         for p, z in enumerate(sides(ids, ev[pos], o)):
             zz[pos, p] = mid[pos, p, 8:24, :] - z
     acc[...] = inner[...]
-    accumulate(trip, cf, acc, lambda m, j, p: outer[m, p, slice(1, 1 + HELD)] * zz[j, p])
+    more[...] = jnp.zeros(more.shape, F32)
+    held = slice(1, 1 + HELD)
+    accumulate(trip, coef, (acc, more), lambda m, j, p: outer[m, p, held] * zz[j, p])
     for d, (src, out) in enumerate(((t0, o0), (t1, o1), (t2, o2), (t3, o3))):
         for k in range(LOCAL):
             for p in range(2):
                 at = k * 36 + 18 * p + 1
-                out[k, p] = src[at : at + HELD, :] - acc[LOCAL * d + k, p]
-
-
-def second_sweep(
-    cf, ids, mean, far, ev, m0, m1, m2, m3, r0, r1, r2, r3, smoothed, residual, rate, pad
-):
-    g = ids[0]
+                pos = LOCAL * d + k
+                out[k, p] = src[at : at + HELD, :] - (acc[pos, p] + more[pos, p])
+
+
+def final_rates(ids, mean, far, ev, rate, pad):
     below, above = sides(ids, ev[EDGE : EDGE + ROWS, :], far[EDGE // 2 : EDGE // 2 + ROWS, :])
     pad[0:8, :] = jnp.zeros((8, LANES), F32)
     pad[8 + ROWS :, :] = jnp.zeros((8, LANES), F32)
@@ -284,8 +306,7 @@
         own = mean[p]
         pad[8 : 8 + ROWS, :] = own
         others = (
-            above if p else mean[1],
-            mean[0] if p else below,
+            above if p else mean[1], mean[0] if p else below,
             pad[9 : 9 + ROWS, :], pad[7 : 7 + ROWS, :],
             lane_next(own), lane_prev(own),
         )
@@ -294,6 +315,10 @@
             face = 0.5 * (own + other)
             total = face if total is None else total + face
         rate[p] = 0.8 / total
+
+
+def second_sweep(ids, rate, inverse, m0, m1, m2, m3, r0, r1, r2, r3, smoothed, residual):
+    g = ids[0]
     for d, (mid, res) in enumerate(((m0, r0), (m1, r1), (m2, r2), (m3, r3))):
         rows = pl.ds(pl.multiple_of(HELD * (g ^ d), HELD), HELD)
         for p in range(2):
@@ -301,24 +326,13 @@
             for k in range(LOCAL):
                 left = res[k, p]
                 residual[k, p, rows, :] = left
-                smoothed[k, p, rows, :] = mid[k, p] + left * here * cf[ENTRIES + k]
+                smoothed[k, p, rows, :] = mid[k, p] + left * here * inverse[k : k + 1, :]
 
 
 def body(start_field, source, mean_field, kl_fields, triples, coef):
     g = lax.axis_index("mode").astype(jnp.int32)
     slab = lax.axis_index("space").astype(jnp.int32)
     ids = jnp.stack([g, slab % 2, ((slab % 4 == 0) | (slab % 4 == 3)).astype(jnp.int32)])
-    modes = triples[:, 1:]
-    at = LOCAL * ((modes // LOCAL) ^ g) + modes % LOCAL
-    trip = jnp.concatenate([triples[:, 0], at[:, 0], at[:, 1]])
-    diag = jnp.sum(
-        jnp.where(
-            (triples[:, 0:1] == 0) & (at[:, 0:1] == jnp.arange(SLOTS)[None]), coef[:, None], 0.0
-        ),
-        axis=0,
-    )
-    cf = jnp.concatenate([coef, 1.0 / diag])
-
     count = lax.axis_size("space")
     def both(pairs):
         return [pair for a, b in pairs for pair in ((a, b), (b, a))]
@@ -342,13 +356,45 @@
     sends = pl.pallas_call(
         pack_start,
         out_shape=[shape(360, LANES)] * 4,
-        in_specs=[SMEM, HBM],
+        in_specs=[SMEM, VMEM],
         out_specs=[VMEM] * 4,
-        scratch_shapes=[pltpu.VMEM((LOCAL, 2, ROWS + 16, LANES), F32), pltpu.SemaphoreType.DMA],
         name="pack_start",
         **PARAMS,
     )(ids, start_field)
     starts = trade(sends)
+    near = pl.pallas_call(
+        pack_near,
+        out_shape=shape(EDGE // 2, LANES),
+        in_specs=[SMEM] + [VMEM] * 2,
+        out_specs=VMEM,
+        name="pack_near",
+        **PARAMS,
+    )(ids, *starts[:2])
+    mean_late, kl_late, source, near = lax.optimization_barrier(
+        (mean_field, kl_fields, source, near)
+    )
+    near = meet(near, hops)
+    *parts, starts[3] = lax.optimization_barrier((
+        *pl.pallas_call(
+            pack_source,
+            out_shape=[shape(324, LANES)] * 4,
+            in_specs=[SMEM, HBM],
+            out_specs=[VMEM] * 4,
+            scratch_shapes=[
+                pltpu.VMEM((LOCAL, 2, ROWS + 16, LANES), F32), pltpu.SemaphoreType.DMA
+            ],
+            name="pack_source",
+            **PARAMS,
+        )(ids, source),
+        starts[3],
+    ))
+    sources = trade(parts)
+    triples, starts[2], sources[1], near = lax.optimization_barrier(
+        (triples, starts[2], sources[1], near)
+    )
+    modes = triples[:, 1:]
+    at = LOCAL * ((modes // LOCAL) ^ g) + modes % LOCAL
+    trip = jnp.concatenate([triples[:, 0], at[:, 0], at[:, 1]])
     fields = pl.pallas_call(
         pack_fields,
         out_shape=[shape(EDGE_FIELDS, LANES)] * 2,
@@ -360,16 +406,7 @@
         ],
         name="pack_fields",
         **PARAMS,
-    )(ids, mean_field, kl_fields)
-    near = pl.pallas_call(
-        pack_near,
-        out_shape=shape(EDGE // 2, LANES),
-        in_specs=[SMEM] + [VMEM] * 2,
-        out_specs=VMEM,
-        name="pack_near",
-        **PARAMS,
-    )(ids, *starts[:2])
-    near = meet(near, hops if RELAY_FIRST else odds)
+    )(ids, mean_late, kl_late)
     even, odd = pl.pallas_call(
         pack_far,
         out_shape=[shape(EDGE + EDGE_FIELDS, LANES), shape(EDGE // 2 + EDGE_FIELDS, LANES)],
@@ -379,38 +416,28 @@
         **PARAMS,
     )(ids, *starts, *fields)
     edges = (near, meet(odd, odds), meet(even, evens))
-    source, odd = lax.optimization_barrier((source, odd))
-    sources = trade(pl.pallas_call(
-        pack_source,
-        out_shape=[shape(324, LANES)] * 4,
-        in_specs=[SMEM, HBM],
-        out_specs=[VMEM] * 4,
-        scratch_shapes=[pltpu.VMEM((LOCAL, 2, ROWS + 16, LANES), F32), pltpu.SemaphoreType.DMA],
-        name="pack_source",
-        **PARAMS,
-    )(ids, source))
-    relayed = ()
-    if RELAY_FIRST:
-        near, sources[0] = lax.optimization_barrier((near, sources[0]))
-        relayed = (meet(near, relay),)
-    acc, faces = pl.pallas_call(
+    relayed = meet(near, relay)
+    acc, faces, inverse = pl.pallas_call(
         first_inner,
-        out_shape=[shape(SLOTS, 2, 24, LANES), shape(FIELDS, 7, 2, 24, LANES)],
+        out_shape=[
+            shape(SLOTS, 2, 24, LANES), shape(FIELDS, 7, 2, 24, LANES), shape(SLOTS, LANES)
+        ],
         in_specs=[SMEM] * 3 + [VMEM] * 4 + [HBM] * 2,
-        out_specs=[VMEM] * 2,
+        out_specs=[VMEM] * 3,
         scratch_shapes=[
             pltpu.VMEM((FIELDS, 2, ROWS + 16, LANES), F32),
             pltpu.VMEM((FIELDS, 2, 40, LANES), F32),
             pltpu.VMEM((SLOTS, 2, 40, LANES), F32),
             pltpu.VMEM((SLOTS, 2, 24, LANES), F32),
             pltpu.VMEM((SLOTS, 2, 24, LANES), F32),
+            pltpu.SMEM((SLOTS + 1,), F32),
             pltpu.SemaphoreType.DMA((2,)),
         ],
         cost_estimate=COST,
         name="first_inner",
         **PARAMS,
-    )(trip, cf, ids, *starts, mean_field, kl_fields)
-    operands = (trip, cf, ids, acc, faces, *relayed, *starts, *sources, *edges)
+    )(trip, coef, ids, *starts, mean_field, kl_fields)
+    operands = (trip, coef, ids, acc, faces, inverse, relayed, *starts, *sources, *edges)
     mid, *mids, even, odd_a, odd_b, outer = pl.pallas_call(
         first_outer,
         out_shape=[shape(SLOTS, 2, 32, LANES)]
@@ -420,48 +447,53 @@
         + [shape(FIELDS, 2, 24, LANES)],
         in_specs=[SMEM] * 3 + [VMEM] * (len(operands) - 3),
         out_specs=[VMEM] * 9,
-        scratch_shapes=[pltpu.VMEM((SLOTS, 2, 24, LANES), F32)] * 2
+        scratch_shapes=[pltpu.VMEM((SLOTS, 2, 24, LANES), F32)] * 3
         + [pltpu.VMEM((ROWS + 16, LANES), F32)],
         name="first_outer",
         **PARAMS,
     )(*operands)
-    near = meet(odd_a, hops if RELAY_SECOND else odds)
+    near = meet(odd_a, hops)
     met = (near, meet(odd_b, odds), meet(even, evens))
-    relayed = (meet(near, relay),) if RELAY_SECOND else ()
+    relayed = meet(near, relay)
     mids = trade(mids)
     acc = pl.pallas_call(
         second_inner,
         out_shape=shape(SLOTS, 2, HELD, LANES),
-        in_specs=[SMEM] * 2 + [VMEM] * 2,
+        in_specs=[SMEM] * 3 + [VMEM] * 2,
         out_specs=VMEM,
         scratch_shapes=[pltpu.VMEM((SLOTS, 2, HELD, LANES), F32)] * 2,
         cost_estimate=COST,
         name="second_inner",
         **PARAMS,
-    )(trip, cf, mid, faces)
-    operands = (trip, cf, ids, acc, outer, mid, *relayed, *sources, *met)
+    )(trip, coef, ids, mid, faces)
+    operands = (trip, coef, ids, acc, outer, mid, relayed, *sources, *met)
     lefts = pl.pallas_call(
         second_outer,
         out_shape=[shape(LOCAL, 2, HELD, LANES)] * 4,
         in_specs=[SMEM] * 3 + [VMEM] * (len(operands) - 3),
         out_specs=[VMEM] * 4,
-        scratch_shapes=[pltpu.VMEM((SLOTS, 2, HELD, LANES), F32)] * 2,
+        scratch_shapes=[pltpu.VMEM((SLOTS, 2, HELD, LANES), F32)] * 3,
         name="second_outer",
         **PARAMS,
     )(*operands)
     lefts = trade(lefts)
+    rate = pl.pallas_call(
+        final_rates,
+        out_shape=shape(2, ROWS, LANES),
+        in_specs=[SMEM] + [VMEM] * 3,
+        out_specs=VMEM,
+        scratch_shapes=[pltpu.VMEM((ROWS + 16, LANES), F32)],
+        name="final_rates",
+        **PARAMS,
+    )(ids, mean_field, *edges[1:])
     smoothed, residual = pl.pallas_call(
         second_sweep,
         out_shape=[shape(LOCAL, 2, ROWS, LANES)] * 2,
-        in_specs=[SMEM] * 2 + [VMEM] * 11,
+        in_specs=[SMEM] + [VMEM] * 10,
         out_specs=[VMEM] * 2,
-        scratch_shapes=[
-            pltpu.VMEM((2, ROWS, LANES), F32),
-            pltpu.VMEM((ROWS + 16, LANES), F32),
-        ],
         name="second_sweep",
         **PARAMS,
-    )(cf, ids, mean_field, *edges[1:], *mids, *lefts)
+    )(ids, rate, inverse, *mids, *lefts)
     return (smoothed, residual)
 
 

time: 77.7 us -> 75.1 us (0.967)
  other arithmetic: 2.44 us -> 0.17 us
  waiting for transfers between devices: 18 us -> 20.2 us
  local copies, waits for them, and re-layouts: 2.87 us -> 1.1 us
    ppermute x8, waiting for transfers between devices: 1.66 us -> 9.73 us  [meet(): return lax.ppermute(x, 'space', pairs)]
    ppermute x12, waiting for transfers between devices: 16.3 us -> 10.4 us  [trade(): lax.ppermute(parts[d], 'mode', [(i, i ^ d) for i in range(GROUPS)])]
    unnamed x14 -> x12, local copies, waits for them, and re-layouts: 2.86 us -> 1.09 us
    ppermute x8, starting transfers between devices: 22.4 us -> 21.2 us  [meet(): return lax.ppermute(x, 'space', pairs)]
    ppermute x12, starting transfers between devices: 13.6 us -> 14.5 us  [trade(): lax.ppermute(parts[d], 'mode', [(i, i ^ d) for i in range(GROUPS)])]
    reduce_sum x1 -> x0, other arithmetic: 0.8 us -> none  [body(): jnp.sum(jnp.where((triples[:, 0:1] == 0) & (at[:, 0:1] == jnp.arange(SLOT...]
  transfers between devices with their start and end apart: 20 -> 20, of which waited for: 8 -> 7; matrix products, arithmetic and copies ran while one was open for 3% -> 0% of each run, Pallas kernels for 16% -> 17%
where the time goes in v3:
time: 75.1 us; the launch traced here: 74.9 us
  starting transfers between devices  35.7 us (48%)
  waiting for transfers between devices  20.2 us (27%)
  Pallas kernels  16.9 us (23%)
  local copies, waits for them, and re-layouts  1.1 us (1%)
  between operations  0.91 us (1%)
    ppermute x8, starting transfers between devices, meet(): return lax.ppermute(x, 'space', pairs)  21.2 us
    ppermute x12, starting transfers between devices, trade(): lax.ppermute(parts[d], 'mode', [(i, i ^ d) for i in range(GROUPS)])  14.5 us
    ppermute x12, waiting for transfers between devices, trade(): lax.ppermute(parts[d], 'mode', [(i, i ^ d) for i in range(GROUPS)])  10.4 us
    ppermute x8, waiting for transfers between devices, meet(): return lax.ppermute(x, 'space', pairs)  9.73 us
    pallas_call x1, Pallas kernels, body(): pl.pallas_call(first_inner, out_shape=[shape(SLOTS, 2, 24, LANES), shape(...  4.34 us
    pallas_call x1, Pallas kernels, body(): pl.pallas_call(second_inner, out_shape=shape(SLOTS, 2, HELD, LANES), in_s...  3.36 us
    pallas_call x1, Pallas kernels, body(): pl.pallas_call(first_outer, out_shape=[shape(SLOTS, 2, 32, LANES)] + [sha...  1.97 us
    pallas_call x1, Pallas kernels, body(): pl.pallas_call(second_sweep, out_shape=[shape(LOCAL, 2, ROWS, LANES)] * 2...  1.67 us
  transfers between devices with their start and end apart: 20, of which 7 were waited for; matrix products, arithmetic and copies ran while one was open for 0% of the time, Pallas kernels for 17%

profile of v3, /device:TPU:9, one launch (start us, length us, event | category | flops | bytes accessed | tf_op | source)
XLA Modules:
  0.0 74.9 jit_solution(9275909917983173823)
XLA Ops:
  0.7 1.1 %copy-done.1 = f32[9,2,64,128]{3,2,1,0:T(8,128)S(1)} copy-done((f32[9,2,64,128]{3,2,1,0:T(8,128)S(1)}, f32[9,2,64,128]{3,2,1,0:T(8,128)}, u32[]{:S(2)}) %copy-start.1) | copy-done | bytes 589848
  3.3 1.6 %collective-permute-start.2 = (f32[360,128]{1,0:T(8,128)S(1)}, f32[360,128]{1,0:T(8,128)S(1)}, u32[]{:S(2)}, u32[]{:S(2)}) collective-permute-start(f32[360,128]{1,0:T(8,128)S(1)} %get-tuple-element.51), channel_id=1, source_target_pairs={{0,3},{1,2},{2,1},{3,0},{4,7},{5,6},{6,5},{7,4},{8,11},{9,10},{10,... | collective-permute-start | bytes 552968 | tf_op jit(solution)/shard_map/ppermute | solution.py:352
  6.2 3.9 %collective-permute-done.2.s3.rest_4_ = f32[360,128]{1,0:T(8,128)S(1)} collective-permute-done((f32[360,128]{1,0:T(8,128)S(1)}, f32[360,128]{1,0:T(8,128)S(1)}, u32[]{:S(2)}, u32[]{:S(2)}) %collective-permute-start.2) | collective-permute-done | bytes 184352 | tf_op jit(solution)/shard_map/ppermute | solution.py:352
  10.3 2.5 %collective-permute-start.4 = (f32[324,128]{1,0:T(8,128)S(1)}, f32[324,128]{1,0:T(8,128)S(1)}, u32[]{:S(2)}, u32[]{:S(2)}) collective-permute-start(f32[324,128]{1,0:T(8,128)S(1)} %pack_near.1), channel_id=1, source_target_pairs={{4,8},{8,4},{20,24},{24,20},{36,40},{40,36},{52,56},{56,52},{68,72... | collective-permute-start | bytes 497672 | tf_op jit(solution)/shard_map/ppermute | solution.py:348
  12.8 1.5 %collective-permute-start.8 = (f32[324,128]{1,0:T(8,128)S(1)}, f32[324,128]{1,0:T(8,128)S(1)}, u32[]{:S(2)}, u32[]{:S(2)}) collective-permute-start(f32[324,128]{1,0:T(8,128)S(1)} %get-tuple-element.69), channel_id=1, source_target_pairs={{0,2},{1,3},{2,0},{3,1},{4,6},{5,7},{6,4},{7,5},{8,10},{9,11},{10,... | collective-permute-start | bytes 497672 | tf_op jit(solution)/shard_map/ppermute | solution.py:352
  15.8 1.2 %collective-permute-done.4.rest_9_ = f32[324,128]{1,0:T(8,128)S(1)} collective-permute-done((f32[324,128]{1,0:T(8,128)S(1)}, f32[324,128]{1,0:T(8,128)S(1)}, u32[]{:S(2)}, u32[]{:S(2)}) %collective-permute-start.4) | collective-permute-done | bytes 165920 | tf_op jit(solution)/shard_map/ppermute | solution.py:348
  17.8 9.7 %collective-permute-start.5 = (f32[460,128]{1,0:T(8,128)S(1)}, f32[460,128]{1,0:T(8,128)S(1)}, u32[]{:S(2)}, u32[]{:S(2)}) collective-permute-start(f32[460,128]{1,0:T(8,128)S(1)} %get-tuple-element.60), channel_id=1, source_target_pairs={{4,8},{8,4},{12,16},{16,12},{20,24},{24,20},{28,32},{32,28},{36,40... | collective-permute-start | bytes 706568 | tf_op jit(solution)/shard_map/ppermute | solution.py:348
  27.5 1.9 %collective-permute-start.7 = (f32[324,128]{1,0:T(8,128)S(1)}, f32[324,128]{1,0:T(8,128)S(1)}, u32[]{:S(2)}, u32[]{:S(2)}) collective-permute-start(f32[324,128]{1,0:T(8,128)S(1)} %collective-permute-done.4.rest_9_), channel_id=1, source_target_pairs={{0,16},{16,32},{32,48},{48,64},{64,80},{80,96},{96,112},{112,128},... | collective-permute-start | bytes 497672 | tf_op jit(solution)/shard_map/ppermute | solution.py:348
  29.5 4.3 %first_inner.1 = (f32[36,2,24,128]{3,2,1,0:T(8,128)S(1)}, f32[5,7,2,24,128]{4,3,2,1,0:T(8,128)S(1)}, f32[36,128]{1,0:T(8,128)S(1)}) custom-call(s32[468]{0:T(512)S(1)} %pad_add_fusion.trip, f32[156]{0:T(256)S(1)} %copy-done.4, s32[3]{0:T(128)S(1)} %pad_add_fusion.1.ids, f32[360,128]{1,0:T(8,128)S(1)} %get-tuple-element.43.s0.rest_1_, ...), custom_call_target="tpu_custom_call" | custom-call | flops 20000000 | bytes 12000000 | tf_op jit(solution)/shard_map/first_inner/pallas_call | solution.py:420
  33.9 6.8 %collective-permute-done.7.rest_0_ = f32[324,128]{1,0:T(8,128)S(1)} collective-permute-done((f32[324,128]{1,0:T(8,128)S(1)}, f32[324,128]{1,0:T(8,128)S(1)}, u32[]{:S(2)}, u32[]{:S(2)}) %collective-permute-start.7) | collective-permute-done | bytes 165920 | tf_op jit(solution)/shard_map/ppermute | solution.py:348
  40.7 2.0 %first_outer.1 = (f32[36,2,32,128]{3,2,1,0:T(8,128)S(1)}, f32[9,2,16,128]{3,2,1,0:T(8,128)S(1)}, f32[9,2,16,128]{3,2,1,0:T(8,128)S(1)}, f32[9,2,16,128]{3,2,1,0:...) custom-call(s32[468]{0:T(512)S(1)} %pad_add_fusion.trip, ...), custom_call_target="tpu_custom_call" | custom-call | tf_op jit(solution)/shard_map/first_outer/pallas_call | solution.py:441
  42.8 3.4 %collective-permute-start.15 = (f32[18,16,128]{2,1,0:T(8,128)S(1)}, f32[18,16,128]{2,1,0:T(8,128)S(1)}, u32[]{:S(2)}, u32[]{:S(2)}) collective-permute-start(f32[18,16,128]{2,1,0:T(8,128)S(1)} %get-tuple-element.78), channel_id=1, source_target_pairs={{4,8},{8,4},{12,16},{16,12},{20,24},{24,20},{28,32},{32,28},{36,40... | collective-permute-start | bytes 442376 | tf_op jit(solution)/shard_map/ppermute | solution.py:348
  46.3 1.6 %collective-permute-done.13.rest_5_ = f32[18,16,128]{2,1,0:T(8,128)S(1)} collective-permute-done((f32[18,16,128]{2,1,0:T(8,128)S(1)}, f32[18,16,128]{2,1,0:T(8,128)S(1)}, u32[]{:S(2)}, u32[]{:S(2)}) %collective-permute-start.13) | collective-permute-done | bytes 147488 | tf_op jit(solution)/shard_map/ppermute | solution.py:348
  47.9 3.4 %collective-permute-start.14 = (f32[18,16,128]{2,1,0:T(8,128)S(1)}, f32[18,16,128]{2,1,0:T(8,128)S(1)}, u32[]{:S(2)}, u32[]{:S(2)}) collective-permute-start(f32[18,16,128]{2,1,0:T(8,128)S(1)} %collective-permute-done.13.rest_5_), channel_id=1, source_target_pairs={{0,16},{16,32},{32,48},{48,64},{64,80},{80,96},{96,112},{112,128},... | collective-permute-start | bytes 442376 | tf_op jit(solution)/shard_map/ppermute | solution.py:348
  51.3 2.5 %collective-permute-start.10 = (f32[9,2,16,128]{3,2,1,0:T(8,128)S(1)}, f32[9,2,16,128]{3,2,1,0:T(8,128)S(1)}, u32[]{:S(2)}, u32[]{:S(2)}) collective-permute-start(f32[9,2,16,128]{3,2,1,0:T(8,128)S(1)} %get-tuple-element.72), channel_id=1, source_target_pairs={{0,1},{1,0},{2,3},{3,2},{4,5},{5,4},{6,7},{7,6},{8,9},{9,8},{10,11... | collective-permute-start | bytes 442376 | tf_op jit(solution)/shard_map/ppermute | solution.py:352
  53.8 0.9 %collective-permute-start.11 = (f32[9,2,16,128]{3,2,1,0:T(8,128)S(1)}, f32[9,2,16,128]{3,2,1,0:T(8,128)S(1)}, u32[]{:S(2)}, u32[]{:S(2)}) collective-permute-start(f32[9,2,16,128]{3,2,1,0:T(8,128)S(1)} %get-tuple-element.73), channel_id=1, source_target_pairs={{0,2},{1,3},{2,0},{3,1},{4,6},{5,7},{6,4},{7,5},{8,10},{9,11},{10,... | collective-permute-start | bytes 442376 | tf_op jit(solution)/shard_map/ppermute | solution.py:352
  54.7 3.4 %second_inner.1.inner = f32[36,2,16,128]{3,2,1,0:T(8,128)S(1)} custom-call(s32[468]{0:T(512)S(1)} %pad_add_fusion.trip, f32[156]{0:T(256)S(1)} %copy-done.4, s32[3]{0:T(128)S(1)} %pad_add_fusion.1.ids, f32[36,2,32,128]{3,2,1,0:T(8,128)S(1)} %get-tuple-element.75.mid, f32[5,7,2,24,128]{4,3,2,1,0:T(8,128)S(1)} %get-tuple-element.65.faces), custom_call_target="tpu_custom_call" | custom-call | flops 20000000 | bytes 12000000 | tf_op jit(solution)/shard_map/second_inner/pallas_call | solution.py:459
  58.1 1.7 %collective-permute-start.12 = (f32[9,2,16,128]{3,2,1,0:T(8,128)S(1)}, f32[9,2,16,128]{3,2,1,0:T(8,128)S(1)}, u32[]{:S(2)}, u32[]{:S(2)}) collective-permute-start(f32[9,2,16,128]{3,2,1,0:T(8,128)S(1)} %get-tuple-element.74), channel_id=1, source_target_pairs={{0,3},{1,2},{2,1},{3,0},{4,7},{5,6},{6,5},{7,4},{8,11},{9,10},{10,... | collective-permute-start | bytes 442376 | tf_op jit(solution)/shard_map/ppermute | solution.py:352
  59.8 1.7 %second_outer.1 = (f32[9,2,16,128]{3,2,1,0:T(8,128)S(1)}, f32[9,2,16,128]{3,2,1,0:T(8,128)S(1)}, f32[9,2,16,128]{3,2,1,0:T(8,128)S(1)}, f32[9,2,16,128]{3,2,1,0:T(8,128)S(1)}) custom-call(s32[468]{0:T(512)S(1)} %pad_add_fusion.trip, f32[156]{0:T(256)S(1)} %copy-done.4, s32[3]{0:T(128)S(1)} %pad_add_fusion.1.ids, f32[36,2,16,128]{3,2,1,0:T(8,128)S(1)} %second_inner.1.inner, ...), custom_call_target="tpu_custom_call" | custom-call | tf_op jit(solution)/shard_map/second_outer/pallas_call | solution.py:470
  61.5 2.6 %collective-permute-start.17 = (f32[9,2,16,128]{3,2,1,0:T(8,128)S(1)}, f32[9,2,16,128]{3,2,1,0:T(8,128)S(1)}, u32[]{:S(2)}, u32[]{:S(2)}) collective-permute-start(f32[9,2,16,128]{3,2,1,0:T(8,128)S(1)} %get-tuple-element.81), channel_id=1, source_target_pairs={{0,1},{1,0},{2,3},{3,2},{4,5},{5,4},{6,7},{7,6},{8,9},{9,8},{10,11... | collective-permute-start | bytes 442376 | tf_op jit(solution)/shard_map/ppermute | solution.py:352
  64.1 1.8 %collective-permute-start.18 = (f32[9,2,16,128]{3,2,1,0:T(8,128)S(1)}, f32[9,2,16,128]{3,2,1,0:T(8,128)S(1)}, u32[]{:S(2)}, u32[]{:S(2)}) collective-permute-start(f32[9,2,16,128]{3,2,1,0:T(8,128)S(1)} %get-tuple-element.82), channel_id=1, source_target_pairs={{0,2},{1,3},{2,0},{3,1},{4,6},{5,7},{6,4},{7,5},{8,10},{9,11},{10,... | collective-permute-start | bytes 442376 | tf_op jit(solution)/shard_map/ppermute | solution.py:352
  66.7 3.3 %collective-permute-done.18.r2 = f32[9,2,16,128]{3,2,1,0:T(8,128)S(1)} collective-permute-done((f32[9,2,16,128]{3,2,1,0:T(8,128)S(1)}, f32[9,2,16,128]{3,2,1,0:T(8,128)S(1)}, u32[]{:S(2)}, u32[]{:S(2)}) %collective-permute-start.18) | collective-permute-done | bytes 147488 | tf_op jit(solution)/shard_map/ppermute | solution.py:352
  70.0 3.2 %collective-permute-done.19.r3 = f32[9,2,16,128]{3,2,1,0:T(8,128)S(1)} collective-permute-done((f32[9,2,16,128]{3,2,1,0:T(8,128)S(1)}, f32[9,2,16,128]{3,2,1,0:T(8,128)S(1)}, u32[]{:S(2)}, u32[]{:S(2)}) %collective-permute-start.19) | collective-permute-done | bytes 147488 | tf_op jit(solution)/shard_map/ppermute | solution.py:352
  73.2 1.7 %second_sweep.1 = (f32[9,2,64,128]{3,2,1,0:T(8,128)}, f32[9,2,64,128]{3,2,1,0:T(8,128)}) custom-call(s32[3]{0:T(128)S(1)} %pad_add_fusion.1.ids, f32[2,64,128]{2,1,0:T(8,128)S(1)} %final_rates.1.rate, f32[36,128]{1,0:T(8,128)S(1)} %get-tuple-element.63.inverse, f32[9,2,16,128]{3,2,1,0:T(8,128)S(1)} %get-tuple-element.71.m0, ...), custom_call_target="tpu_custom_call" | custom-call | tf_op jit(solution)/shard_map/second_sweep/pallas_call | solution.py:489
  (45 shorter events, 6.3 us)
Async XLA Ops:
  0.6 14.4 %copy-start = (f32[4,2,64,128]{3,2,1,0:T(8,128)S(1)}, f32[4,2,64,128]{3,2,1,0:T(8,128)}, u32[]{:S(2)}) copy-start(f32[4,2,64,128]{3,2,1,0:T(8,128)} %kl.2) | copy-start | bytes 786436
  2.5 15.2 %copy-start.5 = (s32[156,3]{0,1:T(4,128)S(1)}, s32[156,3]{0,1:T(4,128)}, u32[]{:S(2)}) copy-start(s32[156,3]{0,1:T(4,128)} %param.10) | copy-start | bytes 5620
  2.5 2.4 %collective-permute-start = (f32[360,128]{1,0:T(8,128)S(1)}, f32[360,128]{1,0:T(8,128)S(1)}, u32[]{:S(2)}, u32[]{:S(2)}) collective-permute-start(f32[360,128]{1,0:T(8,128)S(1)} %get-tuple-element.44), channel_id=1, source_target_pairs={{0,1},{1,0},{2,3},{3,2},{4,5},{5,4},{6,7},{7,6},{8,9},{9,8},{10,11... | collective-permute-start | bytes 552968 | tf_op jit(solution)/shard_map/ppermute | solution.py:352
  3.3 6.9 %collective-permute-start.2 = (f32[360,128]{1,0:T(8,128)S(1)}, f32[360,128]{1,0:T(8,128)S(1)}, u32[]{:S(2)}, u32[]{:S(2)}) collective-permute-start(f32[360,128]{1,0:T(8,128)S(1)} %get-tuple-element.51), channel_id=1, source_target_pairs={{0,3},{1,2},{2,1},{3,0},{4,7},{5,6},{6,5},{7,4},{8,11},{9,10},{10,... | collective-permute-start | bytes 552968 | tf_op jit(solution)/shard_map/ppermute | solution.py:352
  4.9 10.9 %collective-permute-start.1 = (f32[360,128]{1,0:T(8,128)S(1)}, f32[360,128]{1,0:T(8,128)S(1)}, u32[]{:S(2)}, u32[]{:S(2)}) collective-permute-start(f32[360,128]{1,0:T(8,128)S(1)} %get-tuple-element.45), channel_id=1, source_target_pairs={{0,2},{1,3},{2,0},{3,1},{4,6},{5,7},{6,4},{7,5},{8,10},{9,11},{10,... | collective-permute-start | bytes 552968 | tf_op jit(solution)/shard_map/ppermute | solution.py:352
  5.0 24.5 %slice-start = ((s32[156,3]{0,1:T(4,128)}), s32[156,1]{0,1:T(1,128)S(1)}, s32[]{:S(2)}) async-start(s32[156,3]{0,1:T(4,128)} %param.10), calls=%async_computation | async-start | bytes 2048 | tf_op jit(solution)/shard_map/slice | solution.py:397
  5.0 24.6 %copy-start.4 = (f32[156]{0:T(256)S(1)}, f32[156]{0:T(256)}, u32[]{:S(2)}) copy-start(f32[156]{0:T(256)} %coef.7) | copy-start | bytes 1876
  10.2 5.6 %collective-permute-start.3 = (f32[324,128]{1,0:T(8,128)S(1)}, f32[324,128]{1,0:T(8,128)S(1)}, u32[]{:S(2)}, u32[]{:S(2)}) collective-permute-start(f32[324,128]{1,0:T(8,128)S(1)} %get-tuple-element.52), channel_id=1, source_target_pairs={{0,1},{1,0},{2,3},{3,2},{4,5},{5,4},{6,7},{7,6},{8,9},{9,8},{10,11... | collective-permute-start | bytes 497672 | tf_op jit(solution)/shard_map/ppermute | solution.py:352
  10.3 6.7 %collective-permute-start.4 = (f32[324,128]{1,0:T(8,128)S(1)}, f32[324,128]{1,0:T(8,128)S(1)}, u32[]{:S(2)}, u32[]{:S(2)}) collective-permute-start(f32[324,128]{1,0:T(8,128)S(1)} %pack_near.1), channel_id=1, source_target_pairs={{4,8},{8,4},{20,24},{24,20},{36,40},{40,36},{52,56},{56,52},{68,72... | collective-permute-start | bytes 497672 | tf_op jit(solution)/shard_map/ppermute | solution.py:348
  12.8 21.1 %collective-permute-start.8 = (f32[324,128]{1,0:T(8,128)S(1)}, f32[324,128]{1,0:T(8,128)S(1)}, u32[]{:S(2)}, u32[]{:S(2)}) collective-permute-start(f32[324,128]{1,0:T(8,128)S(1)} %get-tuple-element.69), channel_id=1, source_target_pairs={{0,2},{1,3},{2,0},{3,1},{4,6},{5,7},{6,4},{7,5},{8,10},{9,11},{10,... | collective-permute-start | bytes 497672 | tf_op jit(solution)/shard_map/ppermute | solution.py:352
  14.3 19.6 %collective-permute-start.9 = (f32[324,128]{1,0:T(8,128)S(1)}, f32[324,128]{1,0:T(8,128)S(1)}, u32[]{:S(2)}, u32[]{:S(2)}) collective-permute-start(f32[324,128]{1,0:T(8,128)S(1)} %get-tuple-element.70), channel_id=1, source_target_pairs={{0,3},{1,2},{2,1},{3,0},{4,7},{5,6},{6,5},{7,4},{8,11},{9,10},{10,... | collective-permute-start | bytes 497672 | tf_op jit(solution)/shard_map/ppermute | solution.py:352
  17.6 23.0 %collective-permute-start.6 = (f32[784,128]{1,0:T(8,128)S(1)}, f32[784,128]{1,0:T(8,128)S(1)}, u32[]{:S(2)}, u32[]{:S(2)}) collective-permute-start(f32[784,128]{1,0:T(8,128)S(1)} %get-tuple-element.61), channel_id=1, source_target_pairs={{0,4},{4,0},{8,12},{12,8},{16,20},{20,16},{24,28},{28,24},{32,36},... | collective-permute-start | bytes 1204232 | tf_op jit(solution)/shard_map/ppermute | solution.py:348
  17.8 22.9 %collective-permute-start.5 = (f32[460,128]{1,0:T(8,128)S(1)}, f32[460,128]{1,0:T(8,128)S(1)}, u32[]{:S(2)}, u32[]{:S(2)}) collective-permute-start(f32[460,128]{1,0:T(8,128)S(1)} %get-tuple-element.60), channel_id=1, source_target_pairs={{4,8},{8,4},{12,16},{16,12},{20,24},{24,20},{28,32},{32,28},{36,40... | collective-permute-start | bytes 706568 | tf_op jit(solution)/shard_map/ppermute | solution.py:348
  27.5 13.2 %collective-permute-start.7 = (f32[324,128]{1,0:T(8,128)S(1)}, f32[324,128]{1,0:T(8,128)S(1)}, u32[]{:S(2)}, u32[]{:S(2)}) collective-permute-start(f32[324,128]{1,0:T(8,128)S(1)} %collective-permute-done.4.rest_9_), channel_id=1, source_target_pairs={{0,16},{16,32},{32,48},{48,64},{64,80},{80,96},{96,112},{112,128},... | collective-permute-start | bytes 497672 | tf_op jit(solution)/shard_map/ppermute | solution.py:348
  42.6 5.3 %collective-permute-start.13 = (f32[18,16,128]{2,1,0:T(8,128)S(1)}, f32[18,16,128]{2,1,0:T(8,128)S(1)}, u32[]{:S(2)}, u32[]{:S(2)}) collective-permute-start(f32[18,16,128]{2,1,0:T(8,128)S(1)} %get-tuple-element.77), channel_id=1, source_target_pairs={{4,8},{8,4},{20,24},{24,20},{36,40},{40,36},{52,56},{56,52},{68,72... | collective-permute-start | bytes 442376 | tf_op jit(solution)/shard_map/ppermute | solution.py:348
  42.7 17.1 %collective-permute-start.16 = (f32[36,16,128]{2,1,0:T(8,128)S(1)}, f32[36,16,128]{2,1,0:T(8,128)S(1)}, u32[]{:S(2)}, u32[]{:S(2)}) collective-permute-start(f32[36,16,128]{2,1,0:T(8,128)S(1)} %get-tuple-element.79), channel_id=1, source_target_pairs={{0,4},{4,0},{8,12},{12,8},{16,20},{20,16},{24,28},{28,24},{32,36},... | collective-permute-start | bytes 884744 | tf_op jit(solution)/shard_map/ppermute | solution.py:348
  42.8 15.2 %collective-permute-start.15 = (f32[18,16,128]{2,1,0:T(8,128)S(1)}, f32[18,16,128]{2,1,0:T(8,128)S(1)}, u32[]{:S(2)}, u32[]{:S(2)}) collective-permute-start(f32[18,16,128]{2,1,0:T(8,128)S(1)} %get-tuple-element.78), channel_id=1, source_target_pairs={{4,8},{8,4},{12,16},{16,12},{20,24},{24,20},{28,32},{32,28},{36,40... | collective-permute-start | bytes 442376 | tf_op jit(solution)/shard_map/ppermute | solution.py:348
  47.9 11.9 %collective-permute-start.14 = (f32[18,16,128]{2,1,0:T(8,128)S(1)}, f32[18,16,128]{2,1,0:T(8,128)S(1)}, u32[]{:S(2)}, u32[]{:S(2)}) collective-permute-start(f32[18,16,128]{2,1,0:T(8,128)S(1)} %collective-permute-done.13.rest_5_), channel_id=1, source_target_pairs={{0,16},{16,32},{32,48},{48,64},{64,80},{80,96},{96,112},{112,128},... | collective-permute-start | bytes 442376 | tf_op jit(solution)/shard_map/ppermute | solution.py:348
  51.3 14.6 %collective-permute-start.10 = (f32[9,2,16,128]{3,2,1,0:T(8,128)S(1)}, f32[9,2,16,128]{3,2,1,0:T(8,128)S(1)}, u32[]{:S(2)}, u32[]{:S(2)}) collective-permute-start(f32[9,2,16,128]{3,2,1,0:T(8,128)S(1)} %get-tuple-element.72), channel_id=1, source_target_pairs={{0,1},{1,0},{2,3},{3,2},{4,5},{5,4},{6,7},{7,6},{8,9},{9,8},{10,11... | collective-permute-start | bytes 442376 | tf_op jit(solution)/shard_map/ppermute | solution.py:352
  53.8 12.8 %collective-permute-start.11 = (f32[9,2,16,128]{3,2,1,0:T(8,128)S(1)}, f32[9,2,16,128]{3,2,1,0:T(8,128)S(1)}, u32[]{:S(2)}, u32[]{:S(2)}) collective-permute-start(f32[9,2,16,128]{3,2,1,0:T(8,128)S(1)} %get-tuple-element.73), channel_id=1, source_target_pairs={{0,2},{1,3},{2,0},{3,1},{4,6},{5,7},{6,4},{7,5},{8,10},{9,11},{10,... | collective-permute-start | bytes 442376 | tf_op jit(solution)/shard_map/ppermute | solution.py:352
  58.1 8.6 %collective-permute-start.12 = (f32[9,2,16,128]{3,2,1,0:T(8,128)S(1)}, f32[9,2,16,128]{3,2,1,0:T(8,128)S(1)}, u32[]{:S(2)}, u32[]{:S(2)}) collective-permute-start(f32[9,2,16,128]{3,2,1,0:T(8,128)S(1)} %get-tuple-element.74), channel_id=1, source_target_pairs={{0,3},{1,2},{2,1},{3,0},{4,7},{5,6},{6,5},{7,4},{8,11},{9,10},{10,... | collective-permute-start | bytes 442376 | tf_op jit(solution)/shard_map/ppermute | solution.py:352
  61.5 5.2 %collective-permute-start.17 = (f32[9,2,16,128]{3,2,1,0:T(8,128)S(1)}, f32[9,2,16,128]{3,2,1,0:T(8,128)S(1)}, u32[]{:S(2)}, u32[]{:S(2)}) collective-permute-start(f32[9,2,16,128]{3,2,1,0:T(8,128)S(1)} %get-tuple-element.81), channel_id=1, source_target_pairs={{0,1},{1,0},{2,3},{3,2},{4,5},{5,4},{6,7},{7,6},{8,9},{9,8},{10,11... | collective-permute-start | bytes 442376 | tf_op jit(solution)/shard_map/ppermute | solution.py:352
  64.1 5.9 %collective-permute-start.18 = (f32[9,2,16,128]{3,2,1,0:T(8,128)S(1)}, f32[9,2,16,128]{3,2,1,0:T(8,128)S(1)}, u32[]{:S(2)}, u32[]{:S(2)}) collective-permute-start(f32[9,2,16,128]{3,2,1,0:T(8,128)S(1)} %get-tuple-element.82), channel_id=1, source_target_pairs={{0,2},{1,3},{2,0},{3,1},{4,6},{5,7},{6,4},{7,5},{8,10},{9,11},{10,... | collective-permute-start | bytes 442376 | tf_op jit(solution)/shard_map/ppermute | solution.py:352
  65.9 7.3 %collective-permute-start.19 = (f32[9,2,16,128]{3,2,1,0:T(8,128)S(1)}, f32[9,2,16,128]{3,2,1,0:T(8,128)S(1)}, u32[]{:S(2)}, u32[]{:S(2)}) collective-permute-start(f32[9,2,16,128]{3,2,1,0:T(8,128)S(1)} %get-tuple-element.83), channel_id=1, source_target_pairs={{0,3},{1,2},{2,1},{3,0},{4,7},{5,6},{6,5},{7,4},{8,11},{9,10},{10,... | collective-permute-start | bytes 442376 | tf_op jit(solution)/shard_map/ppermute | solution.py:352
  (3 other events, 18.0 us)

commit v4 on v3

--- a/solution.py
+++ b/solution.py
@@ -14,13 +14,14 @@
 ENTRIES = 156
 EDGE = 18 * SLOTS
 EDGE_FIELDS = ROWS + 18 * (FIELDS - 1)
-UNROLL = 2
+UNROLL = 3
 NEAR = 2 * LOCAL
 F32 = jnp.float32
 VMEM = pl.BlockSpec(memory_space=pltpu.VMEM)
 SMEM = pl.BlockSpec(memory_space=pltpu.SMEM)
 HBM = pl.BlockSpec(memory_space=pltpu.HBM)
 COST = pl.CostEstimate(flops=20_000_000, bytes_accessed=12_000_000, transcendentals=0)
+SIDE_COST = pl.CostEstimate(flops=5_000_000, bytes_accessed=3_000_000, transcendentals=0)
 PARAMS = dict(compiler_params=pltpu.CompilerParams(vmem_limit_bytes=40 * 2**20))
 
 
@@ -75,22 +76,20 @@
         pl.when(q == GROUPS - 1)(functools.partial(clear, 18))
 
 
-def pack_fields(ids, mean, kl, even, odd, klp, sems):
+def pack_fields(ids, mean, kl, even, odd, own, padded, sems):
     g, parity = ids[0], ids[1]
-    two = fill_padded(kl, klp, sems.at[0])
-    edges = []
-    for out, plane, sem in ((even, 1 - parity, 1), (odd, parity, 2)):
-        edges.append(
-            pltpu.make_async_copy(mean.at[plane], out.at[pl.ds(0, ROWS), :], sems.at[sem])
-        )
-        edges[-1].start()
+    one = fill_padded(mean, padded.at[0], sems.at[0])
+    two = fill_padded(kl, padded.at[pl.ds(1, FIELDS - 1)], sems.at[1])
+    one.wait()
     two.wait()
+    for m in range(FIELDS):
+        for p in range(2):
+            own[m, p, 7:27, :] = window(padded, (m, p), g, -2, 20)
     for out, plane in ((even, 1 - parity), (odd, parity)):
-        for m in range(FIELDS - 1):
-            at = ROWS + 18 * m
-            out[at : at + 18, :] = window(klp, (m, plane), g, -1, 18)
-    for edge in edges:
-        edge.wait()
+        out[0:ROWS, :] = padded[0, plane, 8 : 8 + ROWS, :]
+        for m in range(1, FIELDS):
+            at = ROWS + 18 * (m - 1)
+            out[at : at + 18, :] = own[m, plane, 8:26, :]
 
 
 def pack_source(ids, source, o0, o1, o2, o3, padded, sem):
@@ -139,6 +138,11 @@
     return jnp.where(ids[2] == 1, relayed, straight)
 
 
+def rows_of(src, plane, lower, upper, count):
+    low, high = src[lower : lower + count, :], src[upper : upper + count, :]
+    return jnp.where(plane == 0, low, high)
+
+
 def accumulate(trip, coef, accs, term, visit=None):
     def step(e, carry):
         for lane, acc in enumerate(accs):
@@ -146,19 +150,15 @@
             m, i, j, c = trip[n], trip[ENTRIES + n], trip[2 * ENTRIES + n], coef[n]
             if visit is not None:
                 visit(m, i, c)
-            for p in range(2):
-                acc[i, p] += c * term(m, j, p)
+            term(acc, m, i, j, c)
         return carry
 
     lax.fori_loop(0, ENTRIES // len(accs), step, 0, unroll=UNROLL)
 
 
 def first_inner(
-    trip, coef, ids, s0, s1, s2, s3, mean, kl, acc, faces, inverse, klp, ae, vv, nxt, prv, diag, sems
+    trip, coef, s0, s1, s2, s3, ae, acc, faces, inverse, vv, nxt, prv, diag
 ):
-    g = ids[0]
-    one = fill_padded(mean, klp.at[0], sems.at[0])
-    two = fill_padded(kl, klp.at[pl.ds(1, FIELDS - 1)], sems.at[1])
     for d, src in enumerate((s0, s1, s2, s3)):
         for k in range(LOCAL):
             pos = LOCAL * d + k
@@ -167,11 +167,6 @@
                 mine = vv[pos, p, 8:32, :]
                 nxt[pos, p] = lane_next(mine)
                 prv[pos, p] = lane_prev(mine)
-    one.wait()
-    two.wait()
-    for m in range(FIELDS):
-        for p in range(2):
-            ae[m, p, 7:27, :] = window(klp, (m, p), g, -2, 20)
     for m in range(FIELDS):
         for p in range(2):
             own = ae[m, p, 8:32, :]
@@ -189,10 +184,12 @@
             faces[m, 1, p] = own
     acc[...] = jnp.zeros(acc.shape, F32)
 
-    def term(m, j, p):
-        total = faces[m, 0, p] * vv[j, p, 8:32, :] + faces[m, 2, p] * vv[j, 1 - p, 8:32, :]
-        total += faces[m, 3, p] * vv[j, p, 9:33, :] + faces[m, 4, p] * vv[j, p, 7:31, :]
-        return total + (faces[m, 5, p] * nxt[j, p] + faces[m, 6, p] * prv[j, p])
+    def term(acc, m, i, j, c):
+        for p in range(2):
+            total = faces[m, 0, p] * vv[j, p, 8:32, :] + faces[m, 2, p] * vv[j, 1 - p, 8:32, :]
+            total += faces[m, 3, p] * vv[j, p, 9:33, :] + faces[m, 4, p] * vv[j, p, 7:31, :]
+            total += faces[m, 5, p] * nxt[j, p] + faces[m, 6, p] * prv[j, p]
+            acc[i, p] += c * total
 
     def visit(m, i, c):
         diag[jnp.where(m == 0, i, SLOTS)] = c
@@ -202,100 +199,136 @@
         inverse[pos : pos + 1, :] = 1.0 / jnp.full((1, LANES), diag[pos], F32)
 
 
-def first_outer(
-    trip, coef, ids, inner, faces, inverse, *rest
+def first_side(odd, trip, coef, ids, inner, faces, inverse, *rest):
+    count = 3 if odd else 1
+    planes, rest = rest[:count], rest[count:]
+    starts, sources, rest = rest[:4], rest[4:8], rest[8:]
+    mid, *sends, outer, acc, more, zz, pad = rest
+    g = ids[0]
+    p = ids[1] if odd else 1 - ids[1]
+    if odd:
+        near, far, relayed = planes
+        base, fields = EDGE // 2, far
+    else:
+        base, fields = EDGE, planes[0]
+    for m in range(FIELDS):
+        at = base + ROWS + 18 * (m - 1)
+        if m == 0:
+            pad[0:8, :] = jnp.zeros((8, LANES), F32)
+            pad[8 : 8 + ROWS, :] = fields[base : base + ROWS, :]
+            pad[8 + ROWS :, :] = jnp.zeros((8, LANES), F32)
+            other = window(pad, (), g, -1, 18)
+        else:
+            other = fields[at : at + 18, :]
+        outer[m, 0:18, :] = 0.5 * (faces[m, 1, p, 0:18, :] + other)
+    for pos in range(SLOTS):
+        rows = slice(18 * pos, 18 * pos + 18)
+        if not odd:
+            z = planes[0][rows, :]
+        elif pos < NEAR:
+            z = near_odd(ids, near[rows, :], relayed[rows, :])
+        else:
+            z = far[18 * (pos - NEAR) : 18 * (pos - NEAR) + 18, :]
+        at = pos % LOCAL * 40 + 1
+        zz[pos, 0:18, :] = rows_of(starts[pos // LOCAL], p, at, at + 20, 18) - z
+    acc[...] = inner[:, p]
+    more[...] = jnp.zeros(more.shape, F32)
+
+    def term(acc, m, i, j, c):
+        acc[i] += c * (outer[m] * zz[j])
+
+    accumulate(trip, coef, (acc, more), term)
+    row = HELD * g - 1 + lax.broadcasted_iota(jnp.int32, (18, LANES), 0)
+    inside = (row >= 0) & (row < ROWS)
+    rate = 0.8 / (faces[0, 0, p, 0:18, :] + outer[0, 0:18, :])
+    for pos in range(SLOTS):
+        at = pos % LOCAL * 36
+        first = rows_of(sources[pos // LOCAL], p, at, at + 18, 18)
+        first = first - (acc[pos, 0:18, :] + more[pos, 0:18, :])
+        at = pos % LOCAL * 40 + 1
+        moved = rows_of(starts[pos // LOCAL], p, at, at + 20, 18)
+        moved = moved + first * rate * inverse[pos : pos + 1, :]
+        moved = jnp.where(inside, moved, 0.0)
+        mid[pos, 7:25, :] = moved
+        if odd:
+            sends[pos // NEAR][pos % NEAR] = moved[1 : 1 + HELD]
+        else:
+            sends[0][pos] = moved[1 : 1 + HELD]
+
+
+HERE = slice(1, 1 + HELD)
+
+
+def in_plane(faces, p, m, j, mine, other, nxt, prv):
+    total = faces[m, 0, p, HERE] * mine[j, 8:24, :] + faces[m, 2, p, HERE] * other[j, 8:24, :]
+    total += faces[m, 3, p, HERE] * mine[j, 9:25, :] + faces[m, 4, p, HERE] * mine[j, 7:23, :]
+    return total + (faces[m, 5, p, HERE] * nxt[j] + faces[m, 6, p, HERE] * prv[j])
+
+
+def shift_lanes(mine, nxt, prv):
+    for pos in range(SLOTS):
+        held = mine[pos, 8:24, :]
+        nxt[pos] = lane_next(held)
+        prv[pos] = lane_prev(held)
+
+
+def second_even(
+    trip, coef, ids, faces, outer, mine, other, met, t0, t1, t2, t3, o0, o1, o2, o3,
+    acc, more, zz, nxt, prv,
 ):
-    relayed, *rest = rest
-    s0, s1, s2, s3, t0, t1, t2, t3, near, far, ev = rest[:11]
-    mid, b0, b1, b2, b3, even, odd_a, odd_b, outer, acc, more, zz, pad = rest[11:]
-    g, top = ids[0], ids[1] == 0
-    for m in range(FIELDS):
-        at = ROWS + 18 * (m - 1)
-        rows = slice(at, at + 18) if m else slice(0, ROWS)
-        e = ev[EDGE + rows.start : EDGE + rows.stop, :]
-        o = far[EDGE // 2 + rows.start : EDGE // 2 + rows.stop, :]
-        for p, other in enumerate(sides(ids, e, o)):
-            if m == 0:
-                pad[0:8, :] = jnp.zeros((8, LANES), F32)
-                pad[8 : 8 + ROWS, :] = other
-                pad[8 + ROWS :, :] = jnp.zeros((8, LANES), F32)
-                other = window(pad, (), g, -1, 18)
-            outer[m, p, 0:18, :] = 0.5 * (faces[m, 1, p, 0:18, :] + other)
-    for d, src in enumerate((s0, s1, s2, s3)):
+    p = 1 - ids[1]
+    shift_lanes(mine, nxt, prv)
+    for pos in range(SLOTS):
+        zz[pos] = mine[pos, 8:24, :] - met[pos]
+    acc[...] = jnp.zeros(acc.shape, F32)
+    more[...] = jnp.zeros(more.shape, F32)
+
+    def term(acc, m, i, j, c):
+        total = in_plane(faces, p, m, j, mine, other, nxt, prv)
+        acc[i] += c * (total + outer[m, HERE] * zz[j])
+
+    accumulate(trip, coef, (acc, more), term)
+    for d, (src, out) in enumerate(((t0, o0), (t1, o1), (t2, o2), (t3, o3))):
         for k in range(LOCAL):
             pos = LOCAL * d + k
-            rows = slice(18 * pos, 18 * pos + 18)
-            if pos < NEAR:
-                o = near_odd(ids, near[rows, :], relayed[rows, :])
-            else:
-                o = far[18 * (pos - NEAR) : 18 * (pos - NEAR) + 18, :]
-            for p, z in enumerate(sides(ids, ev[rows, :], o)):
-                at = k * 40 + 20 * p + 1
-                zz[pos, p, 0:18, :] = src[at : at + 18, :] - z
+            out[k, 0] = mine[pos, 8:24, :]
+            out[k, 1] = other[pos, 8:24, :]
+            at = k * 36 + 1
+            out[k, 2] = rows_of(src, p, at, at + 18, HELD) - (acc[pos] + more[pos])
+
+
+def second_inner(trip, coef, ids, faces, mine, other, acc, more, nxt, prv):
+    p = ids[1]
+    shift_lanes(mine, nxt, prv)
+    acc[...] = jnp.zeros(acc.shape, F32)
+    more[...] = jnp.zeros(more.shape, F32)
+
+    def term(acc, m, i, j, c):
+        acc[i] += c * in_plane(faces, p, m, j, mine, other, nxt, prv)
+
+    accumulate(trip, coef, (acc, more), term)
+
+
+def second_odd(
+    trip, coef, ids, inner, extra, outer, mine, near, far, relayed, t0, t1, t2, t3,
+    o0, o1, o2, o3, acc, more, zz,
+):
+    p = ids[1]
+    for pos in range(SLOTS):
+        z = near_odd(ids, near[pos], relayed[pos]) if pos < NEAR else far[pos - NEAR]
+        zz[pos] = mine[pos, 8:24, :] - z
     acc[...] = inner[...]
-    more[...] = jnp.zeros(more.shape, F32)
-    accumulate(trip, coef, (acc, more), lambda m, j, p: outer[m, p] * zz[j, p])
-    row = HELD * g - 1 + lax.broadcasted_iota(jnp.int32, (18, LANES), 0)
-    inside = (row >= 0) & (row < ROWS)
-    rates = [0.8 / (faces[0, 0, p, 0:18, :] + outer[0, p, 0:18, :]) for p in range(2)]
-    for d, (start, src, out) in enumerate(
-        ((s0, t0, b0), (s1, t1, b1), (s2, t2, b2), (s3, t3, b3))
-    ):
+    more[...] = extra[...]
+
+    def term(acc, m, i, j, c):
+        acc[i] += c * (outer[m, HERE] * zz[j])
+
+    accumulate(trip, coef, (acc, more), term)
+    for d, (src, out) in enumerate(((t0, o0), (t1, o1), (t2, o2), (t3, o3))):
         for k in range(LOCAL):
             pos = LOCAL * d + k
-            helds = []
-            for p in range(2):
-                at = k * 36 + 18 * p
-                first = src[at : at + 18, :] - (acc[pos, p, 0:18, :] + more[pos, p, 0:18, :])
-                at = k * 40 + 20 * p + 1
-                moved = start[at : at + 18, :] + first * rates[p] * inverse[pos : pos + 1, :]
-                moved = jnp.where(inside, moved, 0.0)
-                mid[pos, p, 7:25, :] = moved
-                held = moved[1 : 1 + HELD]
-                out[k, p] = held
-                helds.append(held)
-            even[pos] = jnp.where(top, helds[1], helds[0])
-            (odd_a if pos < NEAR else odd_b)[pos % NEAR] = jnp.where(top, helds[0], helds[1])
-
-
-def second_inner(trip, coef, ids, mid, faces, acc, nxt, prv):
-    for pos in range(SLOTS):
-        for p in range(2):
-            mine = mid[pos, p, 8:24, :]
-            nxt[pos, p] = lane_next(mine)
-            prv[pos, p] = lane_prev(mine)
-    acc[...] = jnp.zeros(acc.shape, F32)
-    held = slice(1, 1 + HELD)
-
-    def term(m, j, p):
-        total = faces[m, 0, p, held] * mid[j, p, 8:24, :]
-        total += faces[m, 2, p, held] * mid[j, 1 - p, 8:24, :]
-        total += faces[m, 3, p, held] * mid[j, p, 9:25, :] + faces[m, 4, p, held] * mid[j, p, 7:23, :]
-        return total + (faces[m, 5, p, held] * nxt[j, p] + faces[m, 6, p, held] * prv[j, p])
-
-    accumulate(trip, coef, (acc,), term)
-
-
-def second_outer(trip, coef, ids, inner, outer, mid, *rest):
-    relayed, *rest = rest
-    t0, t1, t2, t3, near, far, ev, o0, o1, o2, o3, acc, more, zz = rest
-    for pos in range(SLOTS):
-        if pos < NEAR:
-            o = near_odd(ids, near[pos], relayed[pos])
-        else:
-            o = far[pos - NEAR]
-        for p, z in enumerate(sides(ids, ev[pos], o)):
-            zz[pos, p] = mid[pos, p, 8:24, :] - z
-    acc[...] = inner[...]
-    more[...] = jnp.zeros(more.shape, F32)
-    held = slice(1, 1 + HELD)
-    accumulate(trip, coef, (acc, more), lambda m, j, p: outer[m, p, held] * zz[j, p])
-    for d, (src, out) in enumerate(((t0, o0), (t1, o1), (t2, o2), (t3, o3))):
-        for k in range(LOCAL):
-            for p in range(2):
-                at = k * 36 + 18 * p + 1
-                pos = LOCAL * d + k
-                out[k, p] = src[at : at + HELD, :] - (acc[pos, p] + more[pos, p])
+            at = k * 36 + 1
+            out[k] = rows_of(src, p, at, at + 18, HELD) - (acc[pos] + more[pos])
 
 
 def final_rates(ids, mean, far, ev, rate, pad):
@@ -318,15 +351,16 @@
 
 
 def second_sweep(ids, rate, inverse, m0, m1, m2, m3, r0, r1, r2, r3, smoothed, residual):
-    g = ids[0]
+    g, parity = ids[0], ids[1]
     for d, (mid, res) in enumerate(((m0, r0), (m1, r1), (m2, r2), (m3, r3))):
         rows = pl.ds(pl.multiple_of(HELD * (g ^ d), HELD), HELD)
-        for p in range(2):
-            here = rate[p, rows, :]
+        for p in (0, 1):
+            plane = parity if p else 1 - parity
+            here = rate[plane, rows, :]
             for k in range(LOCAL):
-                left = res[k, p]
-                residual[k, p, rows, :] = left
-                smoothed[k, p, rows, :] = mid[k, p] + left * here * inverse[k : k + 1, :]
+                left = res[k] if p else mid[k, 2]
+                residual[k, plane, rows, :] = left
+                smoothed[k, plane, rows, :] = mid[k, p] + left * here * inverse[k : k + 1, :]
 
 
 def body(start_field, source, mean_field, kl_fields, triples, coef):
@@ -395,14 +429,14 @@
     modes = triples[:, 1:]
     at = LOCAL * ((modes // LOCAL) ^ g) + modes % LOCAL
     trip = jnp.concatenate([triples[:, 0], at[:, 0], at[:, 1]])
-    fields = pl.pallas_call(
+    *fields, own_fields = pl.pallas_call(
         pack_fields,
-        out_shape=[shape(EDGE_FIELDS, LANES)] * 2,
+        out_shape=[shape(EDGE_FIELDS, LANES)] * 2 + [shape(FIELDS, 2, 40, LANES)],
         in_specs=[SMEM, HBM, HBM],
-        out_specs=[VMEM] * 2,
+        out_specs=[VMEM] * 3,
         scratch_shapes=[
-            pltpu.VMEM((FIELDS - 1, 2, ROWS + 16, LANES), F32),
-            pltpu.SemaphoreType.DMA((3,)),
+            pltpu.VMEM((FIELDS, 2, ROWS + 16, LANES), F32),
+            pltpu.SemaphoreType.DMA((2,)),
         ],
         name="pack_fields",
         **PARAMS,
@@ -422,61 +456,71 @@
         out_shape=[
             shape(SLOTS, 2, 24, LANES), shape(FIELDS, 7, 2, 24, LANES), shape(SLOTS, LANES)
         ],
-        in_specs=[SMEM] * 3 + [VMEM] * 4 + [HBM] * 2,
+        in_specs=[SMEM] * 2 + [VMEM] * 5,
         out_specs=[VMEM] * 3,
         scratch_shapes=[
-            pltpu.VMEM((FIELDS, 2, ROWS + 16, LANES), F32),
-            pltpu.VMEM((FIELDS, 2, 40, LANES), F32),
             pltpu.VMEM((SLOTS, 2, 40, LANES), F32),
             pltpu.VMEM((SLOTS, 2, 24, LANES), F32),
             pltpu.VMEM((SLOTS, 2, 24, LANES), F32),
             pltpu.SMEM((SLOTS + 1,), F32),
-            pltpu.SemaphoreType.DMA((2,)),
         ],
         cost_estimate=COST,
         name="first_inner",
         **PARAMS,
-    )(trip, coef, ids, *starts, mean_field, kl_fields)
-    operands = (trip, coef, ids, acc, faces, inverse, relayed, *starts, *sources, *edges)
-    mid, *mids, even, odd_a, odd_b, outer = pl.pallas_call(
-        first_outer,
-        out_shape=[shape(SLOTS, 2, 32, LANES)]
-        + [shape(LOCAL, 2, HELD, LANES)] * 4
-        + [shape(SLOTS, HELD, LANES)]
-        + [shape(SLOTS // 2, HELD, LANES)] * 2
-        + [shape(FIELDS, 2, 24, LANES)],
-        in_specs=[SMEM] * 3 + [VMEM] * (len(operands) - 3),
-        out_specs=[VMEM] * 9,
-        scratch_shapes=[pltpu.VMEM((SLOTS, 2, 24, LANES), F32)] * 3
-        + [pltpu.VMEM((ROWS + 16, LANES), F32)],
-        name="first_outer",
-        **PARAMS,
-    )(*operands)
+    )(trip, coef, *starts, own_fields)
+    def side(odd, planes, sends):
+        operands = (trip, coef, ids, acc, faces, inverse, *planes, *starts, *sources)
+        return pl.pallas_call(
+            functools.partial(first_side, odd),
+            out_shape=[shape(SLOTS, 32, LANES)]
+            + [shape(SLOTS // sends, HELD, LANES)] * sends
+            + [shape(FIELDS, 24, LANES)],
+            in_specs=[SMEM] * 3 + [VMEM] * (len(operands) - 3),
+            out_specs=[VMEM] * (2 + sends),
+            scratch_shapes=[pltpu.VMEM((SLOTS, 24, LANES), F32)] * 3
+            + [pltpu.VMEM((ROWS + 16, LANES), F32)],
+            cost_estimate=SIDE_COST,
+            name="first_odd" if odd else "first_even",
+            **PARAMS,
+        )(*operands)
+
+    near, far, even = edges
+    mid_even, even, outer_even = side(False, (even,), 1)
+    even = meet(even, evens)
+    mid_odd, odd_a, odd_b, outer_odd = side(True, (near, far, relayed), 2)
     near = meet(odd_a, hops)
-    met = (near, meet(odd_b, odds), meet(even, evens))
+    far = meet(odd_b, odds)
     relayed = meet(near, relay)
-    mids = trade(mids)
+    held = pltpu.VMEM((SLOTS, HELD, LANES), F32)
+    mids = trade(pl.pallas_call(
+        second_even,
+        out_shape=[shape(LOCAL, 3, HELD, LANES)] * 4,
+        in_specs=[SMEM] * 3 + [VMEM] * 9,
+        out_specs=[VMEM] * 4,
+        scratch_shapes=[held] * 5,
+        cost_estimate=COST,
+        name="second_even",
+        **PARAMS,
+    )(trip, coef, ids, faces, outer_even, mid_even, mid_odd, even, *sources))
     acc = pl.pallas_call(
         second_inner,
-        out_shape=shape(SLOTS, 2, HELD, LANES),
-        in_specs=[SMEM] * 3 + [VMEM] * 2,
-        out_specs=VMEM,
-        scratch_shapes=[pltpu.VMEM((SLOTS, 2, HELD, LANES), F32)] * 2,
+        out_shape=[shape(SLOTS, HELD, LANES)] * 2,
+        in_specs=[SMEM] * 3 + [VMEM] * 3,
+        out_specs=[VMEM] * 2,
+        scratch_shapes=[held] * 2,
         cost_estimate=COST,
         name="second_inner",
         **PARAMS,
-    )(trip, coef, ids, mid, faces)
-    operands = (trip, coef, ids, acc, outer, mid, relayed, *sources, *met)
-    lefts = pl.pallas_call(
-        second_outer,
-        out_shape=[shape(LOCAL, 2, HELD, LANES)] * 4,
-        in_specs=[SMEM] * 3 + [VMEM] * (len(operands) - 3),
+    )(trip, coef, ids, faces, mid_odd, mid_even)
+    lefts = trade(pl.pallas_call(
+        second_odd,
+        out_shape=[shape(LOCAL, HELD, LANES)] * 4,
+        in_specs=[SMEM] * 3 + [VMEM] * 11,
         out_specs=[VMEM] * 4,
-        scratch_shapes=[pltpu.VMEM((SLOTS, 2, HELD, LANES), F32)] * 3,
-        name="second_outer",
-        **PARAMS,
-    )(*operands)
-    lefts = trade(lefts)
+        scratch_shapes=[held] * 3,
+        name="second_odd",
+        **PARAMS,
+    )(trip, coef, ids, *acc, outer_odd, mid_odd, near, far, relayed, *sources))
     rate = pl.pallas_call(
         final_rates,
         out_shape=shape(2, ROWS, LANES),

time: 75.1 us -> 72.6 us (0.967)
  starting transfers between devices: 35.7 us -> 32.4 us
  waiting for transfers between devices: 20.2 us -> 17.3 us
  Pallas kernels: 16.9 us -> 19.1 us
  local copies, waits for them, and re-layouts: 1.1 us -> 2.45 us
    ppermute x12, starting transfers between devices: 14.5 us -> 10.6 us  [trade(): lax.ppermute(parts[d], 'mode', [(i, i ^ d) for i in range(GROUPS)])]
    pallas_call x4 -> x6, Pallas kernels: 7.67 us -> 10.2 us  [the longest x2 3.33 us: side(): pl.pallas_call(functools.partial(first_side, odd), out_shape=[shape(SLOTS...]
    ppermute x8, waiting for transfers between devices: 9.73 us -> 7.54 us  [meet(): return lax.ppermute(x, 'space', pairs)]
  transfers between devices with their start and end apart: 20 -> 20, of which waited for: 7 -> 8; matrix products, arithmetic and copies ran while one was open for 0% -> 0% of each run, Pallas kernels for 17% -> 23%
where the time goes in v4:
time: 72.6 us; the launch traced here: 72.3 us
  starting transfers between devices  32.4 us (45%)
  Pallas kernels  19.1 us (26%)
  waiting for transfers between devices  17.3 us (24%)
  local copies, waits for them, and re-layouts  2.45 us (3%)
  between operations  0.87 us (1%)
    ppermute x8, starting transfers between devices, meet(): return lax.ppermute(x, 'space', pairs)  21.8 us
    ppermute x12, starting transfers between devices, trade(): lax.ppermute(parts[d], 'mode', [(i, i ^ d) for i in range(GROUPS)])  10.6 us
    ppermute x12, waiting for transfers between devices, trade(): lax.ppermute(parts[d], 'mode', [(i, i ^ d) for i in range(GROUPS)])  9.81 us
    ppermute x8, waiting for transfers between devices, meet(): return lax.ppermute(x, 'space', pairs)  7.54 us
    pallas_call x1, Pallas kernels, body(): pl.pallas_call(first_inner, out_shape=[shape(SLOTS, 2, 24, LANES), shape(...  3.99 us
    pallas_call x2, Pallas kernels, side(): pl.pallas_call(functools.partial(first_side, odd), out_shape=[shape(SLOTS...  3.33 us
    pallas_call x1, Pallas kernels, body(): pl.pallas_call(second_even, out_shape=[shape(LOCAL, 3, HELD, LANES)] * 4,...  2.57 us
    pallas_call x1, Pallas kernels, body(): pl.pallas_call(second_inner, out_shape=[shape(SLOTS, HELD, LANES)] * 2, i...  2.23 us
  transfers between devices with their start and end apart: 20, of which 8 were waited for; matrix products, arithmetic and copies ran while one was open for 0% of the time, Pallas kernels for 23%

profile of v4, /device:TPU:9, one launch (start us, length us, event | category | flops | bytes accessed | tf_op | source)
XLA Modules:
  0.0 72.3 jit_solution(7961484234810281426)
XLA Ops:
  0.7 1.1 %copy-done = f32[9,2,64,128]{3,2,1,0:T(8,128)S(1)} copy-done((f32[9,2,64,128]{3,2,1,0:T(8,128)S(1)}, f32[9,2,64,128]{3,2,1,0:T(8,128)}, u32[]{:S(2)}) %copy-start) | copy-done | bytes 589848
  3.3 1.6 %collective-permute-start.2 = (f32[360,128]{1,0:T(8,128)S(1)}, f32[360,128]{1,0:T(8,128)S(1)}, u32[]{:S(2)}, u32[]{:S(2)}) collective-permute-start(f32[360,128]{1,0:T(8,128)S(1)} %get-tuple-element.56), channel_id=1, source_target_pairs={{0,3},{1,2},{2,1},{3,0},{4,7},{5,6},{6,5},{7,4},{8,11},{9,10},{10,... | collective-permute-start | bytes 552968 | tf_op jit(solution)/shard_map/ppermute | solution.py:386
  5.5 2.6 %collective-permute-start.4 = (f32[324,128]{1,0:T(8,128)S(1)}, f32[324,128]{1,0:T(8,128)S(1)}, u32[]{:S(2)}, u32[]{:S(2)}) collective-permute-start(f32[324,128]{1,0:T(8,128)S(1)} %pack_near.1), channel_id=1, source_target_pairs={{4,8},{8,4},{20,24},{24,20},{36,40},{40,36},{52,56},{56,52},{68,72... | collective-permute-start | bytes 497672 | tf_op jit(solution)/shard_map/ppermute | solution.py:382
  8.8 1.3 %collective-permute-done.2.s3.rest_4_.rest_6_ = f32[360,128]{1,0:T(8,128)S(1)} collective-permute-done((f32[360,128]{1,0:T(8,128)S(1)}, f32[360,128]{1,0:T(8,128)S(1)}, u32[]{:S(2)}, u32[]{:S(2)}) %collective-permute-start.2) | collective-permute-done | bytes 184352 | tf_op jit(solution)/shard_map/ppermute | solution.py:386
  10.3 1.5 %collective-permute-start.7 = (f32[324,128]{1,0:T(8,128)S(1)}, f32[324,128]{1,0:T(8,128)S(1)}, u32[]{:S(2)}, u32[]{:S(2)}) collective-permute-start(f32[324,128]{1,0:T(8,128)S(1)} %get-tuple-element.74), channel_id=1, source_target_pairs={{0,2},{1,3},{2,0},{3,1},{4,6},{5,7},{6,4},{7,5},{8,10},{9,11},{10,... | collective-permute-start | bytes 497672 | tf_op jit(solution)/shard_map/ppermute | solution.py:386
  14.3 1.3 %collective-permute-start.6 = (f32[784,128]{1,0:T(8,128)S(1)}, f32[784,128]{1,0:T(8,128)S(1)}, u32[]{:S(2)}, u32[]{:S(2)}) collective-permute-start(f32[784,128]{1,0:T(8,128)S(1)} %get-tuple-element.66), channel_id=1, source_target_pairs={{0,4},{4,0},{8,12},{12,8},{16,20},{20,16},{24,28},{28,24},{32,36},... | collective-permute-start | bytes 1204232 | tf_op jit(solution)/shard_map/ppermute | solution.py:382
  15.6 8.9 %collective-permute-start.5 = (f32[460,128]{1,0:T(8,128)S(1)}, f32[460,128]{1,0:T(8,128)S(1)}, u32[]{:S(2)}, u32[]{:S(2)}) collective-permute-start(f32[460,128]{1,0:T(8,128)S(1)} %get-tuple-element.65), channel_id=1, source_target_pairs={{4,8},{8,4},{12,16},{16,12},{20,24},{24,20},{28,32},{32,28},{36,40... | collective-permute-start | bytes 706568 | tf_op jit(solution)/shard_map/ppermute | solution.py:382
  24.6 1.9 %collective-permute-start.9 = (f32[324,128]{1,0:T(8,128)S(1)}, f32[324,128]{1,0:T(8,128)S(1)}, u32[]{:S(2)}, u32[]{:S(2)}) collective-permute-start(f32[324,128]{1,0:T(8,128)S(1)} %collective-permute-done.4.rest_0_), channel_id=1, source_target_pairs={{0,16},{16,32},{32,48},{48,64},{64,80},{80,96},{96,112},{112,128},... | collective-permute-start | bytes 497672 | tf_op jit(solution)/shard_map/ppermute | solution.py:382
  28.0 4.0 %first_inner.1 = (f32[36,2,24,128]{3,2,1,0:T(8,128)S(1)}, f32[5,7,2,24,128]{4,3,2,1,0:T(8,128)S(1)}, f32[36,128]{1,0:T(8,128)S(1)}) custom-call(s32[468]{0:T(512)S(1)} %pad_add_fusion.trip, f32[156]{0:T(256)S(1)} %copy-done.4, f32[360,128]{1,0:T(8,128)S(1)} %get-tuple-element.48.s0.rest_1_.rest_3_, f32[360,128]{1,0:T(8,128)S(1)} %collective-permute-done.s1.rest_2_.rest_4_, ...), custom_call_target="tpu_custom_call" | custom-call | flops 20000000 | bytes 12000000 | tf_op jit(solution)/shard_map/first_inner/pallas_call | solution.py:454
  32.0 1.7 %first_even.1 = (f32[36,32,128]{2,1,0:T(8,128)S(1)}, f32[36,16,128]{2,1,0:T(8,128)S(1)}, f32[5,24,128]{2,1,0:T(8,128)S(1)}) custom-call(s32[468]{0:T(512)S(1)} %pad_add_fusion.trip, f32[156]{0:T(256)S(1)} %copy-done.4, s32[3]{0:T(128)S(1)} %pad_add_fusion.1.ids, f32[36,2,24,128]{3,2,1,0:T(8,128)S(1)} %get-tuple-element.71.inner, ...), custom_call_target="tpu_custom_call" | custom-call | flops 5000000 | bytes 3000000 | tf_op jit(solution)/shard_map/first_even/pallas_call | solution.py:473
  33.8 5.7 %collective-permute-done.9.rest_2_ = f32[324,128]{1,0:T(8,128)S(1)} collective-permute-done((f32[324,128]{1,0:T(8,128)S(1)}, f32[324,128]{1,0:T(8,128)S(1)}, u32[]{:S(2)}, u32[]{:S(2)}) %collective-permute-start.9) | collective-permute-done | bytes 165920 | tf_op jit(solution)/shard_map/ppermute | solution.py:382
  39.6 1.7 %first_odd.1 = (f32[36,32,128]{2,1,0:T(8,128)S(1)}, f32[18,16,128]{2,1,0:T(8,128)S(1)}, f32[18,16,128]{2,1,0:T(8,128)S(1)}, f32[5,24,128]{2,1,0:T(8,128)S(1)}) custom-call(s32[468]{0:T(512)S(1)} %pad_add_fusion.trip, f32[156]{0:T(256)S(1)} %copy-done.4, s32[3]{0:T(128)S(1)} %pad_add_fusion.1.ids, f32[36,2,24,128]{3,2,1,0:T(8,128)S(1)} %get-tuple-element.71.inner, ...), custom_call_target="tpu_custom_call" | custom-call | flops 5000000 | bytes 3000000 | tf_op jit(solution)/shard_map/first_odd/pallas_call | solution.py:473
  41.4 3.5 %collective-permute-start.15 = (f32[18,16,128]{2,1,0:T(8,128)S(1)}, f32[18,16,128]{2,1,0:T(8,128)S(1)}, u32[]{:S(2)}, u32[]{:S(2)}) collective-permute-start(f32[18,16,128]{2,1,0:T(8,128)S(1)} %get-tuple-element.89), channel_id=1, source_target_pairs={{4,8},{8,4},{12,16},{16,12},{20,24},{24,20},{28,32},{32,28},{36,40... | collective-permute-start | bytes 442376 | tf_op jit(solution)/shard_map/ppermute | solution.py:382
  44.8 1.7 %collective-permute-done.14.near = f32[18,16,128]{2,1,0:T(8,128)S(1)} collective-permute-done((f32[18,16,128]{2,1,0:T(8,128)S(1)}, f32[18,16,128]{2,1,0:T(8,128)S(1)}, u32[]{:S(2)}, u32[]{:S(2)}) %collective-permute-start.14) | collective-permute-done | bytes 147488 | tf_op jit(solution)/shard_map/ppermute | solution.py:382
  46.5 3.4 %collective-permute-start.16 = (f32[18,16,128]{2,1,0:T(8,128)S(1)}, f32[18,16,128]{2,1,0:T(8,128)S(1)}, u32[]{:S(2)}, u32[]{:S(2)}) collective-permute-start(f32[18,16,128]{2,1,0:T(8,128)S(1)} %collective-permute-done.14.near), channel_id=1, source_target_pairs={{0,16},{16,32},{32,48},{48,64},{64,80},{80,96},{96,112},{112,128},... | collective-permute-start | bytes 442376 | tf_op jit(solution)/shard_map/ppermute | solution.py:382
  49.9 2.6 %second_even.1 = (f32[9,3,16,128]{3,2,1,0:T(8,128)S(1)}, f32[9,3,16,128]{3,2,1,0:T(8,128)S(1)}, f32[9,3,16,128]{3,2,1,0:T(8,128)S(1)}, f32[9,3,16,128]{3,2,1,0:T(8,128)S(1)}) custom-call(s32[468]{0:T(512)S(1)} %pad_add_fusion.trip, f32[156]{0:T(256)S(1)} %copy-done.4, s32[3]{0:T(128)S(1)} %pad_add_fusion.1.ids, ...), custom_call_target="tpu_custom_call" | custom-call | flops 20000000 | bytes 12000000 | tf_op jit(solution)/shard_map/second_even/pallas_call | solution.py:495
  52.5 3.0 %collective-permute-start.11 = (f32[9,3,16,128]{3,2,1,0:T(8,128)S(1)}, f32[9,3,16,128]{3,2,1,0:T(8,128)S(1)}, u32[]{:S(2)}, u32[]{:S(2)}) collective-permute-start(f32[9,3,16,128]{3,2,1,0:T(8,128)S(1)} %get-tuple-element.82), channel_id=1, source_target_pairs={{0,1},{1,0},{2,3},{3,2},{4,5},{5,4},{6,7},{7,6},{8,9},{9,8},{10,11... | collective-permute-start | bytes 663560 | tf_op jit(solution)/shard_map/ppermute | solution.py:386
  55.6 1.7 %collective-permute-start.13 = (f32[9,3,16,128]{3,2,1,0:T(8,128)S(1)}, f32[9,3,16,128]{3,2,1,0:T(8,128)S(1)}, u32[]{:S(2)}, u32[]{:S(2)}) collective-permute-start(f32[9,3,16,128]{3,2,1,0:T(8,128)S(1)} %get-tuple-element.84), channel_id=1, source_target_pairs={{0,3},{1,2},{2,1},{3,0},{4,7},{5,6},{6,5},{7,4},{8,11},{9,10},{10,... | collective-permute-start | bytes 663560 | tf_op jit(solution)/shard_map/ppermute | solution.py:386
  57.3 2.2 %second_inner.1 = (f32[36,16,128]{2,1,0:T(8,128)S(1)}, f32[36,16,128]{2,1,0:T(8,128)S(1)}) custom-call(s32[468]{0:T(512)S(1)} %pad_add_fusion.trip, f32[156]{0:T(256)S(1)} %copy-done.4, s32[3]{0:T(128)S(1)} %pad_add_fusion.1.ids, f32[5,7,2,24,128]{4,3,2,1,0:T(8,128)S(1)} %get-tuple-element.70.faces, f32[36,32,128]{2,1,0:T(8,128)S(1)} %get-tuple-element.79.other.mine, ...), custom_call_target="tpu_custom_call" | custom-call | flops 20000000 | bytes 12000000 | tf_op jit(solution)/shard_map/second_inner/pallas_call | solution.py:505
  59.5 1.5 %second_odd.1 = (f32[9,16,128]{2,1,0:T(8,128)S(1)}, f32[9,16,128]{2,1,0:T(8,128)S(1)}, f32[9,16,128]{2,1,0:T(8,128)S(1)}, f32[9,16,128]{2,1,0:T(8,128)S(1)}) custom-call(s32[468]{0:T(512)S(1)} %pad_add_fusion.trip, f32[156]{0:T(256)S(1)} %copy-done.4, s32[3]{0:T(128)S(1)} %pad_add_fusion.1.ids, f32[36,16,128]{2,1,0:T(8,128)S(1)} %get-tuple-element.85.inner, ...), custom_call_target="tpu_custom_call" | custom-call | tf_op jit(solution)/shard_map/second_odd/pallas_call | solution.py:515
  61.4 0.9 %collective-permute-done.17.r1 = f32[9,16,128]{2,1,0:T(8,128)S(1)} collective-permute-done((f32[9,16,128]{2,1,0:T(8,128)S(1)}, f32[9,16,128]{2,1,0:T(8,128)S(1)}, u32[]{:S(2)}, u32[]{:S(2)}) %collective-permute-start.17) | collective-permute-done | bytes 73760 | tf_op jit(solution)/shard_map/ppermute | solution.py:386
  63.9 5.0 %collective-permute-done.18.r2 = f32[9,16,128]{2,1,0:T(8,128)S(1)} collective-permute-done((f32[9,16,128]{2,1,0:T(8,128)S(1)}, f32[9,16,128]{2,1,0:T(8,128)S(1)}, u32[]{:S(2)}, u32[]{:S(2)}) %collective-permute-start.18) | collective-permute-done | bytes 73760 | tf_op jit(solution)/shard_map/ppermute | solution.py:386
  68.9 1.8 %collective-permute-done.19.r3 = f32[9,16,128]{2,1,0:T(8,128)S(1)} collective-permute-done((f32[9,16,128]{2,1,0:T(8,128)S(1)}, f32[9,16,128]{2,1,0:T(8,128)S(1)}, u32[]{:S(2)}, u32[]{:S(2)}) %collective-permute-start.19) | collective-permute-done | bytes 73760 | tf_op jit(solution)/shard_map/ppermute | solution.py:386
  70.6 1.7 %second_sweep.1 = (f32[9,2,64,128]{3,2,1,0:T(8,128)}, f32[9,2,64,128]{3,2,1,0:T(8,128)}) custom-call(s32[3]{0:T(128)S(1)} %pad_add_fusion.1.ids, f32[2,64,128]{2,1,0:T(8,128)S(1)} %final_rates.1.rate, f32[36,128]{1,0:T(8,128)S(1)} %get-tuple-element.69.inverse, f32[9,3,16,128]{3,2,1,0:T(8,128)S(1)} %get-tuple-element.81.m0, ...), custom_call_target="tpu_custom_call" | custom-call | tf_op jit(solution)/shard_map/second_sweep/pallas_call | solution.py:533
  (47 shorter events, 9.2 us)
Async XLA Ops:
  1.8 6.3 %copy-start.1 = (f32[9,2,64,128]{3,2,1,0:T(8,128)S(1)}, f32[9,2,64,128]{3,2,1,0:T(8,128)}, u32[]{:S(2)}) copy-start(f32[9,2,64,128]{3,2,1,0:T(8,128)} %source) | copy-start | bytes 1769476
  2.5 2.4 %collective-permute-start = (f32[360,128]{1,0:T(8,128)S(1)}, f32[360,128]{1,0:T(8,128)S(1)}, u32[]{:S(2)}, u32[]{:S(2)}) collective-permute-start(f32[360,128]{1,0:T(8,128)S(1)} %get-tuple-element.49), channel_id=1, source_target_pairs={{0,1},{1,0},{2,3},{3,2},{4,5},{5,4},{6,7},{7,6},{8,9},{9,8},{10,11... | collective-permute-start | bytes 552968 | tf_op jit(solution)/shard_map/ppermute | solution.py:386
  3.3 6.9 %collective-permute-start.2 = (f32[360,128]{1,0:T(8,128)S(1)}, f32[360,128]{1,0:T(8,128)S(1)}, u32[]{:S(2)}, u32[]{:S(2)}) collective-permute-start(f32[360,128]{1,0:T(8,128)S(1)} %get-tuple-element.56), channel_id=1, source_target_pairs={{0,3},{1,2},{2,1},{3,0},{4,7},{5,6},{6,5},{7,4},{8,11},{9,10},{10,... | collective-permute-start | bytes 552968 | tf_op jit(solution)/shard_map/ppermute | solution.py:386
  4.9 8.8 %collective-permute-start.1 = (f32[360,128]{1,0:T(8,128)S(1)}, f32[360,128]{1,0:T(8,128)S(1)}, u32[]{:S(2)}, u32[]{:S(2)}) collective-permute-start(f32[360,128]{1,0:T(8,128)S(1)} %get-tuple-element.50), channel_id=1, source_target_pairs={{0,2},{1,3},{2,0},{3,1},{4,6},{5,7},{6,4},{7,5},{8,10},{9,11},{10,... | collective-permute-start | bytes 552968 | tf_op jit(solution)/shard_map/ppermute | solution.py:386
  5.5 6.8 %copy-start.2 = (f32[4,2,64,128]{3,2,1,0:T(8,128)S(1)}, f32[4,2,64,128]{3,2,1,0:T(8,128)}, u32[]{:S(2)}) copy-start(f32[4,2,64,128]{3,2,1,0:T(8,128)} %kl) | copy-start | bytes 786436
  5.5 6.8 %copy-start.3 = (f32[2,64,128]{2,1,0:T(8,128)S(1)}, f32[2,64,128]{2,1,0:T(8,128)}, u32[]{:S(2)}) copy-start(f32[2,64,128]{2,1,0:T(8,128)} %mean.2) | copy-start | bytes 196612
  5.5 8.2 %collective-permute-start.4 = (f32[324,128]{1,0:T(8,128)S(1)}, f32[324,128]{1,0:T(8,128)S(1)}, u32[]{:S(2)}, u32[]{:S(2)}) collective-permute-start(f32[324,128]{1,0:T(8,128)S(1)} %pack_near.1), channel_id=1, source_target_pairs={{4,8},{8,4},{20,24},{24,20},{36,40},{40,36},{52,56},{56,52},{68,72... | collective-permute-start | bytes 497672 | tf_op jit(solution)/shard_map/ppermute | solution.py:382
  10.1 3.6 %collective-permute-start.3 = (f32[324,128]{1,0:T(8,128)S(1)}, f32[324,128]{1,0:T(8,128)S(1)}, u32[]{:S(2)}, u32[]{:S(2)}) collective-permute-start(f32[324,128]{1,0:T(8,128)S(1)} %get-tuple-element.57), channel_id=1, source_target_pairs={{0,1},{1,0},{2,3},{3,2},{4,5},{5,4},{6,7},{7,6},{8,9},{9,8},{10,11... | collective-permute-start | bytes 497672 | tf_op jit(solution)/shard_map/ppermute | solution.py:386
  10.3 21.7 %collective-permute-start.7 = (f32[324,128]{1,0:T(8,128)S(1)}, f32[324,128]{1,0:T(8,128)S(1)}, u32[]{:S(2)}, u32[]{:S(2)}) collective-permute-start(f32[324,128]{1,0:T(8,128)S(1)} %get-tuple-element.74), channel_id=1, source_target_pairs={{0,2},{1,3},{2,0},{3,1},{4,6},{5,7},{6,4},{7,5},{8,10},{9,11},{10,... | collective-permute-start | bytes 497672 | tf_op jit(solution)/shard_map/ppermute | solution.py:386
  11.8 20.2 %collective-permute-start.8 = (f32[324,128]{1,0:T(8,128)S(1)}, f32[324,128]{1,0:T(8,128)S(1)}, u32[]{:S(2)}, u32[]{:S(2)}) collective-permute-start(f32[324,128]{1,0:T(8,128)S(1)} %get-tuple-element.75), channel_id=1, source_target_pairs={{0,3},{1,2},{2,1},{3,0},{4,7},{5,6},{6,5},{7,4},{8,11},{9,10},{10,... | collective-permute-start | bytes 497672 | tf_op jit(solution)/shard_map/ppermute | solution.py:386
  13.7 1.9 %copy-start.5 = (s32[156,3]{0,1:T(4,128)S(1)}, s32[156,3]{0,1:T(4,128)}, u32[]{:S(2)}) copy-start(s32[156,3]{0,1:T(4,128)} %param.10) | copy-start | bytes 5620
  14.3 17.7 %collective-permute-start.6 = (f32[784,128]{1,0:T(8,128)S(1)}, f32[784,128]{1,0:T(8,128)S(1)}, u32[]{:S(2)}, u32[]{:S(2)}) collective-permute-start(f32[784,128]{1,0:T(8,128)S(1)} %get-tuple-element.66), channel_id=1, source_target_pairs={{0,4},{4,0},{8,12},{12,8},{16,20},{20,16},{24,28},{28,24},{32,36},... | collective-permute-start | bytes 1204232 | tf_op jit(solution)/shard_map/ppermute | solution.py:382
  15.6 23.9 %collective-permute-start.5 = (f32[460,128]{1,0:T(8,128)S(1)}, f32[460,128]{1,0:T(8,128)S(1)}, u32[]{:S(2)}, u32[]{:S(2)}) collective-permute-start(f32[460,128]{1,0:T(8,128)S(1)} %get-tuple-element.65), channel_id=1, source_target_pairs={{4,8},{8,4},{12,16},{16,12},{20,24},{24,20},{28,32},{32,28},{36,40... | collective-permute-start | bytes 706568 | tf_op jit(solution)/shard_map/ppermute | solution.py:382
  24.6 14.9 %collective-permute-start.9 = (f32[324,128]{1,0:T(8,128)S(1)}, f32[324,128]{1,0:T(8,128)S(1)}, u32[]{:S(2)}, u32[]{:S(2)}) collective-permute-start(f32[324,128]{1,0:T(8,128)S(1)} %collective-permute-done.4.rest_0_), channel_id=1, source_target_pairs={{0,16},{16,32},{32,48},{48,64},{64,80},{80,96},{96,112},{112,128},... | collective-permute-start | bytes 497672 | tf_op jit(solution)/shard_map/ppermute | solution.py:382
  33.7 16.3 %collective-permute-start.10 = (f32[36,16,128]{2,1,0:T(8,128)S(1)}, f32[36,16,128]{2,1,0:T(8,128)S(1)}, u32[]{:S(2)}, u32[]{:S(2)}) collective-permute-start(f32[36,16,128]{2,1,0:T(8,128)S(1)} %get-tuple-element.80), channel_id=1, source_target_pairs={{0,4},{4,0},{8,12},{12,8},{16,20},{20,16},{24,28},{28,24},{32,36},... | collective-permute-start | bytes 884744 | tf_op jit(solution)/shard_map/ppermute | solution.py:382
  41.3 5.3 %collective-permute-start.14 = (f32[18,16,128]{2,1,0:T(8,128)S(1)}, f32[18,16,128]{2,1,0:T(8,128)S(1)}, u32[]{:S(2)}, u32[]{:S(2)}) collective-permute-start(f32[18,16,128]{2,1,0:T(8,128)S(1)} %get-tuple-element.88), channel_id=1, source_target_pairs={{4,8},{8,4},{20,24},{24,20},{36,40},{40,36},{52,56},{56,52},{68,72... | collective-permute-start | bytes 442376 | tf_op jit(solution)/shard_map/ppermute | solution.py:382
  41.4 18.2 %collective-permute-start.15 = (f32[18,16,128]{2,1,0:T(8,128)S(1)}, f32[18,16,128]{2,1,0:T(8,128)S(1)}, u32[]{:S(2)}, u32[]{:S(2)}) collective-permute-start(f32[18,16,128]{2,1,0:T(8,128)S(1)} %get-tuple-element.89), channel_id=1, source_target_pairs={{4,8},{8,4},{12,16},{16,12},{20,24},{24,20},{28,32},{32,28},{36,40... | collective-permute-start | bytes 442376 | tf_op jit(solution)/shard_map/ppermute | solution.py:382
  46.5 13.0 %collective-permute-start.16 = (f32[18,16,128]{2,1,0:T(8,128)S(1)}, f32[18,16,128]{2,1,0:T(8,128)S(1)}, u32[]{:S(2)}, u32[]{:S(2)}) collective-permute-start(f32[18,16,128]{2,1,0:T(8,128)S(1)} %collective-permute-done.14.near), channel_id=1, source_target_pairs={{0,16},{16,32},{32,48},{48,64},{64,80},{80,96},{96,112},{112,128},... | collective-permute-start | bytes 442376 | tf_op jit(solution)/shard_map/ppermute | solution.py:382
  52.5 18.1 %collective-permute-start.11 = (f32[9,3,16,128]{3,2,1,0:T(8,128)S(1)}, f32[9,3,16,128]{3,2,1,0:T(8,128)S(1)}, u32[]{:S(2)}, u32[]{:S(2)}) collective-permute-start(f32[9,3,16,128]{3,2,1,0:T(8,128)S(1)} %get-tuple-element.82), channel_id=1, source_target_pairs={{0,1},{1,0},{2,3},{3,2},{4,5},{5,4},{6,7},{7,6},{8,9},{9,8},{10,11... | collective-permute-start | bytes 663560 | tf_op jit(solution)/shard_map/ppermute | solution.py:386
  55.6 15.1 %collective-permute-start.12 = (f32[9,3,16,128]{3,2,1,0:T(8,128)S(1)}, f32[9,3,16,128]{3,2,1,0:T(8,128)S(1)}, u32[]{:S(2)}, u32[]{:S(2)}) collective-permute-start(f32[9,3,16,128]{3,2,1,0:T(8,128)S(1)} %get-tuple-element.83), channel_id=1, source_target_pairs={{0,2},{1,3},{2,0},{3,1},{4,6},{5,7},{6,4},{7,5},{8,10},{9,11},{10,... | collective-permute-start | bytes 663560 | tf_op jit(solution)/shard_map/ppermute | solution.py:386
  55.6 15.1 %collective-permute-start.13 = (f32[9,3,16,128]{3,2,1,0:T(8,128)S(1)}, f32[9,3,16,128]{3,2,1,0:T(8,128)S(1)}, u32[]{:S(2)}, u32[]{:S(2)}) collective-permute-start(f32[9,3,16,128]{3,2,1,0:T(8,128)S(1)} %get-tuple-element.84), channel_id=1, source_target_pairs={{0,3},{1,2},{2,1},{3,0},{4,7},{5,6},{6,5},{7,4},{8,11},{9,10},{10,... | collective-permute-start | bytes 663560 | tf_op jit(solution)/shard_map/ppermute | solution.py:386
  61.0 1.4 %collective-permute-start.17 = (f32[9,16,128]{2,1,0:T(8,128)S(1)}, f32[9,16,128]{2,1,0:T(8,128)S(1)}, u32[]{:S(2)}, u32[]{:S(2)}) collective-permute-start(f32[9,16,128]{2,1,0:T(8,128)S(1)} %get-tuple-element.91), channel_id=1, source_target_pairs={{0,1},{1,0},{2,3},{3,2},{4,5},{5,4},{6,7},{7,6},{8,9},{9,8},{10,11... | collective-permute-start | bytes 221192 | tf_op jit(solution)/shard_map/ppermute | solution.py:386
  61.4 7.5 %collective-permute-start.18 = (f32[9,16,128]{2,1,0:T(8,128)S(1)}, f32[9,16,128]{2,1,0:T(8,128)S(1)}, u32[]{:S(2)}, u32[]{:S(2)}) collective-permute-start(f32[9,16,128]{2,1,0:T(8,128)S(1)} %get-tuple-element.92), channel_id=1, source_target_pairs={{0,2},{1,3},{2,0},{3,1},{4,6},{5,7},{6,4},{7,5},{8,10},{9,11},{10,... | collective-permute-start | bytes 221192 | tf_op jit(solution)/shard_map/ppermute | solution.py:386
  62.4 8.3 %collective-permute-start.19 = (f32[9,16,128]{2,1,0:T(8,128)S(1)}, f32[9,16,128]{2,1,0:T(8,128)S(1)}, u32[]{:S(2)}, u32[]{:S(2)}) collective-permute-start(f32[9,16,128]{2,1,0:T(8,128)S(1)} %get-tuple-element.93), channel_id=1, source_target_pairs={{0,3},{1,2},{2,1},{3,0},{4,7},{5,6},{6,5},{7,4},{8,11},{9,10},{10,... | collective-permute-start | bytes 221192 | tf_op jit(solution)/shard_map/ppermute | solution.py:386
  (3 other events, 2.4 us)

commit v5 on v4

--- a/solution.py
+++ b/solution.py
@@ -14,7 +14,7 @@
 ENTRIES = 156
 EDGE = 18 * SLOTS
 EDGE_FIELDS = ROWS + 18 * (FIELDS - 1)
-UNROLL = 3
+UNROLL = 6
 NEAR = 2 * LOCAL
 F32 = jnp.float32
 VMEM = pl.BlockSpec(memory_space=pltpu.VMEM)

time: 72.6 us -> 72.4 us (level)
  no operation moved by 1% of the time
where the time goes in v5:
time: 72.4 us; the launch traced here: 72.1 us
  starting transfers between devices  32.6 us (45%)
  Pallas kernels  18.6 us (26%)
  waiting for transfers between devices  17.4 us (24%)
  local copies, waits for them, and re-layouts  2.45 us (3%)
  between operations  0.87 us (1%)
    ppermute x8, starting transfers between devices, meet(): return lax.ppermute(x, 'space', pairs)  21.8 us
    ppermute x12, starting transfers between devices, trade(): lax.ppermute(parts[d], 'mode', [(i, i ^ d) for i in range(GROUPS)])  10.8 us
    ppermute x12, waiting for transfers between devices, trade(): lax.ppermute(parts[d], 'mode', [(i, i ^ d) for i in range(GROUPS)])  9.85 us
    ppermute x8, waiting for transfers between devices, meet(): return lax.ppermute(x, 'space', pairs)  7.59 us
    pallas_call x1, Pallas kernels, body(): pl.pallas_call(first_inner, out_shape=[shape(SLOTS, 2, 24, LANES), shape(...  4.02 us
    pallas_call x2, Pallas kernels, side(): pl.pallas_call(functools.partial(first_side, odd), out_shape=[shape(SLOTS...  3.15 us
    pallas_call x1, Pallas kernels, body(): pl.pallas_call(second_even, out_shape=[shape(LOCAL, 3, HELD, LANES)] * 4,...  2.47 us
    pallas_call x1, Pallas kernels, body(): pl.pallas_call(second_inner, out_shape=[shape(SLOTS, HELD, LANES)] * 2, i...  2.1 us
  transfers between devices with their start and end apart: 20, of which 8 were waited for; matrix products, arithmetic and copies ran while one was open for 0% of the time, Pallas kernels for 23%

profile of v5, /device:TPU:9, one launch (start us, length us, event | category | flops | bytes accessed | tf_op | source)
XLA Modules:
  0.0 72.1 jit_solution(1568930315468168370)
XLA Ops:
  0.7 1.1 %copy-done = f32[9,2,64,128]{3,2,1,0:T(8,128)S(1)} copy-done((f32[9,2,64,128]{3,2,1,0:T(8,128)S(1)}, f32[9,2,64,128]{3,2,1,0:T(8,128)}, u32[]{:S(2)}) %copy-start) | copy-done | bytes 589848
  3.3 1.6 %collective-permute-start.2 = (f32[360,128]{1,0:T(8,128)S(1)}, f32[360,128]{1,0:T(8,128)S(1)}, u32[]{:S(2)}, u32[]{:S(2)}) collective-permute-start(f32[360,128]{1,0:T(8,128)S(1)} %get-tuple-element.56), channel_id=1, source_target_pairs={{0,3},{1,2},{2,1},{3,0},{4,7},{5,6},{6,5},{7,4},{8,11},{9,10},{10,... | collective-permute-start | bytes 552968 | tf_op jit(solution)/shard_map/ppermute | solution.py:386
  5.5 2.6 %collective-permute-start.4 = (f32[324,128]{1,0:T(8,128)S(1)}, f32[324,128]{1,0:T(8,128)S(1)}, u32[]{:S(2)}, u32[]{:S(2)}) collective-permute-start(f32[324,128]{1,0:T(8,128)S(1)} %pack_near.1), channel_id=1, source_target_pairs={{4,8},{8,4},{20,24},{24,20},{36,40},{40,36},{52,56},{56,52},{68,72... | collective-permute-start | bytes 497672 | tf_op jit(solution)/shard_map/ppermute | solution.py:382
  8.8 1.3 %collective-permute-done.2.s3.rest_4_.rest_6_ = f32[360,128]{1,0:T(8,128)S(1)} collective-permute-done((f32[360,128]{1,0:T(8,128)S(1)}, f32[360,128]{1,0:T(8,128)S(1)}, u32[]{:S(2)}, u32[]{:S(2)}) %collective-permute-start.2) | collective-permute-done | bytes 184352 | tf_op jit(solution)/shard_map/ppermute | solution.py:386
  10.3 1.5 %collective-permute-start.7 = (f32[324,128]{1,0:T(8,128)S(1)}, f32[324,128]{1,0:T(8,128)S(1)}, u32[]{:S(2)}, u32[]{:S(2)}) collective-permute-start(f32[324,128]{1,0:T(8,128)S(1)} %get-tuple-element.74), channel_id=1, source_target_pairs={{0,2},{1,3},{2,0},{3,1},{4,6},{5,7},{6,4},{7,5},{8,10},{9,11},{10,... | collective-permute-start | bytes 497672 | tf_op jit(solution)/shard_map/ppermute | solution.py:386
  14.3 1.3 %collective-permute-start.6 = (f32[784,128]{1,0:T(8,128)S(1)}, f32[784,128]{1,0:T(8,128)S(1)}, u32[]{:S(2)}, u32[]{:S(2)}) collective-permute-start(f32[784,128]{1,0:T(8,128)S(1)} %get-tuple-element.66), channel_id=1, source_target_pairs={{0,4},{4,0},{8,12},{12,8},{16,20},{20,16},{24,28},{28,24},{32,36},... | collective-permute-start | bytes 1204232 | tf_op jit(solution)/shard_map/ppermute | solution.py:382
  15.6 8.9 %collective-permute-start.5 = (f32[460,128]{1,0:T(8,128)S(1)}, f32[460,128]{1,0:T(8,128)S(1)}, u32[]{:S(2)}, u32[]{:S(2)}) collective-permute-start(f32[460,128]{1,0:T(8,128)S(1)} %get-tuple-element.65), channel_id=1, source_target_pairs={{4,8},{8,4},{12,16},{16,12},{20,24},{24,20},{28,32},{32,28},{36,40... | collective-permute-start | bytes 706568 | tf_op jit(solution)/shard_map/ppermute | solution.py:382
  24.6 1.9 %collective-permute-start.9 = (f32[324,128]{1,0:T(8,128)S(1)}, f32[324,128]{1,0:T(8,128)S(1)}, u32[]{:S(2)}, u32[]{:S(2)}) collective-permute-start(f32[324,128]{1,0:T(8,128)S(1)} %collective-permute-done.4.rest_0_), channel_id=1, source_target_pairs={{0,16},{16,32},{32,48},{48,64},{64,80},{80,96},{96,112},{112,128},... | collective-permute-start | bytes 497672 | tf_op jit(solution)/shard_map/ppermute | solution.py:382
  28.0 4.0 %first_inner.1 = (f32[36,2,24,128]{3,2,1,0:T(8,128)S(1)}, f32[5,7,2,24,128]{4,3,2,1,0:T(8,128)S(1)}, f32[36,128]{1,0:T(8,128)S(1)}) custom-call(s32[468]{0:T(512)S(1)} %pad_add_fusion.trip, f32[156]{0:T(256)S(1)} %copy-done.4, f32[360,128]{1,0:T(8,128)S(1)} %get-tuple-element.48.s0.rest_1_.rest_3_, f32[360,128]{1,0:T(8,128)S(1)} %collective-permute-done.s1.rest_2_.rest_4_, ...), custom_call_target="tpu_custom_call" | custom-call | flops 20000000 | bytes 12000000 | tf_op jit(solution)/shard_map/first_inner/pallas_call | solution.py:454
  32.0 1.6 %first_even.1 = (f32[36,32,128]{2,1,0:T(8,128)S(1)}, f32[36,16,128]{2,1,0:T(8,128)S(1)}, f32[5,24,128]{2,1,0:T(8,128)S(1)}) custom-call(s32[468]{0:T(512)S(1)} %pad_add_fusion.trip, f32[156]{0:T(256)S(1)} %copy-done.4, s32[3]{0:T(128)S(1)} %pad_add_fusion.1.ids, f32[36,2,24,128]{3,2,1,0:T(8,128)S(1)} %get-tuple-element.71.inner, ...), custom_call_target="tpu_custom_call" | custom-call | flops 5000000 | bytes 3000000 | tf_op jit(solution)/shard_map/first_even/pallas_call | solution.py:473
  33.7 5.8 %collective-permute-done.9.rest_2_ = f32[324,128]{1,0:T(8,128)S(1)} collective-permute-done((f32[324,128]{1,0:T(8,128)S(1)}, f32[324,128]{1,0:T(8,128)S(1)}, u32[]{:S(2)}, u32[]{:S(2)}) %collective-permute-start.9) | collective-permute-done | bytes 165920 | tf_op jit(solution)/shard_map/ppermute | solution.py:382
  39.6 1.6 %first_odd.1 = (f32[36,32,128]{2,1,0:T(8,128)S(1)}, f32[18,16,128]{2,1,0:T(8,128)S(1)}, f32[18,16,128]{2,1,0:T(8,128)S(1)}, f32[5,24,128]{2,1,0:T(8,128)S(1)}) custom-call(s32[468]{0:T(512)S(1)} %pad_add_fusion.trip, f32[156]{0:T(256)S(1)} %copy-done.4, s32[3]{0:T(128)S(1)} %pad_add_fusion.1.ids, f32[36,2,24,128]{3,2,1,0:T(8,128)S(1)} %get-tuple-element.71.inner, ...), custom_call_target="tpu_custom_call" | custom-call | flops 5000000 | bytes 3000000 | tf_op jit(solution)/shard_map/first_odd/pallas_call | solution.py:473
  41.3 3.5 %collective-permute-start.15 = (f32[18,16,128]{2,1,0:T(8,128)S(1)}, f32[18,16,128]{2,1,0:T(8,128)S(1)}, u32[]{:S(2)}, u32[]{:S(2)}) collective-permute-start(f32[18,16,128]{2,1,0:T(8,128)S(1)} %get-tuple-element.89), channel_id=1, source_target_pairs={{4,8},{8,4},{12,16},{16,12},{20,24},{24,20},{28,32},{32,28},{36,40... | collective-permute-start | bytes 442376 | tf_op jit(solution)/shard_map/ppermute | solution.py:382
  44.8 1.7 %collective-permute-done.14.near = f32[18,16,128]{2,1,0:T(8,128)S(1)} collective-permute-done((f32[18,16,128]{2,1,0:T(8,128)S(1)}, f32[18,16,128]{2,1,0:T(8,128)S(1)}, u32[]{:S(2)}, u32[]{:S(2)}) %collective-permute-start.14) | collective-permute-done | bytes 147488 | tf_op jit(solution)/shard_map/ppermute | solution.py:382
  46.5 3.4 %collective-permute-start.16 = (f32[18,16,128]{2,1,0:T(8,128)S(1)}, f32[18,16,128]{2,1,0:T(8,128)S(1)}, u32[]{:S(2)}, u32[]{:S(2)}) collective-permute-start(f32[18,16,128]{2,1,0:T(8,128)S(1)} %collective-permute-done.14.near), channel_id=1, source_target_pairs={{0,16},{16,32},{32,48},{48,64},{64,80},{80,96},{96,112},{112,128},... | collective-permute-start | bytes 442376 | tf_op jit(solution)/shard_map/ppermute | solution.py:382
  49.9 2.5 %second_even.1 = (f32[9,3,16,128]{3,2,1,0:T(8,128)S(1)}, f32[9,3,16,128]{3,2,1,0:T(8,128)S(1)}, f32[9,3,16,128]{3,2,1,0:T(8,128)S(1)}, f32[9,3,16,128]{3,2,1,0:T(8,128)S(1)}) custom-call(s32[468]{0:T(512)S(1)} %pad_add_fusion.trip, f32[156]{0:T(256)S(1)} %copy-done.4, s32[3]{0:T(128)S(1)} %pad_add_fusion.1.ids, ...), custom_call_target="tpu_custom_call" | custom-call | flops 20000000 | bytes 12000000 | tf_op jit(solution)/shard_map/second_even/pallas_call | solution.py:495
  52.3 3.1 %collective-permute-start.11 = (f32[9,3,16,128]{3,2,1,0:T(8,128)S(1)}, f32[9,3,16,128]{3,2,1,0:T(8,128)S(1)}, u32[]{:S(2)}, u32[]{:S(2)}) collective-permute-start(f32[9,3,16,128]{3,2,1,0:T(8,128)S(1)} %get-tuple-element.82), channel_id=1, source_target_pairs={{0,1},{1,0},{2,3},{3,2},{4,5},{5,4},{6,7},{7,6},{8,9},{9,8},{10,11... | collective-permute-start | bytes 663560 | tf_op jit(solution)/shard_map/ppermute | solution.py:386
  55.4 1.7 %collective-permute-start.13 = (f32[9,3,16,128]{3,2,1,0:T(8,128)S(1)}, f32[9,3,16,128]{3,2,1,0:T(8,128)S(1)}, u32[]{:S(2)}, u32[]{:S(2)}) collective-permute-start(f32[9,3,16,128]{3,2,1,0:T(8,128)S(1)} %get-tuple-element.84), channel_id=1, source_target_pairs={{0,3},{1,2},{2,1},{3,0},{4,7},{5,6},{6,5},{7,4},{8,11},{9,10},{10,... | collective-permute-start | bytes 663560 | tf_op jit(solution)/shard_map/ppermute | solution.py:386
  57.1 2.1 %second_inner.1 = (f32[36,16,128]{2,1,0:T(8,128)S(1)}, f32[36,16,128]{2,1,0:T(8,128)S(1)}) custom-call(s32[468]{0:T(512)S(1)} %pad_add_fusion.trip, f32[156]{0:T(256)S(1)} %copy-done.4, s32[3]{0:T(128)S(1)} %pad_add_fusion.1.ids, f32[5,7,2,24,128]{4,3,2,1,0:T(8,128)S(1)} %get-tuple-element.70.faces, f32[36,32,128]{2,1,0:T(8,128)S(1)} %get-tuple-element.79.other.mine, ...), custom_call_target="tpu_custom_call" | custom-call | flops 20000000 | bytes 12000000 | tf_op jit(solution)/shard_map/second_inner/pallas_call | solution.py:505
  59.2 1.4 %second_odd.1 = (f32[9,16,128]{2,1,0:T(8,128)S(1)}, f32[9,16,128]{2,1,0:T(8,128)S(1)}, f32[9,16,128]{2,1,0:T(8,128)S(1)}, f32[9,16,128]{2,1,0:T(8,128)S(1)}) custom-call(s32[468]{0:T(512)S(1)} %pad_add_fusion.trip, f32[156]{0:T(256)S(1)} %copy-done.4, s32[3]{0:T(128)S(1)} %pad_add_fusion.1.ids, f32[36,16,128]{2,1,0:T(8,128)S(1)} %get-tuple-element.85.inner, ...), custom_call_target="tpu_custom_call" | custom-call | tf_op jit(solution)/shard_map/second_odd/pallas_call | solution.py:515
  61.2 0.9 %collective-permute-done.17.r1 = f32[9,16,128]{2,1,0:T(8,128)S(1)} collective-permute-done((f32[9,16,128]{2,1,0:T(8,128)S(1)}, f32[9,16,128]{2,1,0:T(8,128)S(1)}, u32[]{:S(2)}, u32[]{:S(2)}) %collective-permute-start.17) | collective-permute-done | bytes 73760 | tf_op jit(solution)/shard_map/ppermute | solution.py:386
  63.6 5.1 %collective-permute-done.18.r2 = f32[9,16,128]{2,1,0:T(8,128)S(1)} collective-permute-done((f32[9,16,128]{2,1,0:T(8,128)S(1)}, f32[9,16,128]{2,1,0:T(8,128)S(1)}, u32[]{:S(2)}, u32[]{:S(2)}) %collective-permute-start.18) | collective-permute-done | bytes 73760 | tf_op jit(solution)/shard_map/ppermute | solution.py:386
  68.7 1.8 %collective-permute-done.19.r3 = f32[9,16,128]{2,1,0:T(8,128)S(1)} collective-permute-done((f32[9,16,128]{2,1,0:T(8,128)S(1)}, f32[9,16,128]{2,1,0:T(8,128)S(1)}, u32[]{:S(2)}, u32[]{:S(2)}) %collective-permute-start.19) | collective-permute-done | bytes 73760 | tf_op jit(solution)/shard_map/ppermute | solution.py:386
  70.5 1.7 %second_sweep.1 = (f32[9,2,64,128]{3,2,1,0:T(8,128)}, f32[9,2,64,128]{3,2,1,0:T(8,128)}) custom-call(s32[3]{0:T(128)S(1)} %pad_add_fusion.1.ids, f32[2,64,128]{2,1,0:T(8,128)S(1)} %final_rates.1.rate, f32[36,128]{1,0:T(8,128)S(1)} %get-tuple-element.69.inverse, f32[9,3,16,128]{3,2,1,0:T(8,128)S(1)} %get-tuple-element.81.m0, ...), custom_call_target="tpu_custom_call" | custom-call | tf_op jit(solution)/shard_map/second_sweep/pallas_call | solution.py:533
  (47 shorter events, 9.4 us)
Async XLA Ops:
  1.8 6.3 %copy-start.1 = (f32[9,2,64,128]{3,2,1,0:T(8,128)S(1)}, f32[9,2,64,128]{3,2,1,0:T(8,128)}, u32[]{:S(2)}) copy-start(f32[9,2,64,128]{3,2,1,0:T(8,128)} %source) | copy-start | bytes 1769476
  2.5 2.4 %collective-permute-start = (f32[360,128]{1,0:T(8,128)S(1)}, f32[360,128]{1,0:T(8,128)S(1)}, u32[]{:S(2)}, u32[]{:S(2)}) collective-permute-start(f32[360,128]{1,0:T(8,128)S(1)} %get-tuple-element.49), channel_id=1, source_target_pairs={{0,1},{1,0},{2,3},{3,2},{4,5},{5,4},{6,7},{7,6},{8,9},{9,8},{10,11... | collective-permute-start | bytes 552968 | tf_op jit(solution)/shard_map/ppermute | solution.py:386
  3.3 6.9 %collective-permute-start.2 = (f32[360,128]{1,0:T(8,128)S(1)}, f32[360,128]{1,0:T(8,128)S(1)}, u32[]{:S(2)}, u32[]{:S(2)}) collective-permute-start(f32[360,128]{1,0:T(8,128)S(1)} %get-tuple-element.56), channel_id=1, source_target_pairs={{0,3},{1,2},{2,1},{3,0},{4,7},{5,6},{6,5},{7,4},{8,11},{9,10},{10,... | collective-permute-start | bytes 552968 | tf_op jit(solution)/shard_map/ppermute | solution.py:386
  4.9 8.8 %collective-permute-start.1 = (f32[360,128]{1,0:T(8,128)S(1)}, f32[360,128]{1,0:T(8,128)S(1)}, u32[]{:S(2)}, u32[]{:S(2)}) collective-permute-start(f32[360,128]{1,0:T(8,128)S(1)} %get-tuple-element.50), channel_id=1, source_target_pairs={{0,2},{1,3},{2,0},{3,1},{4,6},{5,7},{6,4},{7,5},{8,10},{9,11},{10,... | collective-permute-start | bytes 552968 | tf_op jit(solution)/shard_map/ppermute | solution.py:386
  5.5 6.8 %copy-start.2 = (f32[4,2,64,128]{3,2,1,0:T(8,128)S(1)}, f32[4,2,64,128]{3,2,1,0:T(8,128)}, u32[]{:S(2)}) copy-start(f32[4,2,64,128]{3,2,1,0:T(8,128)} %kl) | copy-start | bytes 786436
  5.5 6.8 %copy-start.3 = (f32[2,64,128]{2,1,0:T(8,128)S(1)}, f32[2,64,128]{2,1,0:T(8,128)}, u32[]{:S(2)}) copy-start(f32[2,64,128]{2,1,0:T(8,128)} %mean.2) | copy-start | bytes 196612
  5.5 8.2 %collective-permute-start.4 = (f32[324,128]{1,0:T(8,128)S(1)}, f32[324,128]{1,0:T(8,128)S(1)}, u32[]{:S(2)}, u32[]{:S(2)}) collective-permute-start(f32[324,128]{1,0:T(8,128)S(1)} %pack_near.1), channel_id=1, source_target_pairs={{4,8},{8,4},{20,24},{24,20},{36,40},{40,36},{52,56},{56,52},{68,72... | collective-permute-start | bytes 497672 | tf_op jit(solution)/shard_map/ppermute | solution.py:382
  10.1 3.6 %collective-permute-start.3 = (f32[324,128]{1,0:T(8,128)S(1)}, f32[324,128]{1,0:T(8,128)S(1)}, u32[]{:S(2)}, u32[]{:S(2)}) collective-permute-start(f32[324,128]{1,0:T(8,128)S(1)} %get-tuple-element.57), channel_id=1, source_target_pairs={{0,1},{1,0},{2,3},{3,2},{4,5},{5,4},{6,7},{7,6},{8,9},{9,8},{10,11... | collective-permute-start | bytes 497672 | tf_op jit(solution)/shard_map/ppermute | solution.py:386
  10.3 21.7 %collective-permute-start.7 = (f32[324,128]{1,0:T(8,128)S(1)}, f32[324,128]{1,0:T(8,128)S(1)}, u32[]{:S(2)}, u32[]{:S(2)}) collective-permute-start(f32[324,128]{1,0:T(8,128)S(1)} %get-tuple-element.74), channel_id=1, source_target_pairs={{0,2},{1,3},{2,0},{3,1},{4,6},{5,7},{6,4},{7,5},{8,10},{9,11},{10,... | collective-permute-start | bytes 497672 | tf_op jit(solution)/shard_map/ppermute | solution.py:386
  11.8 20.2 %collective-permute-start.8 = (f32[324,128]{1,0:T(8,128)S(1)}, f32[324,128]{1,0:T(8,128)S(1)}, u32[]{:S(2)}, u32[]{:S(2)}) collective-permute-start(f32[324,128]{1,0:T(8,128)S(1)} %get-tuple-element.75), channel_id=1, source_target_pairs={{0,3},{1,2},{2,1},{3,0},{4,7},{5,6},{6,5},{7,4},{8,11},{9,10},{10,... | collective-permute-start | bytes 497672 | tf_op jit(solution)/shard_map/ppermute | solution.py:386
  13.7 1.9 %copy-start.5 = (s32[156,3]{0,1:T(4,128)S(1)}, s32[156,3]{0,1:T(4,128)}, u32[]{:S(2)}) copy-start(s32[156,3]{0,1:T(4,128)} %param.10) | copy-start | bytes 5620
  14.3 17.7 %collective-permute-start.6 = (f32[784,128]{1,0:T(8,128)S(1)}, f32[784,128]{1,0:T(8,128)S(1)}, u32[]{:S(2)}, u32[]{:S(2)}) collective-permute-start(f32[784,128]{1,0:T(8,128)S(1)} %get-tuple-element.66), channel_id=1, source_target_pairs={{0,4},{4,0},{8,12},{12,8},{16,20},{20,16},{24,28},{28,24},{32,36},... | collective-permute-start | bytes 1204232 | tf_op jit(solution)/shard_map/ppermute | solution.py:382
  15.6 23.9 %collective-permute-start.5 = (f32[460,128]{1,0:T(8,128)S(1)}, f32[460,128]{1,0:T(8,128)S(1)}, u32[]{:S(2)}, u32[]{:S(2)}) collective-permute-start(f32[460,128]{1,0:T(8,128)S(1)} %get-tuple-element.65), channel_id=1, source_target_pairs={{4,8},{8,4},{12,16},{16,12},{20,24},{24,20},{28,32},{32,28},{36,40... | collective-permute-start | bytes 706568 | tf_op jit(solution)/shard_map/ppermute | solution.py:382
  24.6 14.9 %collective-permute-start.9 = (f32[324,128]{1,0:T(8,128)S(1)}, f32[324,128]{1,0:T(8,128)S(1)}, u32[]{:S(2)}, u32[]{:S(2)}) collective-permute-start(f32[324,128]{1,0:T(8,128)S(1)} %collective-permute-done.4.rest_0_), channel_id=1, source_target_pairs={{0,16},{16,32},{32,48},{48,64},{64,80},{80,96},{96,112},{112,128},... | collective-permute-start | bytes 497672 | tf_op jit(solution)/shard_map/ppermute | solution.py:382
  33.6 16.2 %collective-permute-start.10 = (f32[36,16,128]{2,1,0:T(8,128)S(1)}, f32[36,16,128]{2,1,0:T(8,128)S(1)}, u32[]{:S(2)}, u32[]{:S(2)}) collective-permute-start(f32[36,16,128]{2,1,0:T(8,128)S(1)} %get-tuple-element.80), channel_id=1, source_target_pairs={{0,4},{4,0},{8,12},{12,8},{16,20},{20,16},{24,28},{28,24},{32,36},... | collective-permute-start | bytes 884744 | tf_op jit(solution)/shard_map/ppermute | solution.py:382
  41.2 5.3 %collective-permute-start.14 = (f32[18,16,128]{2,1,0:T(8,128)S(1)}, f32[18,16,128]{2,1,0:T(8,128)S(1)}, u32[]{:S(2)}, u32[]{:S(2)}) collective-permute-start(f32[18,16,128]{2,1,0:T(8,128)S(1)} %get-tuple-element.88), channel_id=1, source_target_pairs={{4,8},{8,4},{20,24},{24,20},{36,40},{40,36},{52,56},{56,52},{68,72... | collective-permute-start | bytes 442376 | tf_op jit(solution)/shard_map/ppermute | solution.py:382
  41.3 17.9 %collective-permute-start.15 = (f32[18,16,128]{2,1,0:T(8,128)S(1)}, f32[18,16,128]{2,1,0:T(8,128)S(1)}, u32[]{:S(2)}, u32[]{:S(2)}) collective-permute-start(f32[18,16,128]{2,1,0:T(8,128)S(1)} %get-tuple-element.89), channel_id=1, source_target_pairs={{4,8},{8,4},{12,16},{16,12},{20,24},{24,20},{28,32},{32,28},{36,40... | collective-permute-start | bytes 442376 | tf_op jit(solution)/shard_map/ppermute | solution.py:382
  46.5 12.8 %collective-permute-start.16 = (f32[18,16,128]{2,1,0:T(8,128)S(1)}, f32[18,16,128]{2,1,0:T(8,128)S(1)}, u32[]{:S(2)}, u32[]{:S(2)}) collective-permute-start(f32[18,16,128]{2,1,0:T(8,128)S(1)} %collective-permute-done.14.near), channel_id=1, source_target_pairs={{0,16},{16,32},{32,48},{48,64},{64,80},{80,96},{96,112},{112,128},... | collective-permute-start | bytes 442376 | tf_op jit(solution)/shard_map/ppermute | solution.py:382
  52.3 18.1 %collective-permute-start.11 = (f32[9,3,16,128]{3,2,1,0:T(8,128)S(1)}, f32[9,3,16,128]{3,2,1,0:T(8,128)S(1)}, u32[]{:S(2)}, u32[]{:S(2)}) collective-permute-start(f32[9,3,16,128]{3,2,1,0:T(8,128)S(1)} %get-tuple-element.82), channel_id=1, source_target_pairs={{0,1},{1,0},{2,3},{3,2},{4,5},{5,4},{6,7},{7,6},{8,9},{9,8},{10,11... | collective-permute-start | bytes 663560 | tf_op jit(solution)/shard_map/ppermute | solution.py:386
  55.4 15.1 %collective-permute-start.12 = (f32[9,3,16,128]{3,2,1,0:T(8,128)S(1)}, f32[9,3,16,128]{3,2,1,0:T(8,128)S(1)}, u32[]{:S(2)}, u32[]{:S(2)}) collective-permute-start(f32[9,3,16,128]{3,2,1,0:T(8,128)S(1)} %get-tuple-element.83), channel_id=1, source_target_pairs={{0,2},{1,3},{2,0},{3,1},{4,6},{5,7},{6,4},{7,5},{8,10},{9,11},{10,... | collective-permute-start | bytes 663560 | tf_op jit(solution)/shard_map/ppermute | solution.py:386
  55.4 15.1 %collective-permute-start.13 = (f32[9,3,16,128]{3,2,1,0:T(8,128)S(1)}, f32[9,3,16,128]{3,2,1,0:T(8,128)S(1)}, u32[]{:S(2)}, u32[]{:S(2)}) collective-permute-start(f32[9,3,16,128]{3,2,1,0:T(8,128)S(1)} %get-tuple-element.84), channel_id=1, source_target_pairs={{0,3},{1,2},{2,1},{3,0},{4,7},{5,6},{6,5},{7,4},{8,11},{9,10},{10,... | collective-permute-start | bytes 663560 | tf_op jit(solution)/shard_map/ppermute | solution.py:386
  60.6 1.5 %collective-permute-start.17 = (f32[9,16,128]{2,1,0:T(8,128)S(1)}, f32[9,16,128]{2,1,0:T(8,128)S(1)}, u32[]{:S(2)}, u32[]{:S(2)}) collective-permute-start(f32[9,16,128]{2,1,0:T(8,128)S(1)} %get-tuple-element.91), channel_id=1, source_target_pairs={{0,1},{1,0},{2,3},{3,2},{4,5},{5,4},{6,7},{7,6},{8,9},{9,8},{10,11... | collective-permute-start | bytes 221192 | tf_op jit(solution)/shard_map/ppermute | solution.py:386
  61.2 7.4 %collective-permute-start.18 = (f32[9,16,128]{2,1,0:T(8,128)S(1)}, f32[9,16,128]{2,1,0:T(8,128)S(1)}, u32[]{:S(2)}, u32[]{:S(2)}) collective-permute-start(f32[9,16,128]{2,1,0:T(8,128)S(1)} %get-tuple-element.92), channel_id=1, source_target_pairs={{0,2},{1,3},{2,0},{3,1},{4,6},{5,7},{6,4},{7,5},{8,10},{9,11},{10,... | collective-permute-start | bytes 221192 | tf_op jit(solution)/shard_map/ppermute | solution.py:386
  62.1 8.3 %collective-permute-start.19 = (f32[9,16,128]{2,1,0:T(8,128)S(1)}, f32[9,16,128]{2,1,0:T(8,128)S(1)}, u32[]{:S(2)}, u32[]{:S(2)}) collective-permute-start(f32[9,16,128]{2,1,0:T(8,128)S(1)} %get-tuple-element.93), channel_id=1, source_target_pairs={{0,3},{1,2},{2,1},{3,0},{4,7},{5,6},{6,5},{7,4},{8,11},{9,10},{10,... | collective-permute-start | bytes 221192 | tf_op jit(solution)/shard_map/ppermute | solution.py:386
  (3 other events, 2.4 us)
